TPU v7x, 32 devices: a whole 2x2x4 slice. The times are simulated.
32 devices in a mesh: rows: 8 (over y, x, core), ch: 4 (over z).
Axes of the slice: x: 2, y: 2, z: 4, core: 2. Of those that a mesh axis runs over, the one named last changes fastest.
Arguments:
- frames: bfloat16 [128, 1024, 512], P('rows', None, 'ch'), may hold values from -6 to 6
- style_vector: bfloat16 [128, 4, 128], P('rows'), may hold values from -5 to 5
- segment_ids: int32 [128, 1024], P('rows'), may hold values from 0 to 3, as said below
- padding: int32 [128, 1024], P('rows'), may hold values from 0 to 1, as said below
- fc1_weight: bfloat16 [2, 128, 512], P(None, None, 'ch'), may hold values from -0.375 to 0.375
- fc1_bias: bfloat16 [2, 512], P(None, 'ch'), may hold values from -3 to 3
- conv1_weight: bfloat16 [3, 512, 512], P(None, None, 'ch'), may hold values from -0.15625 to 0.15625
- fc2_weight: bfloat16 [2, 128, 512], P(None, None, 'ch'), may hold values from -0.375 to 0.375
- fc2_bias: bfloat16 [2, 512], P(None, 'ch'), may hold values from -3 to 3
- conv2_weight: bfloat16 [3, 512, 512], P(None, None, 'ch'), may hold values from -0.15625 to 0.15625
- conv2_bias: bfloat16 [512], P('ch'), may hold values from -3 to 3
- cotangent: bfloat16 [128, 1024, 512], P('rows', None, 'ch'), may hold values from -6 to 6
Outputs:
- output: bfloat16 [128, 1024, 512], P('rows', None, 'ch')
- grad_frames: bfloat16 [128, 1024, 512], P('rows', None, 'ch')
- grad_style: float32 [128, 4, 128], P('rows')
- grad_fc1_weight: float32 [2, 128, 512], P(None, None, 'ch')
- grad_fc1_bias: float32 [2, 512], P(None, 'ch')
- grad_conv1_weight: float32 [3, 512, 512], P(None, None, 'ch')
- grad_fc2_weight: float32 [2, 128, 512], P(None, None, 'ch')
- grad_fc2_bias: float32 [2, 512], P(None, 'ch')
- grad_conv2_weight: float32 [3, 512, 512], P(None, None, 'ch')
- grad_conv2_bias: float32 [512], P('ch')
Inputs may be any that keep to these rules, and one draw needn't show every extreme that they name: `segment_ids`: in each row the ids never fall, begin at 0 and end at 3, and change only at frames that are multiples of 16. `padding`: in each row the zeros, if any, are the last frames.
All inputs are finite; a program needn't handle non-finite values.
Results may differ from a plain program's by a relative error of at most 0.0095.
Values may be sent and summed in bfloat16 or wider, within the bound.
No kernel may reach another device: no remote copies, remote signals or barrier semaphores. Data moves between devices by JAX's collectives and lax.ppermute only.
A program may use at most 320 MiB of HBM per device.

v0:
```python
import math

import jax
import jax.numpy as jnp
from jax import lax
from jax.sharding import PartitionSpec as P

var_floor = 0.1
inv_root = math.sqrt(0.5)
highest = lax.Precision.HIGHEST


def shift_down(values):
    return jnp.concatenate([jnp.zeros_like(values[:, :1]), values[:, :-1]], axis=1)


def shift_up(values):
    return jnp.concatenate([values[:, 1:], jnp.zeros_like(values[:, :1])], axis=1)


def joints(segment_ids):
    same_seg = segment_ids[:, 1:] == segment_ids[:, :-1]
    false_col = jnp.zeros_like(same_seg[:, :1])
    left_join = jnp.concatenate([false_col, same_seg], axis=1)[..., None]
    right_join = jnp.concatenate([same_seg, false_col], axis=1)[..., None]
    return (left_join, right_join)


def layout(segment_ids, padding, segments):
    member = (segment_ids[..., None] == jnp.arange(segments, dtype=jnp.int32)).astype(jnp.float32)
    padded_mask = padding.astype(jnp.float32)[..., None]
    return (member, padded_mask)


def adain_act(inputs, style_in, weight_in, bias_in, member, padded_mask):
    weights_seg = member * padded_mask
    counts = jnp.maximum(jnp.sum(weights_seg, axis=1), 1.0)[..., None]
    means = jnp.einsum("rts,rtc->rsc", weights_seg, inputs, precision=highest) / counts
    centered = inputs - jnp.einsum("rts,rsc->rtc", member, means, precision=highest)
    variance = (
        jnp.einsum("rts,rtc->rsc", weights_seg, centered * centered, precision=highest) / counts
    )
    scales = lax.rsqrt(jnp.maximum(variance, var_floor))
    normed = centered * jnp.einsum("rts,rsc->rtc", member, scales, precision=highest)
    project = (
        jnp.einsum("rsi,kic->krsc", style_in, weight_in, precision=highest)
        + bias_in[:, None, None, :]
    )
    affine = jnp.einsum("rts,krsc->krtc", member, project, precision=highest)
    hidden = (1.0 + affine[0]) * normed + affine[1]
    return jax.nn.silu(hidden) * padded_mask


def conv_local(inputs, weight, left_join, right_join):
    taps = jnp.einsum("rti,kio->krto", inputs, weight, preferred_element_type=jnp.float32)
    return (
        taps[1]
        + jnp.where(left_join, shift_down(taps[0]), 0.0)
        + jnp.where(right_join, shift_up(taps[2]), 0.0)
    )


def convolve(shard, weight, left_join, right_join):
    gathered = lax.all_gather(shard, "ch", axis=2, tiled=True)
    return (conv_local(gathered, weight, left_join, right_join), gathered)


def spread(grad_low, left_join, right_join):
    zeros_like = jnp.zeros_like(grad_low)
    first_tap = shift_up(jnp.where(left_join, grad_low, zeros_like))
    last_tap = shift_down(jnp.where(right_join, grad_low, zeros_like))
    return jnp.stack([first_tap, grad_low, last_tap])


def weight_grad(kept, taps):
    return jnp.einsum("rti,krto->kio", kept, taps, preferred_element_type=jnp.float32)


def input_grad(taps, weight):
    partial_sums = jnp.einsum("krto,kio->rti", taps, weight, preferred_element_type=jnp.float32)
    return lax.psum_scatter(partial_sums, "ch", scatter_dimension=2, tiled=True)


def per_device(
    frames,
    style_vector,
    segment_ids,
    padding,
    fc1_weight,
    fc1_bias,
    conv1_weight,
    fc2_weight,
    fc2_bias,
    conv2_weight,
    conv2_bias,
    cotangent,
):
    member, padded_mask = layout(segment_ids, padding, style_vector.shape[1])
    left_join, right_join = joints(segment_ids)
    frames_f = frames.astype(jnp.float32)
    style_f = style_vector.astype(jnp.float32)

    def norm_act(inputs, style_in, weight_in, bias_in):
        return adain_act(inputs, style_in, weight_in, bias_in, member, padded_mask)

    first_act, first_pull = jax.vjp(
        norm_act, frames_f, style_f, fc1_weight.astype(jnp.float32), fc1_bias.astype(jnp.float32)
    )
    first_low = first_act.astype(jnp.bfloat16)
    first_conv, first_kept = convolve(first_low, conv1_weight, left_join, right_join)
    second_act, second_pull = jax.vjp(
        norm_act, first_conv, style_f, fc2_weight.astype(jnp.float32), fc2_bias.astype(jnp.float32)
    )
    second_low = second_act.astype(jnp.bfloat16)
    second_conv, second_kept = convolve(second_low, conv2_weight, left_join, right_join)
    second_conv = second_conv + conv2_bias.astype(jnp.float32)
    output = ((frames_f + second_conv * padded_mask) * inv_root).astype(jnp.bfloat16)
    upstream = cotangent.astype(jnp.float32)
    second_grad = (upstream * padded_mask * inv_root).astype(jnp.bfloat16)
    grad_conv2_bias = jnp.sum(second_grad.astype(jnp.float32), axis=(0, 1))
    second_taps = spread(second_grad, left_join, right_join)
    grad_conv2_weight = weight_grad(second_kept, second_taps)
    second_input = input_grad(second_taps, conv2_weight)
    conv1_grad, style_second, grad_fc2_weight, grad_fc2_bias = second_pull(second_input)
    first_grad = conv1_grad.astype(jnp.bfloat16)
    first_taps = spread(first_grad, left_join, right_join)
    grad_conv1_weight = weight_grad(first_kept, first_taps)
    first_input = input_grad(first_taps, conv1_weight)
    frames_term, style_first, grad_fc1_weight, grad_fc1_bias = first_pull(first_input)
    grad_frames = (upstream * inv_root + frames_term).astype(jnp.bfloat16)
    grad_style = lax.psum((style_first + style_second).astype(jnp.bfloat16), "ch").astype(
        jnp.float32
    )
    (
        grad_fc1_weight,
        grad_fc1_bias,
        grad_conv1_weight,
        grad_fc2_weight,
        grad_fc2_bias,
        grad_conv2_weight,
        grad_conv2_bias,
    ) = lax.psum(
        (
            grad_fc1_weight,
            grad_fc1_bias,
            grad_conv1_weight,
            grad_fc2_weight,
            grad_fc2_bias,
            grad_conv2_weight,
            grad_conv2_bias,
        ),
        "rows",
    )
    return (
        output,
        grad_frames,
        grad_style,
        grad_fc1_weight,
        grad_fc1_bias,
        grad_conv1_weight,
        grad_fc2_weight,
        grad_fc2_bias,
        grad_conv2_weight,
        grad_conv2_bias,
    )


def solution(mesh):
    return jax.shard_map(
        per_device,
        mesh=mesh,
        in_specs=(
            P("rows", None, "ch"),
            P("rows", None, None),
            P("rows", None),
            P("rows", None),
            P(None, None, "ch"),
            P(None, "ch"),
            P(None, None, "ch"),
            P(None, None, "ch"),
            P(None, "ch"),
            P(None, None, "ch"),
            P("ch"),
            P("rows", None, "ch"),
        ),
        out_specs=(
            P("rows", None, "ch"),
            P("rows", None, "ch"),
            P("rows", None, None),
            P(None, None, "ch"),
            P(None, "ch"),
            P(None, None, "ch"),
            P(None, None, "ch"),
            P(None, "ch"),
            P(None, None, "ch"),
            P("ch"),
        ),
        check_vma=False,
    )
```

profile of v0, /device:TPU:0, one launch (start us, length us, event | category | flops | bytes accessed | tf_op | source)
XLA Modules:
  0.0 1992.9 jit_solution(12878085318238654428)
XLA Ops:
  7.3 0.7 convert_element_type.51
  8.0 0.8 convert_element_type.52
  8.8 1.0 select_reduce_fusion
  9.8 6.4 copy.22
  16.2 4.0 convolution_divide_fusion.1
  20.1 6.4 copy.35
  26.6 5.6 convert_subtract_fusion
  32.2 3.2 copy-done.4
  35.4 7.4 fusion.166
  43.0 10.4 convolution_bitcast_fusion.3
  53.3 18.1 convert_reduce_fusion
  71.6 5.1 slice_select_fusion.3
  76.8 5.1 pad_bitcast_fusion.2
  81.9 19.9 convolution_bitcast_fusion.1
  101.9 0.6 copy-done.27
  102.8 10.7 convolution_bitcast_fusion.2
  113.5 247.6 %all-gather.3.cloned.1.call-done = bf16[16,1024,512]{1,2,0:T(8,128)(2,1)} async-done(((bf16[16,1024,128]{1,2,0:T(8,128)(2,1)}), bf16[16,1024,512]{1,2,0:T(8,128)(2,1)}) %all-gather.3.cloned.1.call-update) | async-done | bytes 16777232 | tf_op jit(solution)/shard_map/all_gather | solution.py:64
  361.1 26.3 %fusion.12 = f32[3,16,1024,128]{2,3,1,0:T(8,128)} fusion(bf16[16,1024,512]{1,2,0:T(8,128)(2,1)} %all-gather.3.cloned.1.call-done, bf16[3,512,128]{2,1,0:T(8,128)(2,1)S(1)} %copy-done), kind=kOutput, calls=%fused_computation.26 | convolution fusion | flops 6442450944 | bytes 42336256 | tf_op jit(solution)/shard_map/rti,kio->krto/dot_general | solution.py:55
  387.4 9.4 slice_bitcast_fusion.5
  396.8 2.2 slice.87
  399.0 7.6 fusion.34
  406.7 7.1 convolution_divide_fusion
  413.8 3.9 convolution_subtract_fusion
  417.7 3.2 copy-done.2
  420.9 7.0 fusion.164
  428.0 5.7 fusion.106
  433.7 480.0 %reduce-scatter.3.cloned.1.call-done = f32[16,1024,128]{1,2,0:T(8,128)} async-done(((f32[16,1024,512]{1,2,0:T(8,128)}), f32[16,1024,128]{1,2,0:T(8,128)}) %reduce-scatter.3.cloned.1.call-update) | async-done | bytes 8388624 | tf_op jit(solution)/shard_map/reduce_scatter | solution.py:81
  913.8 20.5 %multiply_bitcast_fusion = (f32[1,16,1024,128]{2,3,1,0:T(8,128)}, f32[16,1024,128]{1,2,0:T(8,128)S(1)}, f32[16,1024,128]{1,2,0:T(8,128)}) fusion(f32[16,1024,128]{1,2,0:T(8,128)} %copy-done.2, f32[16,1024,128]{1,2,0:T(8,128)} %fusion.106, f32[16,1024,128]{1,2,0:T(8,128)} %reduce-scatter.3.cloned.1.call-done, f32[16,1024]{1,0:T(8,128)S(1)} %convert_element_type.52, ...), kind=kLoop, calls=%fused_computation.61 | loop fusion | flops 31457280 | bytes 67174400 | tf_op jit(solution)/shard_map/transpose(jvp())/broadcast_in_dim | solution.py:50
  934.3 3.2 copy-done.5
  937.5 7.3 fusion.81
  944.8 15.4 add_add_fusion.1
  960.2 6.6 fusion.67
  966.8 7.1 add_convert_fusion
  973.9 1.8 slice_select_fusion.1
  975.8 2.8 pad_bitcast_fusion.1
  978.6 4.6 pad_bitcast_fusion
  983.1 18.2 convolution_bitcast_fusion
  1001.4 552.9 %reduce-scatter.5.cloned.1.call-done = f32[16,1024,128]{1,2,0:T(8,128)} async-done(((f32[16,1024,512]{1,2,0:T(8,128)}), f32[16,1024,128]{1,2,0:T(8,128)}) %reduce-scatter.5.cloned.1.call-update) | async-done | bytes 8388624 | tf_op jit(solution)/shard_map/reduce_scatter | solution.py:81
  1554.3 21.9 %multiply_bitcast_fusion.1 = (f32[1,16,1024,128]{2,3,1,0:T(8,128)}, f32[16,1024,128]{1,2,0:T(8,128)}, bf16[16,1024,128]{1,2,0:T(8,128)(2,1)}) fusion(f32[16,1024,128]{1,2,0:T(8,128)} %get-tuple-element.50, f32[2,16,1024,128]{2,3,1,0:T(8,128)} %convolution_bitcast_fusion.3, f32[16,1024,128]{1,2,0:T(8,128)} %reduce-scatter.5.cloned.1.call-done, ...), kind=kLoop, calls=%fused_computation.62 | loop fusion | flops 41943040 | bytes 62980096 | tf_op jit(solution)/shard_map/transpose(jvp())/broadcast_in_dim | solution.py:50
  1576.4 11.5 fusion.200
  1587.8 1.0 convolution_bitcast_fusion.4
  1588.8 15.7 fusion.55
  1604.5 10.8 fusion.90
  1615.3 15.4 add_add_fusion
  1630.7 4.1 fusion.70
  1634.8 9.4 fusion.21
  1644.3 6.4 copy.57
  1650.7 11.5 fusion.199
  1662.6 23.4 %psum.56 = bf16[16,4,128]{2,0,1:T(8,128)(2,1)S(1)} all-reduce(bf16[16,4,128]{2,0,1:T(8,128)(2,1)S(1)} %fusion.74), channel_id=1, replica_groups=mesh['rows'=8,'ch'=4] {'ch'}, use_global_device_ids=true, to_apply=%region_3.4 | all-reduce | flops 8192 | bytes 32768 | tf_op jit(solution)/shard_map/psum | solution.py:131
  1686.0 0.6 copy.58
  1686.7 14.6 all-reduce.14
  1701.2 0.9 convolution_bitcast_fusion.5
  1702.2 162.2 %all-gather.5.cloned.1.call-done = bf16[16,1024,512]{1,2,0:T(8,128)(2,1)} async-done(((bf16[16,1024,128]{1,2,0:T(8,128)(2,1)}), bf16[16,1024,512]{1,2,0:T(8,128)(2,1)}) %all-gather.5.cloned.1.call-update) | async-done | bytes 16777232 | tf_op jit(solution)/shard_map/all_gather | solution.py:64
  1864.3 26.3 %fusion.15 = f32[3,16,1024,128]{2,3,1,0:T(8,128)} fusion(bf16[16,1024,512]{1,2,0:T(8,128)(2,1)} %all-gather.5.cloned.1.call-done, bf16[3,512,128]{2,1,0:T(8,128)(2,1)S(1)} %copy-done.11), kind=kOutput, calls=%fused_computation.27 | convolution fusion | flops 6442450944 | bytes 42336256 | tf_op jit(solution)/shard_map/rti,kio->krto/dot_general | solution.py:55
  1890.6 9.3 slice_bitcast_fusion.1
  1900.0 5.5 slice.93
  1905.4 13.8 fusion.58
  1919.3 14.2 fusion.19
  1933.5 6.4 copy.56
  1939.9 38.4 %all-reduce.18.cloned.1.call-done = (f32[2,128,128]{1,2,0:T(8,128)}, f32[3,512,128]{1,2,0:T(8,128)}, f32[2,128,128]{1,2,0:T(8,128)}, f32[3,512,128]{1,2,0:T(8,128)}) async-done(((f32[2,128,128]{1,2,0:T(8,128)}, f32[3,512,128]{1,2,0:T(8,128)}, f32[2,128,128]{1,2,0:T(8,128)}, f32[3,512,128]{1,2,0:T(8,128)}), (f32[2,128,128]{1,2,0:T(8,128)}, f32[3,512,128]{1,2,0:T(8,128)}, f32[2,128,128]{1,2,0:T(8,128)}, ...) | async-done | bytes 1835024 | tf_op jit(solution)/shard_map/psum | solution.py:142
  1978.2 1.7 copy.59
  1979.9 1.7 copy.61
  1981.6 2.3 copy.60
  1983.8 2.3 copy.62
  (76 shorter events, 1.6 us)
Async XLA Ops:
  7.2 353.9 %copy-start = (bf16[3,512,128]{2,1,0:T(8,128)(2,1)S(1)}, bf16[3,512,128]{2,1,0:T(8,128)(2,1)}, u32[]{:S(2)}) copy-start(bf16[3,512,128]{2,1,0:T(8,128)(2,1)} %param.18) | copy-start | bytes 1179652
  7.2 9.0 copy-start.8
  7.2 353.9 %all-gather.3.cloned.1.call-start = ((), (), s32[]{:S(2)}) async-start(), calls=%async_computation.2 | async-start | bytes 20971520 | tf_op jit(solution)/shard_map/all_gather | solution.py:64
  26.6 16.3 copy-start.12
  26.6 16.3 copy-start.16
  32.1 3.2 copy-start.4
  42.8 10.5 copy-start.22
  71.5 842.3 %reduce-scatter.3.cloned.1.call-start = ((), (), s32[]{:S(2)}) async-start(), calls=%async_computation.4 | async-start | bytes 41943040 | tf_op jit(solution)/shard_map/reduce_scatter | solution.py:81
  76.8 5.1 copy-start.10
  101.8 0.7 copy-start.27
  101.8 0.9 copy-start.14
  101.8 1452.5 %reduce-scatter.5.cloned.1.call-start = ((), (), s32[]{:S(2)}) async-start(), calls=%async_computation.5 | async-start | bytes 41943040 | tf_op jit(solution)/shard_map/reduce_scatter | solution.py:81
  102.7 296.3 %copy-start.18 = (pred[16,1024]{1,0:T(8,128)(4,1)}, pred[16,1024]{1,0:T(8,128)(4,1)S(1)}, u32[]{:S(2)}) copy-start(pred[16,1024]{1,0:T(8,128)(4,1)S(1)} %get-tuple-element.53) | copy-start | bytes 49156
  102.7 296.3 %copy-start.20 = (pred[16,1024]{1,0:T(8,128)(4,1)}, pred[16,1024]{1,0:T(8,128)(4,1)S(1)}, u32[]{:S(2)}) copy-start(pred[16,1024]{1,0:T(8,128)(4,1)S(1)} %get-tuple-element.54) | copy-start | bytes 49156
  417.7 3.2 copy-start.2
  913.8 23.8 %copy-start.3 = (f32[16,1024,128]{1,2,0:T(8,128)S(1)}, f32[16,1024,128]{1,2,0:T(8,128)}, u32[]{:S(2)}) copy-start(f32[16,1024,128]{1,2,0:T(8,128)} %copy-done.2) | copy-start | bytes 25165828
  934.3 3.2 copy-start.5
  960.2 6.6 copy-start.6
  973.8 1.9 copy-start.7
  1001.4 863.0 %all-gather.5.cloned.1.call-start = ((), (), s32[]{:S(2)}) async-start(), calls=%async_computation.3 | async-start | bytes 20971520 | tf_op jit(solution)/shard_map/all_gather | solution.py:64
  1554.3 22.0 %copy-start.28 = (bf16[128]{0:T(256)(128)(2,1)S(1)}, bf16[128]{0:T(256)(128)(2,1)}, u32[]{:S(2)}) copy-start(bf16[128]{0:T(256)(128)(2,1)} %param.22) | copy-start | bytes 772
  1554.3 22.0 %copy-start.24 = (u16[4,128]{1,0:T(4,128)(2,1)S(1)}, u16[4,128]{1,0:T(4,128)(2,1)}, u32[]{:S(2)}) copy-start(u16[4,128]{1,0:T(4,128)(2,1)} %get-tuple-element.20) | copy-start | bytes 3076
  1554.3 22.0 %copy-start.25 = (u16[4,128]{1,0:T(4,128)(2,1)S(1)}, u16[4,128]{1,0:T(4,128)(2,1)}, u32[]{:S(2)}) copy-start(u16[4,128]{1,0:T(4,128)(2,1)} %get-tuple-element.21) | copy-start | bytes 3076
  1576.2 402.0 %all-reduce.18.cloned.1.call-start = ((), (), s32[]{:S(2)}) async-start(), calls=%async_computation.6 | async-start | bytes 3670016 | tf_op jit(solution)/shard_map/psum | solution.py:142
  1576.3 11.5 copy-start.17
  1588.8 15.7 copy-start.23
  1630.7 4.1 copy-start.9
  1650.6 11.5 copy-start.13
  1650.6 11.7 copy-start.15
  1650.6 36.0 %copy-start.26 = (f32[128]{0:T(128)S(1)}, f32[128]{0:T(128)}, u32[]{:S(2)}) copy-start(f32[128]{0:T(128)} %get-tuple-element.31) | copy-start | bytes 1540
  1650.6 213.7 %copy-start.11 = (bf16[3,512,128]{2,1,0:T(8,128)(2,1)S(1)}, bf16[3,512,128]{2,1,0:T(8,128)(2,1)}, u32[]{:S(2)}) copy-start(bf16[3,512,128]{2,1,0:T(8,128)(2,1)} %param.21) | copy-start | bytes 1179652
  1905.4 13.8 copy-start.19
  1905.4 13.8 copy-start.21
  1919.3 66.9 %copy-start.1 = (bf16[3,512,128]{2,1,0:T(8,128)(2,1)S(1)}, bf16[3,512,128]{2,1,0:T(8,128)(2,1)}, u32[]{:S(2)}) copy-start(bf16[3,512,128]{2,1,0:T(8,128)(2,1)} %param.18) | copy-start | bytes 1179652
Sparse Core Ops, SparseCore 0:
  71.6 289.4 all-gather.2
  363.5 550.2 reduce-scatter.2
  1001.5 552.7 reduce-scatter.4
  1576.3 287.9 all-gather.4
  1919.4 58.8 all-reduce.17
where the time goes:
time: 2000 us; the launch traced here: 1990 us
  waiting for transfers between devices  1480 us (74%)
  matrix products  302 us (15%)
  local copies, waits for them, and re-layouts  83.7 us (4%)
  other arithmetic  73.9 us (4%)
  blocking collectives  38 us (2%)
    reduce_scatter x2, waiting for transfers between devices, input_grad(): return lax.psum_scatter(partial_sums, 'ch', scatter_dimension=2, tiled=True)  1030 us
    all_gather x2, waiting for transfers between devices, convolve(): gathered = lax.all_gather(shard, 'ch', axis=2, tiled=True)  410 us
    dot_general x2, matrix products, conv_local(): jnp.einsum('rti,kio->krto', inputs, weight, preferred_element_type=jnp.fl...  52.6 us
    dot_general x4, matrix products, adain_act(): jnp.einsum('rts,rtc->rsc', weights_seg, centered * centered, precision=hi...  45.2 us
    unnamed x67, local copies, waits for them, and re-layouts  44.7 us
    dot_general x4, matrix products, adain_act(): affine = jnp.einsum('rts,krsc->krtc', member, project, precision=highest)  44 us
    broadcast_in_dim x2, other arithmetic, adain_act(): hidden = (1.0 + affine[0]) * normed + affine[1]  42.4 us
    dot_general x4, matrix products, adain_act(): jnp.einsum('rts,rsc->rtc', member, scales, precision=highest)  41.9 us
  transfers between devices with their start and end apart: 5, of which 5 were waited for; matrix products, arithmetic and copies ran while one was open for 11% of the time, Pallas kernels for 0%

commit v1 on v0

v1 whole, which is shorter than its diff:
```python
import functools
import itertools
import math

import jax
import jax.numpy as jnp
from jax import lax
from jax.experimental import pallas as pl
from jax.experimental.pallas import tpu as pltpu
from jax.sharding import PartitionSpec as P

var_floor = 0.1
inv_root = math.sqrt(0.5)
highest = lax.Precision.HIGHEST
BLOCK = 16
NT = (((1,), (1,)), ((), ()))
TN = (((0,), (0,)), ((), ()))


def row_kernel(
    n, segs, style_n, per, start, at_f, at_c, n_prev, z_ref, len_ref, seg_ref, *refs
):
    f_own, c_own = refs[:2]
    recv_f, recv_c = refs[2 : n + 1], refs[n + 1 : 2 * n]
    style_ref, inv_ref, w_hbm = refs[2 * n : 2 * n + 3]
    prev = refs[2 * n + 3 : 2 * n + 3 + n_prev]
    refs = refs[2 * n + 3 + n_prev :]
    o_own, g_own, sum_hbm = refs[:3]
    outs = refs[3 : n + 2]
    dstyle_ref = refs[n + 2]
    fr, ct, res, sh, a3x, a3y, g3, conv, da, acc, coef, w_ref, wt_ref, sum_ref, sems = refs[n + 3 :]

    z = z_ref[0]
    length = len_ref[0]
    frames, chans = fr.shape
    width = chans // n
    blocks = frames // BLOCK
    wide = 3 * chans
    fc_at = 2 * wide
    bias_at = fc_at + 4 * style_n
    row_iota = (
        lax.broadcasted_iota(jnp.int32, (2, 8, chans), 0) * 8
        + lax.broadcasted_iota(jnp.int32, (2, 8, chans), 1)
    )
    edge = lax.broadcasted_iota(jnp.int32, (8, 128), 0)

    def lanes(k):
        return pl.ds(pl.multiple_of(lax.rem(z + n - k, n) * width, width), width)

    def span(b):
        return pl.ds(pl.multiple_of(b * BLOCK, BLOCK), BLOCK)

    def segment(b):
        return seg_ref[0, b + 1]

    def load(ref, b):
        return ref[span(b), :].astype(jnp.float32).reshape(2, 8, chans)

    def flat(v):
        return v.reshape(BLOCK, chans)

    def keep(b, v):
        return jnp.where(row_iota < length - b * BLOCK, v, 0.0)

    def loop(body, unroll=4):
        def step(i, carry):
            for j in range(unroll):
                body(i * unroll + j)
            return carry

        lax.fori_loop(0, blocks // unroll, step, 0)

    def total(slot):
        return jnp.sum(acc[slot], axis=1)

    def put(slot, v):
        coef[slot] = jnp.broadcast_to(v[:, None, :], (segs, 8, chans))

    def fc_rows(layer, k):
        at = fc_at + (2 * layer + k) * style_n
        return slice(at, at + style_n)

    count = itertools.count()

    def copy(src, dst):
        return pltpu.make_async_copy(src, dst, sems.at[next(count)])

    def begin(*copies):
        for c in copies:
            c.start()

    def finish_copies(*copies):
        for c in copies:
            c.wait()

    def pieces(own, start, received, dst):
        yield copy(own.at[z * per + start], dst.at[:, lanes(0)])
        for k, (ref, at) in enumerate(received, 1):
            yield copy(ref.at[pl.ds(at, frames), :], dst.at[:, lanes(k)])

    def weight_copies(layer):
        rows = pl.ds(layer * wide, wide)
        yield copy(w_hbm.at[rows, :], w_ref.at[rows, :])
        for k in range(3):
            rows = pl.ds(layer * wide + k * chans, chans)
            yield copy(w_hbm.at[rows, :], wt_ref.at[layer, :, k * chans : (k + 1) * chans])

    tail_rows = pl.ds(fc_at, w_ref.shape[0] - fc_at)
    layer_rows = [pl.ds(layer * wide, wide) for layer in range(2)]
    get_fr = list(pieces(f_own, start, zip(recv_f, at_f), fr))
    get_ct = list(pieces(c_own, start, zip(recv_c, at_c), ct))
    get_tail = copy(w_hbm.at[tail_rows, :], w_ref.at[tail_rows, :])
    get_w = [list(weight_copies(layer)) for layer in range(2)]
    begin(*get_fr, get_tail, *get_w[0], *get_w[1], *get_ct)
    get_sums = []
    if n_prev:
        get_sums = [copy(prev[2].at[r, :], sum_ref.at[r, :]) for r in (*layer_rows, tail_rows)]
        begin(*get_sums[::-1])
    else:
        sum_ref[...] = jnp.zeros_like(sum_ref)
    put_sums = [copy(sum_ref.at[r, :], sum_hbm.at[r, :]) for r in (*layer_rows, tail_rows)]

    def put_result(which):
        yield copy(res.at[:, lanes(0)], (o_own, g_own)[which].at[z * per + start])
        for k in range(1, n):
            yield copy(res.at[:, lanes(k)], outs[k - 1].at[which, 0])

    for j in range(chans // 128):
        sh[j, 0:8, :] = jnp.zeros((8, 128), jnp.float32)
        sh[j, 8 + frames :, :] = jnp.zeros((8, 128), jnp.float32)

    inv_count = inv_ref[0]
    style = style_ref[0].astype(jnp.float32)
    finish_copies(*get_fr, get_tail)
    biases = w_ref[bias_at : bias_at + BLOCK, :].astype(jnp.float32)

    def project(layer, k):
        proj = jnp.dot(
            style, w_ref[fc_rows(layer, k), :].astype(jnp.float32),
            precision=highest, preferred_element_type=jnp.float32,
        )
        return proj + biases[2 * layer + k : 2 * layer + k + 1]

    def hold(b, v):
        at = pl.ds(pl.multiple_of(b * BLOCK + 8, 8), BLOCK)
        v = flat(v)
        for j in range(chans // 128):
            sh[j, at, :] = v[:, j * 128 : (j + 1) * 128]

    def statistics(src, layer):
        base = layer * 6
        acc[0] = jnp.zeros_like(acc[0])

        def add_values(b):
            v = keep(b, load(src, b))
            acc[0, segment(b)] += v[0] + v[1]

        loop(add_values)
        put(base, total(0) * inv_count)
        acc[0] = jnp.zeros_like(acc[0])

        def add_squares(b):
            s = segment(b)
            c = keep(b, load(src, b) - coef[base, s])
            c = c * c
            acc[0, s] += c[0] + c[1]

        loop(add_squares)
        var = total(0) * inv_count
        rstd = lax.rsqrt(jnp.maximum(var, var_floor))
        put(base + 1, (1.0 + project(layer, 0)) * rstd)
        put(base + 2, project(layer, 1))
        put(base + 3, rstd)
        put(base + 4, jnp.where(var > var_floor, rstd, 0.0) * inv_count)

    def activation(src, layer):
        base = layer * 6

        def body(b):
            s = segment(b)
            u = coef[base + 1, s] * (load(src, b) - coef[base, s]) + coef[base + 2, s]
            hold(b, keep(b, u * (0.5 * jnp.tanh(0.5 * u) + 0.5)))

        loop(body)

    def spread(dst, first):
        last = 2 - first

        def body(b):
            s = segment(b)
            from_row = jnp.where(seg_ref[0, b] == s, 0, 1)
            to_row = jnp.where(seg_ref[0, b + 2] == s, 8, 7)
            for j in range(chans // 128):

                def part(off):
                    return sh[j, pl.ds(b * BLOCK + off, 8), :]

                def store(tap, low, high):
                    at = tap * chans + j * 128
                    v = jnp.concatenate([low, high], axis=0)
                    dst[span(b), at : at + 128] = v.astype(dst.dtype)

                store(first, jnp.where(edge >= from_row, part(7), 0.0), part(15))
                store(1, part(8), part(16))
                store(last, part(9), jnp.where(edge < to_row, part(17), 0.0))

        loop(body)

    tile = min(frames, 1024)

    def convolve(dst, src, layer):
        def body(i, carry):
            at = pl.ds(pl.multiple_of(i * tile, tile), tile)
            dst[at, :] = jnp.dot(
                src[at, :], w_ref[layer * wide : (layer + 1) * wide, :],
                preferred_element_type=jnp.float32,
            )
            return carry

        lax.fori_loop(0, frames // tile, body, 0)

    def input_grad(dst, src, layer):
        def body(i, carry):
            at = pl.ds(pl.multiple_of(i * tile, tile), tile)
            dst[at, :] = lax.dot_general(
                src[at, :], wt_ref[layer], NT, preferred_element_type=jnp.float32
            )
            return carry

        lax.fori_loop(0, frames // tile, body, 0)

    def weight_grad(layer, kept, grads):
        def body(i, carry):
            at = pl.ds(pl.multiple_of(i * 256, 256), 256)
            to = pl.ds(pl.multiple_of(layer * wide + i * 256, 256), 256)
            sum_ref[to, :] += lax.dot_general(
                kept[:, at], grads[:, chans : 2 * chans], TN, preferred_element_type=jnp.float32
            )
            return carry

        lax.fori_loop(0, wide // 256, body, 0)

    def backward(src, layer):
        base = layer * 6
        acc[...] = jnp.zeros_like(acc)

        def body(b):
            s = segment(b)
            c = load(src, b) - coef[base, s]
            u = coef[base + 1, s] * c + coef[base + 2, s]
            sig = 0.5 * jnp.tanh(0.5 * u) + 0.5
            du = keep(b, load(da, b) * (sig * (1.0 + u * (1.0 - sig))))
            da[span(b), :] = flat(du)
            acc[0, s] += du[0] + du[1]
            duc = du * c
            acc[1, s] += duc[0] + duc[1]

        loop(body)
        dbeta = total(0)
        dgain = total(1) * coef[base + 3, :, 0, :]
        put(base + 4, coef[base + 4, :, 0, :] * dgain)
        put(base + 5, inv_count * dbeta)
        for k, d in enumerate((dgain, dbeta)):
            at = fc_rows(layer, k)
            sum_ref[at, :] += lax.dot_general(
                style, d, TN, precision=highest, preferred_element_type=jnp.float32
            )
            dstyle_ref[0] += lax.dot_general(
                d, w_ref[at, :].astype(jnp.float32), NT,
                precision=highest, preferred_element_type=jnp.float32,
            )
        return [jnp.sum(dgain, axis=0, keepdims=True), jnp.sum(dbeta, axis=0, keepdims=True)]

    def value_grad(src, layer, b):
        base = layer * 6
        s = segment(b)
        c = load(src, b) - coef[base, s]
        dv = coef[base + 1, s] * (load(da, b) - (c * coef[base + 4, s] + coef[base + 5, s]))
        return keep(b, dv)

    statistics(fr, 0)
    activation(fr, 0)
    spread(a3x, 0)
    finish_copies(*get_w[0])
    convolve(conv, a3x, 0)
    statistics(conv, 1)
    activation(conv, 1)
    spread(a3y, 0)
    finish_copies(*get_w[1], *get_ct)
    convolve(da, a3y, 1)
    bias = biases[4:5]
    acc[0, 0] = jnp.zeros_like(acc[0, 0])

    def finish(b):
        y = keep(b, load(da, b) + bias[None])
        res[span(b), :] = flat((load(fr, b) + y) * inv_root).astype(res.dtype)
        g = keep(b, load(ct, b) * inv_root).astype(jnp.bfloat16).astype(jnp.float32)
        hold(b, g)
        acc[0, 0] += g[0] + g[1]

    loop(finish)
    bias_sum = jnp.sum(acc[0, 0], axis=0, keepdims=True)
    put_output = list(put_result(0))
    begin(*put_output)

    dstyle_ref[...] = jnp.zeros_like(dstyle_ref)
    spread(g3, 2)
    finish_copies(*get_sums)
    weight_grad(1, a3y, g3)
    begin(put_sums[1])
    input_grad(da, g3, 1)
    rows_two = backward(conv, 1)

    def round_grad(b):
        hold(b, value_grad(conv, 1, b).astype(jnp.bfloat16).astype(jnp.float32))

    loop(round_grad)
    spread(g3, 2)
    weight_grad(0, a3x, g3)
    begin(put_sums[0])
    input_grad(da, g3, 0)
    rows_one = backward(fr, 0)

    sum_ref[bias_at : bias_at + 8, :] += jnp.concatenate(
        rows_one + rows_two + [bias_sum, jnp.zeros((3, chans), jnp.float32)], axis=0
    )
    begin(put_sums[2])
    finish_copies(*put_output)

    def frames_grad(b):
        dv = value_grad(fr, 0, b)
        res[span(b), :] = flat(load(ct, b) * inv_root + dv).astype(res.dtype)

    loop(frames_grad)
    put_grads = list(put_result(1))
    begin(*put_grads)
    finish_copies(*put_grads, *put_sums)


def block_rows(
    n, per, start, z, lengths, seg_blocks, frames, cotangent, recv_f, recv_c, style, inv, weights, prev
):
    frames_n, width = frames.shape[1:]
    chans = width * n
    segs, style_n = style.shape[1:]
    flat_n = weights.shape[0]
    f32 = jnp.float32

    def here(r, *_):
        return (start + r, 0, 0)

    any_space = pl.BlockSpec(memory_space=pl.ANY)
    sums = jax.ShapeDtypeStruct((flat_n, chans), f32)
    piece = jax.ShapeDtypeStruct((2, 1, frames_n, width), jnp.bfloat16)
    in_specs = (
        [any_space] * 2 * n
        + [pl.BlockSpec((1, segs, style_n), here), pl.BlockSpec((1, segs, chans), here)]
        + [any_space] * (1 + len(prev))
    )
    out_specs = [any_space] * (n + 2) + [pl.BlockSpec((1, segs, style_n), lambda *_: (0, 0, 0))]
    out_shape = (
        [jax.ShapeDtypeStruct(frames.shape, jnp.bfloat16)] * 2
        + [sums]
        + [piece] * (n - 1)
        + [jax.ShapeDtypeStruct((1, segs, style_n), f32)]
    )
    scratch = [
        pltpu.VMEM((frames_n, chans), jnp.bfloat16),
        pltpu.VMEM((frames_n, chans), jnp.bfloat16),
        pltpu.VMEM((frames_n, chans), jnp.bfloat16),
        pltpu.VMEM((chans // 128, frames_n + 16, 128), f32),
        pltpu.VMEM((frames_n, 3 * chans), jnp.bfloat16),
        pltpu.VMEM((frames_n, 3 * chans), jnp.bfloat16),
        pltpu.VMEM((frames_n, 3 * chans), jnp.bfloat16),
        pltpu.VMEM((frames_n, chans), f32),
        pltpu.VMEM((frames_n, chans), f32),
        pltpu.VMEM((2, segs, 8, chans), f32),
        pltpu.VMEM((12, segs, 8, chans), f32),
        pltpu.VMEM((flat_n, chans), jnp.bfloat16),
        pltpu.VMEM((2, chans, 3 * chans), jnp.bfloat16),
        pltpu.VMEM((flat_n, chans), f32),
        pltpu.SemaphoreType.DMA((4 * n + 16,)),
    ]
    first_prev = 3 + 2 * n + 3
    return pl.pallas_call(
        functools.partial(
            row_kernel, n, segs, style_n, per, start,
            [at for _, at in recv_f], [at for _, at in recv_c], len(prev),
        ),
        grid_spec=pltpu.PrefetchScalarGridSpec(
            num_scalar_prefetch=3,
            grid=(1,),
            in_specs=in_specs,
            out_specs=out_specs,
            scratch_shapes=scratch,
        ),
        out_shape=out_shape,
        input_output_aliases={first_prev + i: i for i in range(len(prev))},
        compiler_params=pltpu.CompilerParams(vmem_limit_bytes=48 << 20),
        cost_estimate=pl.CostEstimate(
            flops=6 * 2 * 3 * frames_n * chans * chans,
            bytes_accessed=8 * frames_n * chans + 10 * flat_n * chans,
            transcendentals=4 * frames_n * chans,
        ),
    )(
        z, lengths, seg_blocks, frames, cotangent,
        *[v for v, _ in recv_f], *[v for v, _ in recv_c], style, inv, weights, *prev,
    )


def per_device(
    n,
    n_rows,
    frames,
    style_vector,
    segment_ids,
    padding,
    fc1_weight,
    fc1_bias,
    conv1_weight,
    fc2_weight,
    fc2_bias,
    conv2_weight,
    conv2_bias,
    cotangent,
):
    f32 = jnp.float32
    held, frames_n, width = frames.shape
    segs, style_n = style_vector.shape[1:]
    chans = n * width
    per = held // n
    z = lax.axis_index("ch")

    def shift(k):
        return [(i, (i + k) % n) for i in range(n)]

    def send(v, k):
        return lax.ppermute(v, "ch", shift(k))

    def over_ch(v, pieces, axis):
        whole = jnp.concatenate([v] * n, axis=axis)
        size = v.shape[axis]
        for k, piece in enumerate(pieces, 1):
            at = lax.rem(z + n - k, n) * size
            whole = lax.dynamic_update_slice_in_dim(whole, piece, at, axis)
        return whole

    def after(v, others):
        return lax.optimization_barrier((v, others))[0]

    sizes = [3 * chans, 3 * chans, 2 * style_n, 2 * style_n, 2, 2, 1]
    used = sum(sizes)
    padded = -(-used // (16 * n_rows)) * 16 * n_rows
    shard = jnp.concatenate(
        [
            conv1_weight.reshape(-1, width),
            conv2_weight.reshape(-1, width),
            fc1_weight.reshape(-1, width),
            fc2_weight.reshape(-1, width),
            fc1_bias,
            fc2_bias,
            conv2_bias[None],
            jnp.zeros((padded - used, width), conv1_weight.dtype),
        ]
    )
    part = padded // n_rows
    mine = lax.dynamic_slice_in_dim(shard, lax.axis_index("rows") * part, part, 0)

    def piece(v, k, r):
        at = lax.rem(z + k, n) * per + r
        return lax.dynamic_slice_in_dim(v, at, 1, 0)[0]

    recv_f, recv_c, weight_pieces = [], [], []
    for r in range(per):
        got_f, got_c = [], []
        for k in range(1, n):
            f, c = piece(frames, k, r), piece(cotangent, k, r)
            if r == 0:
                both = send(jnp.concatenate([f, mine]), k)
                got_f.append((both, 0))
                weight_pieces.append(both[frames_n:])
                got_c.append((send(c, k), 0))
            else:
                both = send(jnp.concatenate([f, c]), k)
                got_f.append((both, 0))
                got_c.append((both, frames_n))
        recv_f.append(got_f)
        recv_c.append(got_c)
    mine = after(over_ch(mine, weight_pieces, 1), [recv_c[0][0][0]])
    weights = lax.all_gather(mine, "rows", axis=0, tiled=True)

    first = z * per
    my_ids = lax.dynamic_slice_in_dim(segment_ids, first, per, 0)
    my_pad = lax.dynamic_slice_in_dim(padding, first, per, 0)
    my_style = lax.dynamic_slice_in_dim(style_vector, first, per, 0)
    lengths = jnp.sum(my_pad, axis=1).astype(jnp.int32)
    side = jnp.full((per, 1), -1, jnp.int32)
    seg_blocks = jnp.concatenate([side, my_ids[:, ::BLOCK], side], axis=1)
    counts = jnp.sum(
        jnp.where(my_ids[:, :, None] == jnp.arange(segs, dtype=jnp.int32), my_pad[:, :, None], 0),
        axis=1,
    ).astype(f32)
    inv_count = jnp.broadcast_to(
        (1.0 / jnp.maximum(counts, 1.0))[:, :, None], (per, segs, chans)
    )

    prev, back, dstyles = [], [], []
    for r in range(per):
        results = block_rows(
            n, per, r, z[None], lengths[r : r + 1], seg_blocks[r : r + 1], frames, cotangent,
            recv_f[r], recv_c[r], my_style, inv_count, weights, prev,
        )
        prev = list(results[:3])
        dstyles.append(results[n + 2])
        back.append([send(v, n - k) for k, v in enumerate(results[3 : n + 2], 1)])

    output, grad_frames, sums = prev
    for r in range(per):
        for k in range(1, n):
            at = lax.rem(z + k, n) * per + r
            output = lax.dynamic_update_slice_in_dim(output, back[r][k - 1][0], at, 0)
            grad_frames = lax.dynamic_update_slice_in_dim(grad_frames, back[r][k - 1][1], at, 0)

    style_grad = jnp.concatenate(dstyles, axis=0)
    grad_style = over_ch(style_grad, [send(style_grad, k) for k in range(1, n)], 0)

    sums = after(sums, back[0])
    sums = lax.psum_scatter(sums, "rows", scatter_dimension=0, tiled=True)
    sums = after(sums, back[1])
    total = lax.dynamic_slice_in_dim(sums, z * width, width, 1)
    for k in range(1, n):
        at = lax.rem(z + k, n) * width
        total = total + send(lax.dynamic_slice_in_dim(sums, at, width, 1), k)
    total = after(total, back[2])
    grads = lax.all_gather(total, "rows", axis=0, tiled=True)
    splits = [sum(sizes[: i + 1]) for i in range(len(sizes))]
    g1, g2, gf1, gf2, gb1, gb2, gb = [
        grads[end - size : end] for size, end in zip(sizes, splits)
    ]
    return (
        output,
        grad_frames,
        grad_style,
        gf1.reshape(fc1_weight.shape),
        gb1,
        g1.reshape(conv1_weight.shape),
        gf2.reshape(fc2_weight.shape),
        gb2,
        g2.reshape(conv2_weight.shape),
        gb[0],
    )


def solution(mesh):
    return jax.shard_map(
        functools.partial(per_device, mesh.shape["ch"], mesh.shape["rows"]),
        mesh=mesh,
        in_specs=(
            P("rows", None, "ch"),
            P("rows", None, None),
            P("rows", None),
            P("rows", None),
            P(None, None, "ch"),
            P(None, "ch"),
            P(None, None, "ch"),
            P(None, None, "ch"),
            P(None, "ch"),
            P(None, None, "ch"),
            P("ch"),
            P("rows", None, "ch"),
        ),
        out_specs=(
            P("rows", None, "ch"),
            P("rows", None, "ch"),
            P("rows", None, None),
            P(None, None, "ch"),
            P(None, "ch"),
            P(None, None, "ch"),
            P(None, None, "ch"),
            P(None, "ch"),
            P(None, None, "ch"),
            P("ch"),
        ),
        check_vma=False,
    )
```

time: 2000 us -> 459 us (0.23)
  waiting for transfers between devices: 1480 us -> 133 us
  matrix products: 302 us -> 0 us
  Pallas kernels: 0 us -> 123 us
  starting transfers between devices: 0.21 us -> 115 us
  other arithmetic: 73.9 us -> 19.5 us
  local copies, waits for them, and re-layouts: 83.7 us -> 45.6 us
  blocking collectives: 38 us -> 0 us
    reduce_scatter x2 -> x1, waiting for transfers between devices: 1030 us -> 0.01 us  [per_device(): sums = lax.psum_scatter(sums, 'rows', scatter_dimension=0, tiled=True)]
    all_gather x2, waiting for transfers between devices: 410 us -> 0.01 us  [the longest x1 0.01 us: per_device(): weights = lax.all_gather(mine, 'rows', axis=0, tiled=True)]
    dot_general x32 -> x0, matrix products: 302 us -> none  [the longest x2 52.6 us: conv_local(): jnp.einsum('rti,kio->krto', inputs, weight, preferred_element_type=jnp.fl...]
    ppermute x0 -> x33, waiting for transfers between devices: none -> 133 us  [send(): return lax.ppermute(v, 'ch', shift(k))]
    pallas_call x0 -> x4, Pallas kernels: none -> 123 us  [block_rows(): pl.pallas_call(functools.partial(row_kernel, n, segs, style_n, per, start...]
    ppermute x0 -> x33, starting transfers between devices: none -> 115 us  [send(): return lax.ppermute(v, 'ch', shift(k))]
    broadcast_in_dim x2 -> x0, other arithmetic: 42.4 us -> none  [adain_act(): hidden = (1.0 + affine[0]) * normed + affine[1]]
    unnamed x67 -> x54, local copies, waits for them, and re-layouts: 44.7 us -> 6.12 us
  transfers between devices with their start and end apart: 5 -> 36, of which waited for: 5 -> 9; matrix products, arithmetic and copies ran while one was open for 11% -> 9% of each run, Pallas kernels for 0% -> 27%
where the time goes in v1:
time: 459 us; the launch traced here: 450 us
  waiting for transfers between devices  133 us (29%)
  Pallas kernels  123 us (27%)
  starting transfers between devices  115 us (25%)
  local copies, waits for them, and re-layouts  45.6 us (10%)
  other arithmetic  19.5 us (4%)
  between operations  14.6 us (3%)
    ppermute x33, waiting for transfers between devices, send(): return lax.ppermute(v, 'ch', shift(k))  133 us
    pallas_call x4, Pallas kernels, block_rows(): pl.pallas_call(functools.partial(row_kernel, n, segs, style_n, per, start...  123 us
    ppermute x33, starting transfers between devices, send(): return lax.ppermute(v, 'ch', shift(k))  115 us
    dynamic_update_slice x12, local copies, waits for them, and re-layouts, per_device(): lax.dynamic_update_slice_in_dim(grad_frames, back[r][k - 1][1], at, 0)  19.2 us
    concatenate x9, other arithmetic, per_device(): both = send(jnp.concatenate([f, c]), k)  15.6 us
  transfers between devices with their start and end apart: 36, of which 9 were waited for; matrix products, arithmetic and copies ran while one was open for 9% of the time, Pallas kernels for 27%

profile of v1, /device:TPU:0, one launch (start us, length us, event | category | flops | bytes accessed | tf_op | source)
XLA Modules:
  0.0 450.5 jit_solution(3990864686993983664)
XLA Ops:
  7.3 6.4 %concatenate.56 = bf16[3712,128]{1,0:T(8,128)(2,1)S(1)} concatenate(bf16[1536,128]{1,0:T(8,128)(2,1)} %bitcast.158, bf16[1536,128]{1,0:T(8,128)(2,1)} %bitcast.159, bf16[256,128]{1,0:T(8,128)(2,1)} %bitcast.162, bf16[256,128]{1,0:T(8,128)(2,1)} %bitcast.163, bf16[2,128]{1,0:T(2,128)(2,1)} %param.17, bf16[2,128]{1,0:T(2,128)(2,1)} %param.20, bf16[1,128]{1,0:T(2,128)(2,1)} %bitcast.164, ...), dimensions={0} | concatenate | bytes 1900544 | tf_op jit(solution)/shard_map/concatenate | solution.py:454
  13.8 3.2 dynamic-slice_bitcast_fusion.3
  17.0 1.0 pad_maximum_fusion
  18.1 3.0 collective-permute-start.3
  21.1 2.6 collective-permute-start.4
  23.7 1.3 collective-permute-start.5
  25.0 1.6 dynamic-slice_bitcast_fusion
  27.3 5.8 %collective-permute-done.3.refs_2_ = bf16[1488,128]{1,0:T(8,128)(2,1)S(1)} collective-permute-done((bf16[1488,128]{1,0:T(8,128)(2,1)}, bf16[1488,128]{1,0:T(8,128)(2,1)S(1)}, u32[]{:S(2)}, u32[]{:S(2)}) %collective-permute-start.3) | collective-permute-done | bytes 380960 | tf_op jit(solution)/shard_map/ppermute | solution.py:438
  33.2 16.3 %collective-permute-done.4.refs_3_ = bf16[1488,128]{1,0:T(8,128)(2,1)S(1)} collective-permute-done((bf16[1488,128]{1,0:T(8,128)(2,1)}, bf16[1488,128]{1,0:T(8,128)(2,1)S(1)}, u32[]{:S(2)}, u32[]{:S(2)}) %collective-permute-start.4) | collective-permute-done | bytes 380960 | tf_op jit(solution)/shard_map/ppermute | solution.py:438
  49.6 4.7 %collective-permute-done.6.refs_5_ = bf16[1024,128]{1,0:T(8,128)(2,1)S(1)} collective-permute-done((bf16[1024,128]{1,0:T(8,128)(2,1)S(1)}, bf16[1024,128]{1,0:T(8,128)(2,1)S(1)}, u32[]{:S(2)}, u32[]{:S(2)}) %collective-permute-start.6) | collective-permute-done | bytes 262176 | tf_op jit(solution)/shard_map/ppermute | solution.py:438
  54.4 8.8 %collective-permute-start.13 = (bf16[1024,128]{1,0:T(8,128)(2,1)}, bf16[1024,128]{1,0:T(8,128)(2,1)S(1)}, u32[]{:S(2)}, u32[]{:S(2)}) collective-permute-start(bf16[1024,128]{1,0:T(8,128)(2,1)} %get-tuple-element.77), channel_id=1, source_target_pairs={{0,2},{1,3},{2,0},{3,1},{4,6},{5,7},{6,4},{7,5},{8,10},{9,11},{10,... | collective-permute-start | bytes 786440 | tf_op jit(solution)/shard_map/ppermute | solution.py:438
  63.2 3.0 collective-permute-start.14
  66.2 1.9 pad_maximum_fusion.9
  68.1 1.8 pad_maximum_fusion.10
  70.5 1.8 pad_maximum_fusion.11
  72.3 3.3 collective-permute-start.12
  75.6 0.9 fusion.24
  77.5 1.9 pad_maximum_fusion.6
  79.4 1.9 pad_maximum_fusion.7
  81.2 1.8 pad_maximum_fusion.8
  83.1 1.8 pad_maximum_fusion.4
  84.8 1.9 pad_maximum_fusion.5
  86.8 0.8 pad_maximum_fusion.3
  88.2 15.7 %collective-permute-start.8 = (bf16[2048,128]{1,0:T(8,128)(2,1)}, bf16[2048,128]{1,0:T(8,128)(2,1)}, u32[]{:S(2)}, u32[]{:S(2)}) collective-permute-start(bf16[2048,128]{1,0:T(8,128)(2,1)} %pad_maximum_fusion.7), channel_id=1, source_target_pairs={{0,2},{1,3},{2,0},{3,1},{4,6},{5,7},{6,4},{7,5},{8,10},{9,11},{10,... | collective-permute-start | bytes 1572872 | tf_op jit(solution)/shard_map/ppermute | solution.py:438
  104.0 30.7 %shard_map.195 = (bf16[16,1024,128]{2,1,0:T(8,128)(2,1)}, bf16[16,1024,128]{2,1,0:T(8,128)(2,1)}, f32[3712,512]{1,0:T(8,128)}, bf16[2,1,1024,128]{3,2,1,0:T(8,12...) custom-call(s32[1]{0:T(128)} %bitcast.z_ref, ...), custom_call_target="tpu_custom_call" | custom-call | flops 9663676416 | bytes 23199744 | tf_op jit(solution)/shard_map/pallas_call | solution.py:385
  134.7 3.3 collective-permute-start.9
  138.9 31.0 %collective-permute-start.2 = (bf16[2048,128]{1,0:T(8,128)(2,1)S(1)}, bf16[2048,128]{1,0:T(8,128)(2,1)S(1)}, u32[]{:S(2)}, u32[]{:S(2)}) collective-permute-start(bf16[2048,128]{1,0:T(8,128)(2,1)S(1)} %copy-done.11), channel_id=1, source_target_pairs={{0,3},{1,0},{2,1},{3,2},{4,7},{5,4},{6,5},{7,6},{8,11},{9,8},{10,9... | collective-permute-start | bytes 1572872 | tf_op jit(solution)/shard_map/ppermute | solution.py:438
  169.8 1.0 copy-done.6
  170.9 30.8 %shard_map.196 = (bf16[16,1024,128]{2,1,0:T(8,128)(2,1)}, bf16[16,1024,128]{2,1,0:T(8,128)(2,1)}, f32[3712,512]{1,0:T(8,128)}, bf16[2,1,1024,128]{3,2,1,0:T(8,12...) custom-call(s32[1]{0:T(128)} %bitcast.z_ref, ...), custom_call_target="tpu_custom_call", output_to_operand_aliasing={{0}: (14, {}), {1}: (15, {}), {2}: (16, {})} | custom-call | flops 9663676416 | bytes 23199744 | tf_op jit(solution)/shard_map/pallas_call | solution.py:385
  201.7 0.8 copy-done.2
  204.6 3.5 collective-permute-start.15
  208.3 30.7 %shard_map.197 = (bf16[16,1024,128]{2,1,0:T(8,128)(2,1)}, bf16[16,1024,128]{2,1,0:T(8,128)(2,1)}, f32[3712,512]{1,0:T(8,128)}, bf16[2,1,1024,128]{3,2,1,0:T(8,12...) custom-call(s32[1]{0:T(128)} %bitcast.z_ref, ...), custom_call_target="tpu_custom_call", output_to_operand_aliasing={{0}: (14, {}), {1}: (15, {}), {2}: (16, {})} | custom-call | flops 9663676416 | bytes 23199744 | tf_op jit(solution)/shard_map/pallas_call | solution.py:385
  239.7 30.6 %shard_map.198 = (bf16[16,1024,128]{2,1,0:T(8,128)(2,1)}, bf16[16,1024,128]{2,1,0:T(8,128)(2,1)}, f32[3712,512]{1,0:T(8,128)}, bf16[2,1,1024,128]{3,2,1,0:T(8,12...) custom-call(s32[1]{0:T(128)} %bitcast.z_ref, ...), custom_call_target="tpu_custom_call", output_to_operand_aliasing={{0}: (14, {}), {1}: (15, {}), {2}: (16, {})} | custom-call | flops 9663676416 | bytes 23199744 | tf_op jit(solution)/shard_map/pallas_call | solution.py:385
  271.3 0.8 copy-done.17
  272.2 3.4 collective-permute-start.18
  275.6 0.9 collective-permute-start.19
  276.6 3.8 collective-permute-start.21
  280.7 10.3 %collective-permute-done.18 = bf16[2,1,1024,128]{3,2,1,0:T(8,128)(2,1)S(1)} collective-permute-done((bf16[2,1,1024,128]{3,2,1,0:T(8,128)(2,1)}, bf16[2,1,1024,128]{3,2,1,0:T(8,128)(2,1)S(1)}, u32[]{:S(2)}, u32[]{:S(2)}) %collective-permute-start.18) | collective-permute-done | bytes 524320 | tf_op jit(solution)/shard_map/ppermute | solution.py:438
  291.0 21.7 %collective-permute-start.23 = (bf16[2,1,1024,128]{3,2,1,0:T(8,128)(2,1)S(1)}, bf16[2,1,1024,128]{3,2,1,0:T(8,128)(2,1)}, u32[]{:S(2)}, u32[]{:S(2)}) collective-permute-start(bf16[2,1,1024,128]{3,2,1,0:T(8,128)(2,1)S(1)} %get-tuple-element.61), channel_id=1, source_target_pairs={{0,1},{1,2},{2,3},{3,0},{4,5},{5,6},{6,7},{7,4},{8,9},{9,10},{10,1... | collective-permute-start | bytes 1572872 | tf_op jit(solution)/shard_map/ppermute | solution.py:438
  312.7 33.2 %collective-permute-done.19 = bf16[2,1,1024,128]{3,2,1,0:T(8,128)(2,1)} collective-permute-done((bf16[2,1,1024,128]{3,2,1,0:T(8,128)(2,1)}, bf16[2,1,1024,128]{3,2,1,0:T(8,128)(2,1)}, u32[]{:S(2)}, u32[]{:S(2)}) %collective-permute-start.19) | collective-permute-done | bytes 524320 | tf_op jit(solution)/shard_map/ppermute | solution.py:438
  345.9 1.2 constant_dynamic-slice_fusion.2
  347.3 7.8 %collective-permute-done.30 = f32[464,128]{1,0:T(8,128)S(1)} collective-permute-done((f32[464,128]{1,0:T(8,128)S(1)}, f32[464,128]{1,0:T(8,128)S(1)}, u32[]{:S(2)}, u32[]{:S(2)}) %collective-permute-start.30) | collective-permute-done | bytes 237600 | tf_op jit(solution)/shard_map/ppermute | solution.py:438
  355.9 25.3 %collective-permute-done.31 = f32[464,128]{1,0:T(8,128)S(1)} collective-permute-done((f32[464,128]{1,0:T(8,128)S(1)}, f32[464,128]{1,0:T(8,128)S(1)}, u32[]{:S(2)}, u32[]{:S(2)}) %collective-permute-start.31) | collective-permute-done | bytes 237600 | tf_op jit(solution)/shard_map/ppermute | solution.py:438
  381.2 3.2 collective-permute-done.32
  384.4 1.7 add_add_fusion
  386.1 3.0 collective-permute-start.29
  389.1 1.5 collective-permute-start.24
  391.3 1.9 fusion.11
  393.1 1.9 fusion.10
  395.0 1.9 fusion.9
  396.9 1.9 fusion.8
  398.7 1.9 fusion.7
  400.6 1.9 fusion.6
  402.4 1.9 fusion.5
  404.3 1.9 fusion.4
  406.1 1.9 fusion.3
  408.0 0.8 fusion.2
  408.9 26.2 %collective-permute-done.25 = bf16[2,1,1024,128]{3,2,1,0:T(8,128)(2,1)S(1)} collective-permute-done((bf16[2,1,1024,128]{3,2,1,0:T(8,128)(2,1)S(1)}, bf16[2,1,1024,128]{3,2,1,0:T(8,128)(2,1)S(1)}, u32[]{:S(2)}, u32[]{:S(2)}) %collective-permute-start.25) | collective-permute-done | bytes 524320 | tf_op jit(solution)/shard_map/ppermute | solution.py:438
  435.0 0.8 fusion.1
  435.9 0.8 fusion
  436.7 2.6 fusion.25
  439.3 1.7 fusion.27
  441.0 1.3 fusion.26
  442.3 1.2 slice_bitcast_fusion.24
  (121 shorter events, 10.0 us)
Async XLA Ops:
  7.2 79.6 %copy-start = (bf16[16,4,128]{2,1,0:T(4,128)(2,1)S(1)}, bf16[16,4,128]{2,1,0:T(4,128)(2,1)}, u32[]{:S(2)}) copy-start(bf16[16,4,128]{2,1,0:T(4,128)(2,1)} %param.13) | copy-start | bytes 49156
  7.2 96.7 %all-gather.3.cloned.1.call-start = ((), (), s32[]{:S(2)}) async-start(), calls=%async_computation.1 | async-start | bytes 4276224 | tf_op jit(solution)/shard_map/all_gather | solution.py:490
  13.8 11.2 %copy-start.7 = (bf16[16,1024,128]{2,1,0:T(8,128)(2,1)S(1)}, bf16[16,1024,128]{2,1,0:T(8,128)(2,1)}, u32[]{:S(2)}) copy-start(bf16[16,1024,128]{2,1,0:T(8,128)(2,1)} %refs_1_.7) | copy-start | bytes 12582916
  18.1 15.1 %collective-permute-start.3 = (bf16[1488,128]{1,0:T(8,128)(2,1)}, bf16[1488,128]{1,0:T(8,128)(2,1)S(1)}, u32[]{:S(2)}, u32[]{:S(2)}) collective-permute-start(bf16[1488,128]{1,0:T(8,128)(2,1)} %get-tuple-element.135), channel_id=1, source_target_pairs={{0,1},{1,2},{2,3},{3,0},{4,5},{5,6},{6,7},{7,4},{8,9},{9,10},{10,1... | collective-permute-start | bytes 1142792 | tf_op jit(solution)/shard_map/ppermute | solution.py:438
  21.1 28.4 %collective-permute-start.4 = (bf16[1488,128]{1,0:T(8,128)(2,1)}, bf16[1488,128]{1,0:T(8,128)(2,1)S(1)}, u32[]{:S(2)}, u32[]{:S(2)}) collective-permute-start(bf16[1488,128]{1,0:T(8,128)(2,1)} %get-tuple-element.134), channel_id=1, source_target_pairs={{0,2},{1,3},{2,0},{3,1},{4,6},{5,7},{6,4},{7,5},{8,10},{9,11},{10,... | collective-permute-start | bytes 1142792 | tf_op jit(solution)/shard_map/ppermute | solution.py:438
  23.7 25.8 %collective-permute-start.5 = (bf16[1488,128]{1,0:T(8,128)(2,1)}, bf16[1488,128]{1,0:T(8,128)(2,1)S(1)}, u32[]{:S(2)}, u32[]{:S(2)}) collective-permute-start(bf16[1488,128]{1,0:T(8,128)(2,1)} %get-tuple-element.133), channel_id=1, source_target_pairs={{0,3},{1,0},{2,1},{3,2},{4,7},{5,4},{6,5},{7,6},{8,11},{9,8},{10,9... | collective-permute-start | bytes 1142792 | tf_op jit(solution)/shard_map/ppermute | solution.py:438
  26.6 27.7 %collective-permute-start.6 = (bf16[1024,128]{1,0:T(8,128)(2,1)S(1)}, bf16[1024,128]{1,0:T(8,128)(2,1)S(1)}, u32[]{:S(2)}, u32[]{:S(2)}) collective-permute-start(bf16[1024,128]{1,0:T(8,128)(2,1)S(1)} %get-tuple-element.84), channel_id=1, source_target_pairs={{0,1},{1,2},{2,3},{3,0},{4,5},{5,6},{6,7},{7,4},{8,9},{9,10},{10,1... | collective-permute-start | bytes 786440 | tf_op jit(solution)/shard_map/ppermute | solution.py:438
  49.6 4.7 %copy-start.8 = (bf16[464,512]{1,0:T(8,128)(2,1)}, bf16[464,512]{1,0:T(8,128)(2,1)S(1)}, u32[]{:S(2)}) copy-start(bf16[464,512]{1,0:T(8,128)(2,1)S(1)} %slice_dynamic-update-slice_fusion) | copy-start | bytes 1425412
  54.3 28.7 %copy-start.10 = (bf16[1024,128]{1,0:T(8,128)(2,1)S(1)}, bf16[1024,128]{1,0:T(8,128)(2,1)}, u32[]{:S(2)}) copy-start(bf16[1024,128]{1,0:T(8,128)(2,1)} %get-tuple-element.86) | copy-start | bytes 786436
  54.4 291.5 %reduce-scatter.2.cloned.1.call-start = ((), (), s32[]{:S(2)}) async-start(), calls=%async_computation.2 | async-start | bytes 8552448 | tf_op jit(solution)/shard_map/reduce_scatter | solution.py:528
  54.4 33.2 %collective-permute-start.13 = (bf16[1024,128]{1,0:T(8,128)(2,1)}, bf16[1024,128]{1,0:T(8,128)(2,1)S(1)}, u32[]{:S(2)}, u32[]{:S(2)}) collective-permute-start(bf16[1024,128]{1,0:T(8,128)(2,1)} %get-tuple-element.77), channel_id=1, source_target_pairs={{0,2},{1,3},{2,0},{3,1},{4,6},{5,7},{6,4},{7,5},{8,10},{9,11},{10,... | collective-permute-start | bytes 786440 | tf_op jit(solution)/shard_map/ppermute | solution.py:438
  63.2 25.0 %collective-permute-start.14 = (bf16[1024,128]{1,0:T(8,128)(2,1)}, bf16[1024,128]{1,0:T(8,128)(2,1)S(1)}, u32[]{:S(2)}, u32[]{:S(2)}) collective-permute-start(bf16[1024,128]{1,0:T(8,128)(2,1)} %get-tuple-element.76), channel_id=1, source_target_pairs={{0,3},{1,0},{2,1},{3,2},{4,7},{5,4},{6,5},{7,6},{8,11},{9,8},{10,9... | collective-permute-start | bytes 786440 | tf_op jit(solution)/shard_map/ppermute | solution.py:438
  66.2 20.5 %copy-start.9 = (bf16[1024,128]{1,0:T(8,128)(2,1)S(1)}, bf16[1024,128]{1,0:T(8,128)(2,1)}, u32[]{:S(2)}) copy-start(bf16[1024,128]{1,0:T(8,128)(2,1)} %get-tuple-element.87) | copy-start | bytes 786436
  68.1 66.6 %collective-permute-start.10 = (bf16[2048,128]{1,0:T(8,128)(2,1)}, bf16[2048,128]{1,0:T(8,128)(2,1)}, u32[]{:S(2)}, u32[]{:S(2)}) collective-permute-start(bf16[2048,128]{1,0:T(8,128)(2,1)} %pad_maximum_fusion.9), channel_id=1, source_target_pairs={{0,1},{1,2},{2,3},{3,0},{4,5},{5,6},{6,7},{7,4},{8,9},{9,10},{10,1... | collective-permute-start | bytes 1572872 | tf_op jit(solution)/shard_map/ppermute | solution.py:438
  69.9 68.1 %collective-permute-start.11 = (bf16[2048,128]{1,0:T(8,128)(2,1)}, bf16[2048,128]{1,0:T(8,128)(2,1)}, u32[]{:S(2)}, u32[]{:S(2)}) collective-permute-start(bf16[2048,128]{1,0:T(8,128)(2,1)} %pad_maximum_fusion.10), channel_id=1, source_target_pairs={{0,2},{1,3},{2,0},{3,1},{4,6},{5,7},{6,4},{7,5},{8,10},{9,11},{10,... | collective-permute-start | bytes 1572872 | tf_op jit(solution)/shard_map/ppermute | solution.py:438
  72.3 65.8 %collective-permute-start.12 = (bf16[2048,128]{1,0:T(8,128)(2,1)}, bf16[2048,128]{1,0:T(8,128)(2,1)S(1)}, u32[]{:S(2)}, u32[]{:S(2)}) collective-permute-start(bf16[2048,128]{1,0:T(8,128)(2,1)} %pad_maximum_fusion.11), channel_id=1, source_target_pairs={{0,3},{1,0},{2,1},{3,2},{4,7},{5,4},{6,5},{7,6},{8,11},{9,8},{10,9... | collective-permute-start | bytes 1572872 | tf_op jit(solution)/shard_map/ppermute | solution.py:438
  87.6 116.5 %collective-permute-start.7 = (bf16[2048,128]{1,0:T(8,128)(2,1)}, bf16[2048,128]{1,0:T(8,128)(2,1)}, u32[]{:S(2)}, u32[]{:S(2)}) collective-permute-start(bf16[2048,128]{1,0:T(8,128)(2,1)} %pad_maximum_fusion.6), channel_id=1, source_target_pairs={{0,1},{1,2},{2,3},{3,0},{4,5},{5,6},{6,7},{7,4},{8,9},{9,10},{10,1... | collective-permute-start | bytes 1572872 | tf_op jit(solution)/shard_map/ppermute | solution.py:438
  88.2 116.4 %collective-permute-start.8 = (bf16[2048,128]{1,0:T(8,128)(2,1)}, bf16[2048,128]{1,0:T(8,128)(2,1)}, u32[]{:S(2)}, u32[]{:S(2)}) collective-permute-start(bf16[2048,128]{1,0:T(8,128)(2,1)} %pad_maximum_fusion.7), channel_id=1, source_target_pairs={{0,2},{1,3},{2,0},{3,1},{4,6},{5,7},{6,4},{7,5},{8,10},{9,11},{10,... | collective-permute-start | bytes 1572872 | tf_op jit(solution)/shard_map/ppermute | solution.py:438
  104.0 30.7 %copy-start.14 = (bf16[2048,128]{1,0:T(8,128)(2,1)S(1)}, bf16[2048,128]{1,0:T(8,128)(2,1)}, u32[]{:S(2)}) copy-start(bf16[2048,128]{1,0:T(8,128)(2,1)} %pad_maximum_fusion.8) | copy-start | bytes 1572868
  104.0 34.1 %copy-start.13 = (bf16[2048,128]{1,0:T(8,128)(2,1)S(1)}, bf16[2048,128]{1,0:T(8,128)(2,1)}, u32[]{:S(2)}) copy-start(bf16[2048,128]{1,0:T(8,128)(2,1)} %pad_maximum_fusion.4) | copy-start | bytes 1572868
  104.0 34.9 %copy-start.11 = (bf16[2048,128]{1,0:T(8,128)(2,1)S(1)}, bf16[2048,128]{1,0:T(8,128)(2,1)}, u32[]{:S(2)}) copy-start(bf16[2048,128]{1,0:T(8,128)(2,1)} %pad_maximum_fusion.5) | copy-start | bytes 1572868
  134.7 73.4 %collective-permute-start.9 = (bf16[2048,128]{1,0:T(8,128)(2,1)S(1)}, bf16[2048,128]{1,0:T(8,128)(2,1)S(1)}, u32[]{:S(2)}, u32[]{:S(2)}) collective-permute-start(bf16[2048,128]{1,0:T(8,128)(2,1)S(1)} %copy-done.14), channel_id=1, source_target_pairs={{0,3},{1,0},{2,1},{3,2},{4,7},{5,4},{6,5},{7,6},{8,11},{9,8},{10,9... | collective-permute-start | bytes 1572872 | tf_op jit(solution)/shard_map/ppermute | solution.py:438
  138.1 100.9 %collective-permute-start.1 = (bf16[2048,128]{1,0:T(8,128)(2,1)S(1)}, bf16[2048,128]{1,0:T(8,128)(2,1)S(1)}, u32[]{:S(2)}, u32[]{:S(2)}) collective-permute-start(bf16[2048,128]{1,0:T(8,128)(2,1)S(1)} %copy-done.13), channel_id=1, source_target_pairs={{0,2},{1,3},{2,0},{3,1},{4,6},{5,7},{6,4},{7,5},{8,10},{9,11},{10,... | collective-permute-start | bytes 1572872 | tf_op jit(solution)/shard_map/ppermute | solution.py:438
  138.1 0.8 copy-start.5
  138.9 100.9 %collective-permute-start.2 = (bf16[2048,128]{1,0:T(8,128)(2,1)S(1)}, bf16[2048,128]{1,0:T(8,128)(2,1)S(1)}, u32[]{:S(2)}, u32[]{:S(2)}) collective-permute-start(bf16[2048,128]{1,0:T(8,128)(2,1)S(1)} %copy-done.11), channel_id=1, source_target_pairs={{0,3},{1,0},{2,1},{3,2},{4,7},{5,4},{6,5},{7,6},{8,11},{9,8},{10,9... | collective-permute-start | bytes 1572872 | tf_op jit(solution)/shard_map/ppermute | solution.py:438
  169.8 1.0 copy-start.6
  170.9 33.2 %copy-start.12 = (bf16[2048,128]{1,0:T(8,128)(2,1)S(1)}, bf16[2048,128]{1,0:T(8,128)(2,1)}, u32[]{:S(2)}) copy-start(bf16[2048,128]{1,0:T(8,128)(2,1)} %pad_maximum_fusion.3) | copy-start | bytes 1572868
  201.7 0.8 copy-start.2
  202.5 0.8 copy-start.3
  203.3 0.8 copy-start.4
  204.1 35.7 %collective-permute-start = (bf16[2048,128]{1,0:T(8,128)(2,1)S(1)}, bf16[2048,128]{1,0:T(8,128)(2,1)S(1)}, u32[]{:S(2)}, u32[]{:S(2)}) collective-permute-start(bf16[2048,128]{1,0:T(8,128)(2,1)S(1)} %copy-done.12), channel_id=1, source_target_pairs={{0,1},{1,2},{2,3},{3,0},{4,5},{5,6},{6,7},{7,4},{8,9},{9,10},{10,1... | collective-permute-start | bytes 1572872 | tf_op jit(solution)/shard_map/ppermute | solution.py:438
  204.6 65.8 %collective-permute-start.15 = (bf16[2,1,1024,128]{3,2,1,0:T(8,128)(2,1)S(1)}, bf16[2,1,1024,128]{3,2,1,0:T(8,128)(2,1)S(1)}, u32[]{:S(2)}, u32[]{:S(2)}) collective-permute-start(bf16[2,1,1024,128]{3,2,1,0:T(8,128)(2,1)S(1)} %get-tuple-element.53), channel_id=1, source_target_pairs={{0,3},{1,0},{2,1},{3,2},{4,7},{5,4},{6,5},{7,6},{8,11},{9,8},{10,9... | collective-permute-start | bytes 1572872 | tf_op jit(solution)/shard_map/ppermute | solution.py:438
  208.1 62.3 %collective-permute-start.16 = (bf16[2,1,1024,128]{3,2,1,0:T(8,128)(2,1)S(1)}, bf16[2,1,1024,128]{3,2,1,0:T(8,128)(2,1)S(1)}, u32[]{:S(2)}, u32[]{:S(2)}) collective-permute-start(bf16[2,1,1024,128]{3,2,1,0:T(8,128)(2,1)S(1)} %get-tuple-element.54), channel_id=1, source_target_pairs={{0,2},{1,3},{2,0},{3,1},{4,6},{5,7},{6,4},{7,5},{8,10},{9,11},{10,... | collective-permute-start | bytes 1572872 | tf_op jit(solution)/shard_map/ppermute | solution.py:438
  239.0 31.4 %collective-permute-start.17 = (bf16[2,1,1024,128]{3,2,1,0:T(8,128)(2,1)S(1)}, bf16[2,1,1024,128]{3,2,1,0:T(8,128)(2,1)S(1)}, u32[]{:S(2)}, u32[]{:S(2)}) collective-permute-start(bf16[2,1,1024,128]{3,2,1,0:T(8,128)(2,1)S(1)} %get-tuple-element.55), channel_id=1, source_target_pairs={{0,1},{1,2},{2,3},{3,0},{4,5},{5,6},{6,7},{7,4},{8,9},{9,10},{10,1... | collective-permute-start | bytes 1572872 | tf_op jit(solution)/shard_map/ppermute | solution.py:438
  270.4 0.8 copy-start.15
  270.4 0.9 copy-start.16
  271.3 0.8 copy-start.17
  272.2 164.5 %all-gather.5.cloned.1.call-start = ((), (), s32[]{:S(2)}) async-start(), calls=%async_computation.3 | async-start | bytes 2138112 | tf_op jit(solution)/shard_map/all_gather | solution.py:535
  272.2 18.7 %collective-permute-start.18 = (bf16[2,1,1024,128]{3,2,1,0:T(8,128)(2,1)}, bf16[2,1,1024,128]{3,2,1,0:T(8,128)(2,1)S(1)}, u32[]{:S(2)}, u32[]{:S(2)}) collective-permute-start(bf16[2,1,1024,128]{3,2,1,0:T(8,128)(2,1)} %copy-done.4), channel_id=1, source_target_pairs={{0,3},{1,0},{2,1},{3,2},{4,7},{5,4},{6,5},{7,6},{8,11},{9,8},{10,9... | collective-permute-start | bytes 1572872 | tf_op jit(solution)/shard_map/ppermute | solution.py:438
  275.6 70.3 %collective-permute-start.19 = (bf16[2,1,1024,128]{3,2,1,0:T(8,128)(2,1)}, bf16[2,1,1024,128]{3,2,1,0:T(8,128)(2,1)}, u32[]{:S(2)}, u32[]{:S(2)}) collective-permute-start(bf16[2,1,1024,128]{3,2,1,0:T(8,128)(2,1)} %copy-done.3), channel_id=1, source_target_pairs={{0,2},{1,3},{2,0},{3,1},{4,6},{5,7},{6,4},{7,5},{8,10},{9,11},{10,... | collective-permute-start | bytes 1572872 | tf_op jit(solution)/shard_map/ppermute | solution.py:438
  276.6 69.3 %collective-permute-start.20 = (bf16[2,1,1024,128]{3,2,1,0:T(8,128)(2,1)}, bf16[2,1,1024,128]{3,2,1,0:T(8,128)(2,1)}, u32[]{:S(2)}, u32[]{:S(2)}) collective-permute-start(bf16[2,1,1024,128]{3,2,1,0:T(8,128)(2,1)} %copy-done.2), channel_id=1, source_target_pairs={{0,1},{1,2},{2,3},{3,0},{4,5},{5,6},{6,7},{7,4},{8,9},{9,10},{10,1... | collective-permute-start | bytes 1572872 | tf_op jit(solution)/shard_map/ppermute | solution.py:438
  276.6 109.5 %collective-permute-start.21 = (bf16[2,1,1024,128]{3,2,1,0:T(8,128)(2,1)S(1)}, bf16[2,1,1024,128]{3,2,1,0:T(8,128)(2,1)}, u32[]{:S(2)}, u32[]{:S(2)}) collective-permute-start(bf16[2,1,1024,128]{3,2,1,0:T(8,128)(2,1)S(1)} %get-tuple-element.59), channel_id=1, source_target_pairs={{0,3},{1,0},{2,1},{3,2},{4,7},{5,4},{6,5},{7,6},{8,11},{9,8},{10,9... | collective-permute-start | bytes 1572872 | tf_op jit(solution)/shard_map/ppermute | solution.py:438
  280.4 108.7 %collective-permute-start.22 = (bf16[2,1,1024,128]{3,2,1,0:T(8,128)(2,1)S(1)}, bf16[2,1,1024,128]{3,2,1,0:T(8,128)(2,1)}, u32[]{:S(2)}, u32[]{:S(2)}) collective-permute-start(bf16[2,1,1024,128]{3,2,1,0:T(8,128)(2,1)S(1)} %get-tuple-element.60), channel_id=1, source_target_pairs={{0,2},{1,3},{2,0},{3,1},{4,6},{5,7},{6,4},{7,5},{8,10},{9,11},{10,... | collective-permute-start | bytes 1572872 | tf_op jit(solution)/shard_map/ppermute | solution.py:438
  291.0 21.7 %copy-start.18 = (bf16[2,1,1024,128]{3,2,1,0:T(8,128)(2,1)}, bf16[2,1,1024,128]{3,2,1,0:T(8,128)(2,1)S(1)}, u32[]{:S(2)}) copy-start(bf16[2,1,1024,128]{3,2,1,0:T(8,128)(2,1)S(1)} %collective-permute-done.18) | copy-start | bytes 1572868
  291.0 98.1 %collective-permute-start.23 = (bf16[2,1,1024,128]{3,2,1,0:T(8,128)(2,1)S(1)}, bf16[2,1,1024,128]{3,2,1,0:T(8,128)(2,1)}, u32[]{:S(2)}, u32[]{:S(2)}) collective-permute-start(bf16[2,1,1024,128]{3,2,1,0:T(8,128)(2,1)S(1)} %get-tuple-element.61), channel_id=1, source_target_pairs={{0,1},{1,2},{2,3},{3,0},{4,5},{5,6},{6,7},{7,4},{8,9},{9,10},{10,1... | collective-permute-start | bytes 1572872 | tf_op jit(solution)/shard_map/ppermute | solution.py:438
  347.1 8.0 %collective-permute-start.30 = (f32[464,128]{1,0:T(8,128)S(1)}, f32[464,128]{1,0:T(8,128)S(1)}, u32[]{:S(2)}, u32[]{:S(2)}) collective-permute-start(f32[464,128]{1,0:T(8,128)S(1)} %get-tuple-element.106), channel_id=1, source_target_pairs={{0,1},{1,2},{2,3},{3,0},{4,5},{5,6},{6,7},{7,4},{8,9},{9,10},{10,1... | collective-permute-start | bytes 712712 | tf_op jit(solution)/shard_map/ppermute | solution.py:438
  347.2 33.9 %collective-permute-start.31 = (f32[464,128]{1,0:T(8,128)S(1)}, f32[464,128]{1,0:T(8,128)S(1)}, u32[]{:S(2)}, u32[]{:S(2)}) collective-permute-start(f32[464,128]{1,0:T(8,128)S(1)} %get-tuple-element.108), channel_id=1, source_target_pairs={{0,2},{1,3},{2,0},{3,1},{4,6},{5,7},{6,4},{7,5},{8,10},{9,11},{10,... | collective-permute-start | bytes 712712 | tf_op jit(solution)/shard_map/ppermute | solution.py:438
  355.1 29.2 %collective-permute-start.32 = (f32[464,128]{1,0:T(8,128)S(1)}, f32[464,128]{1,0:T(8,128)S(1)}, u32[]{:S(2)}, u32[]{:S(2)}) collective-permute-start(f32[464,128]{1,0:T(8,128)S(1)} %get-tuple-element.107), channel_id=1, source_target_pairs={{0,3},{1,0},{2,1},{3,2},{4,7},{5,4},{6,5},{7,6},{8,11},{9,8},{10,9... | collective-permute-start | bytes 712712 | tf_op jit(solution)/shard_map/ppermute | solution.py:438
  381.2 9.4 %collective-permute-start.27 = (f32[4,4,128]{2,1,0:T(4,128)S(1)}, f32[4,4,128]{2,1,0:T(4,128)S(1)}, u32[]{:S(2)}, u32[]{:S(2)}) collective-permute-start(f32[4,4,128]{2,1,0:T(4,128)S(1)} %get-tuple-element.136), channel_id=1, source_target_pairs={{0,1},{1,2},{2,3},{3,0},{4,5},{5,6},{6,7},{7,4},{8,9},{9,10},{10,1... | collective-permute-start | bytes 24584 | tf_op jit(solution)/shard_map/ppermute | solution.py:438
  384.4 6.9 %collective-permute-start.28 = (f32[4,4,128]{2,1,0:T(4,128)S(1)}, f32[4,4,128]{2,1,0:T(4,128)S(1)}, u32[]{:S(2)}, u32[]{:S(2)}) collective-permute-start(f32[4,4,128]{2,1,0:T(4,128)S(1)} %get-tuple-element.136), channel_id=1, source_target_pairs={{0,2},{1,3},{2,0},{3,1},{4,6},{5,7},{6,4},{7,5},{8,10},{9,11},{10,... | collective-permute-start | bytes 24584 | tf_op jit(solution)/shard_map/ppermute | solution.py:438
  386.1 5.2 %collective-permute-start.29 = (f32[4,4,128]{2,1,0:T(4,128)S(1)}, f32[4,4,128]{2,1,0:T(4,128)S(1)}, u32[]{:S(2)}, u32[]{:S(2)}) collective-permute-start(f32[4,4,128]{2,1,0:T(4,128)S(1)} %get-tuple-element.136), channel_id=1, source_target_pairs={{0,3},{1,0},{2,1},{3,2},{4,7},{5,4},{6,5},{7,6},{8,11},{9,8},{10,9... | collective-permute-start | bytes 24584 | tf_op jit(solution)/shard_map/ppermute | solution.py:438
  389.1 18.9 %collective-permute-start.24 = (bf16[2,1,1024,128]{3,2,1,0:T(8,128)(2,1)S(1)}, bf16[2,1,1024,128]{3,2,1,0:T(8,128)(2,1)S(1)}, u32[]{:S(2)}, u32[]{:S(2)}) collective-permute-start(bf16[2,1,1024,128]{3,2,1,0:T(8,128)(2,1)S(1)} %get-tuple-element.62), channel_id=1, source_target_pairs={{0,3},{1,0},{2,1},{3,2},{4,7},{5,4},{6,5},{7,6},{8,11},{9,8},{10,9... | collective-permute-start | bytes 1572872 | tf_op jit(solution)/shard_map/ppermute | solution.py:438
  390.6 44.5 %collective-permute-start.25 = (bf16[2,1,1024,128]{3,2,1,0:T(8,128)(2,1)S(1)}, bf16[2,1,1024,128]{3,2,1,0:T(8,128)(2,1)S(1)}, u32[]{:S(2)}, u32[]{:S(2)}) collective-permute-start(bf16[2,1,1024,128]{3,2,1,0:T(8,128)(2,1)S(1)} %get-tuple-element.63), channel_id=1, source_target_pairs={{0,2},{1,3},{2,0},{3,1},{4,6},{5,7},{6,4},{7,5},{8,10},{9,11},{10,... | collective-permute-start | bytes 1572872 | tf_op jit(solution)/shard_map/ppermute | solution.py:438
  390.6 45.3 %collective-permute-start.26 = (bf16[2,1,1024,128]{3,2,1,0:T(8,128)(2,1)S(1)}, bf16[2,1,1024,128]{3,2,1,0:T(8,128)(2,1)S(1)}, u32[]{:S(2)}, u32[]{:S(2)}) collective-permute-start(bf16[2,1,1024,128]{3,2,1,0:T(8,128)(2,1)S(1)} %get-tuple-element.64), channel_id=1, source_target_pairs={{0,1},{1,2},{2,3},{3,0},{4,5},{5,6},{6,7},{7,4},{8,9},{9,10},{10,1... | collective-permute-start | bytes 1572872 | tf_op jit(solution)/shard_map/ppermute | solution.py:438
  391.3 14.9 %copy-start.19 = (f32[16,4,128]{2,1,0:T(4,128)}, f32[16,4,128]{2,1,0:T(4,128)S(1)}, u32[]{:S(2)}) copy-start(f32[16,4,128]{2,1,0:T(4,128)S(1)} %constant_dynamic-update-slice_fusion.20) | copy-start | bytes 98308
  404.3 39.2 %copy-start.1 = (bf16[16,4,128]{2,1,0:T(4,128)(2,1)S(1)}, bf16[16,4,128]{2,1,0:T(4,128)(2,1)}, u32[]{:S(2)}) copy-start(bf16[16,4,128]{2,1,0:T(4,128)(2,1)} %param.13) | copy-start | bytes 49156
Sparse Core Ops, SparseCore 0:
  54.5 42.0 all-gather.2
  272.3 69.1 reduce-scatter.1
  389.2 26.1 all-gather.4

commit v2 on v1

--- a/solution.py
+++ b/solution.py
@@ -12,26 +12,29 @@
 var_floor = 0.1
 inv_root = math.sqrt(0.5)
 highest = lax.Precision.HIGHEST
+COST = 0.5
 BLOCK = 16
 NT = (((1,), (1,)), ((), ()))
 TN = (((0,), (0,)), ((), ()))
 
 
-def row_kernel(
-    n, segs, style_n, per, start, at_f, at_c, n_prev, z_ref, len_ref, seg_ref, *refs
+def rows_kernel(
+    n, segs, style_n, per, first, from_f, from_c, to, has_prev, final, z_ref, len_ref, seg_ref, *refs
 ):
-    f_own, c_own = refs[:2]
-    recv_f, recv_c = refs[2 : n + 1], refs[n + 1 : 2 * n]
-    style_ref, inv_ref, w_hbm = refs[2 * n : 2 * n + 3]
-    prev = refs[2 * n + 3 : 2 * n + 3 + n_prev]
-    refs = refs[2 * n + 3 + n_prev :]
-    o_own, g_own, sum_hbm = refs[:3]
-    outs = refs[3 : n + 2]
-    dstyle_ref = refs[n + 2]
-    fr, ct, res, sh, a3x, a3y, g3, conv, da, acc, coef, w_ref, wt_ref, sum_ref, sems = refs[n + 3 :]
-
+    f_own, c_own, style_ref, inv_ref, w_hbm = refs[:5]
+    refs = refs[5:]
+    n_recv = 1 + max(i for i, _ in from_f + from_c)
+    recv, refs = refs[: n_recv * (n - 1)], refs[n_recv * (n - 1) :]
+    prev, refs = refs[:has_prev], refs[has_prev:]
+    sum_hbm, dstyle_ref, o_own, g_own = refs[:4]
+    outs = refs[4:-16]
+    fr, ct, res, sh, a3x, a3y, g3, conv, da, acc, coef, w_ref, wt_ref, sum_ref = refs[-16:-2]
+    round_ref, sems = refs[-2:]
+
+    row = pl.program_id(0)
+    last_row = len(from_f) - 1
     z = z_ref[0]
-    length = len_ref[0]
+    length = len_ref[row]
     frames, chans = fr.shape
     width = chans // n
     blocks = frames // BLOCK
@@ -51,7 +54,7 @@
         return pl.ds(pl.multiple_of(b * BLOCK, BLOCK), BLOCK)
 
     def segment(b):
-        return seg_ref[0, b + 1]
+        return seg_ref[row, b + 1]
 
     def load(ref, b):
         return ref[span(b), :].astype(jnp.float32).reshape(2, 8, chans)
@@ -93,9 +96,11 @@
         for c in copies:
             c.wait()
 
-    def pieces(own, start, received, dst):
-        yield copy(own.at[z * per + start], dst.at[:, lanes(0)])
-        for k, (ref, at) in enumerate(received, 1):
+    def pieces(own, place, at_row, dst):
+        which, at = place
+        yield copy(own.at[z * per + first + at_row], dst.at[:, lanes(0)])
+        for k in range(1, n):
+            ref = recv[which * (n - 1) + k - 1]
             yield copy(ref.at[pl.ds(at, frames), :], dst.at[:, lanes(k)])
 
     def weight_copies(layer):
@@ -107,23 +112,59 @@
 
     tail_rows = pl.ds(fc_at, w_ref.shape[0] - fc_at)
     layer_rows = [pl.ds(layer * wide, wide) for layer in range(2)]
-    get_fr = list(pieces(f_own, start, zip(recv_f, at_f), fr))
-    get_ct = list(pieces(c_own, start, zip(recv_c, at_c), ct))
     get_tail = copy(w_hbm.at[tail_rows, :], w_ref.at[tail_rows, :])
     get_w = [list(weight_copies(layer)) for layer in range(2)]
-    begin(*get_fr, get_tail, *get_w[0], *get_w[1], *get_ct)
     get_sums = []
-    if n_prev:
-        get_sums = [copy(prev[2].at[r, :], sum_ref.at[r, :]) for r in (*layer_rows, tail_rows)]
-        begin(*get_sums[::-1])
-    else:
-        sum_ref[...] = jnp.zeros_like(sum_ref)
-    put_sums = [copy(sum_ref.at[r, :], sum_hbm.at[r, :]) for r in (*layer_rows, tail_rows)]
-
-    def put_result(which):
-        yield copy(res.at[:, lanes(0)], (o_own, g_own)[which].at[z * per + start])
+    if has_prev:
+        get_sums = [copy(prev[0].at[r, :], sum_ref.at[r, :]) for r in (*layer_rows, tail_rows)]
+    sum_out = round_ref if final else sum_ref
+    put_sums = [copy(sum_out.at[r, :], sum_hbm.at[r, :]) for r in (*layer_rows, tail_rows)]
+
+    def send_sums(part):
+        rows = (*layer_rows, tail_rows)[part]
+        if final:
+
+            def body(i, carry):
+                at = pl.ds(pl.multiple_of(rows.start + i * 128, 16), 128)
+                round_ref[at, :] = sum_ref[at, :].astype(round_ref.dtype)
+                return carry
+
+            lax.fori_loop(0, rows.size // 128, body, 0)
+        begin(put_sums[part])
+
+    mark = next(count)
+    get = []
+    for i in range(last_row + 1):
+        count = itertools.count(mark)
+        get_fr = list(pieces(f_own, from_f[i], i, fr))
+        get_ct = list(pieces(c_own, from_c[i], i, ct))
+        pl.when(row == i)(functools.partial(begin, *get_fr, *get_ct))
+
+    @pl.when(row == 0)
+    def _():
+        begin(get_tail, *get_w[0], *get_w[1], *get_sums[::-1])
+        if not has_prev:
+            sum_ref[...] = jnp.zeros_like(sum_ref)
+
+    mark_out = next(count)
+
+    def put_result(which, at_row):
+        yield copy(res.at[:, lanes(0)], (o_own, g_own)[which].at[z * per + first + at_row])
+        array, at = to[at_row]
         for k in range(1, n):
-            yield copy(res.at[:, lanes(k)], outs[k - 1].at[which, 0])
+            dst = outs[array * (n - 1) + k - 1].at[2 * at + which]
+            yield copy(res.at[:, lanes(k)], dst)
+
+    def start_result(which):
+        nonlocal count
+        for i in range(last_row + 1):
+            count = itertools.count(mark_out + n * which)
+            copies = list(put_result(which, i))
+            pl.when(row == i)(functools.partial(begin, *copies))
+        return copies
+
+    def on_row(i, *copies, act):
+        pl.when(row == i)(functools.partial(act, *copies))
 
     for j in range(chans // 128):
         sh[j, 0:8, :] = jnp.zeros((8, 128), jnp.float32)
@@ -131,7 +172,8 @@
 
     inv_count = inv_ref[0]
     style = style_ref[0].astype(jnp.float32)
-    finish_copies(*get_fr, get_tail)
+    finish_copies(*get_fr)
+    on_row(0, get_tail, act=finish_copies)
     biases = w_ref[bias_at : bias_at + BLOCK, :].astype(jnp.float32)
 
     def project(layer, k):
@@ -188,8 +230,8 @@
 
         def body(b):
             s = segment(b)
-            from_row = jnp.where(seg_ref[0, b] == s, 0, 1)
-            to_row = jnp.where(seg_ref[0, b + 2] == s, 8, 7)
+            from_row = jnp.where(seg_ref[row, b] == s, 0, 1)
+            to_row = jnp.where(seg_ref[row, b + 2] == s, 8, 7)
             for j in range(chans // 128):
 
                 def part(off):
@@ -281,12 +323,13 @@
     statistics(fr, 0)
     activation(fr, 0)
     spread(a3x, 0)
-    finish_copies(*get_w[0])
+    on_row(0, *get_w[0], act=finish_copies)
     convolve(conv, a3x, 0)
     statistics(conv, 1)
     activation(conv, 1)
     spread(a3y, 0)
-    finish_copies(*get_w[1], *get_ct)
+    on_row(0, *get_w[1], act=finish_copies)
+    finish_copies(*get_ct)
     convolve(da, a3y, 1)
     bias = biases[4:5]
     acc[0, 0] = jnp.zeros_like(acc[0, 0])
@@ -300,14 +343,13 @@
 
     loop(finish)
     bias_sum = jnp.sum(acc[0, 0], axis=0, keepdims=True)
-    put_output = list(put_result(0))
-    begin(*put_output)
+    put_output = start_result(0)
 
     dstyle_ref[...] = jnp.zeros_like(dstyle_ref)
     spread(g3, 2)
-    finish_copies(*get_sums)
+    on_row(0, *get_sums, act=finish_copies)
     weight_grad(1, a3y, g3)
-    begin(put_sums[1])
+    on_row(last_row, 1, act=send_sums)
     input_grad(da, g3, 1)
     rows_two = backward(conv, 1)
 
@@ -317,14 +359,14 @@
     loop(round_grad)
     spread(g3, 2)
     weight_grad(0, a3x, g3)
-    begin(put_sums[0])
+    on_row(last_row, 0, act=send_sums)
     input_grad(da, g3, 0)
     rows_one = backward(fr, 0)
 
     sum_ref[bias_at : bias_at + 8, :] += jnp.concatenate(
         rows_one + rows_two + [bias_sum, jnp.zeros((3, chans), jnp.float32)], axis=0
     )
-    begin(put_sums[2])
+    on_row(last_row, 2, act=send_sums)
     finish_copies(*put_output)
 
     def frames_grad(b):
@@ -332,38 +374,41 @@
         res[span(b), :] = flat(load(ct, b) * inv_root + dv).astype(res.dtype)
 
     loop(frames_grad)
-    put_grads = list(put_result(1))
-    begin(*put_grads)
-    finish_copies(*put_grads, *put_sums)
+    finish_copies(*start_result(1))
+    on_row(last_row, *put_sums, act=finish_copies)
 
 
 def block_rows(
-    n, per, start, z, lengths, seg_blocks, frames, cotangent, recv_f, recv_c, style, inv, weights, prev
+    n, per, first, z, lengths, seg_blocks, frames, cotangent, style, inv, weights,
+    recv, from_f, from_c, to, prev, final,
 ):
     frames_n, width = frames.shape[1:]
     chans = width * n
     segs, style_n = style.shape[1:]
     flat_n = weights.shape[0]
+    rows = len(to)
     f32 = jnp.float32
 
     def here(r, *_):
-        return (start + r, 0, 0)
-
+        return (first + r, 0, 0)
+
+    received = [v for group in recv for v in group]
     any_space = pl.BlockSpec(memory_space=pl.ANY)
-    sums = jax.ShapeDtypeStruct((flat_n, chans), f32)
-    piece = jax.ShapeDtypeStruct((2, 1, frames_n, width), jnp.bfloat16)
     in_specs = (
-        [any_space] * 2 * n
+        [any_space] * 2
         + [pl.BlockSpec((1, segs, style_n), here), pl.BlockSpec((1, segs, chans), here)]
-        + [any_space] * (1 + len(prev))
-    )
-    out_specs = [any_space] * (n + 2) + [pl.BlockSpec((1, segs, style_n), lambda *_: (0, 0, 0))]
-    out_shape = (
-        [jax.ShapeDtypeStruct(frames.shape, jnp.bfloat16)] * 2
-        + [sums]
-        + [piece] * (n - 1)
-        + [jax.ShapeDtypeStruct((1, segs, style_n), f32)]
-    )
+        + [any_space] * (1 + len(received) + len(prev))
+    )
+    out_shape = [
+        jax.ShapeDtypeStruct((flat_n, chans), jnp.bfloat16 if final else f32),
+        jax.ShapeDtypeStruct((rows, segs, style_n), f32),
+    ]
+    out_shape += [jax.ShapeDtypeStruct(frames.shape, jnp.bfloat16)] * 2
+    for i in range(1 + max(i for i, _ in to)):
+        size = 2 * sum(j == i for j, _ in to)
+        out_shape += [jax.ShapeDtypeStruct((size, frames_n, width), jnp.bfloat16)] * (n - 1)
+    out_specs = [any_space] * len(out_shape)
+    out_specs[1] = pl.BlockSpec((1, segs, style_n), lambda r, *_: (r, 0, 0))
     scratch = [
         pltpu.VMEM((frames_n, chans), jnp.bfloat16),
         pltpu.VMEM((frames_n, chans), jnp.bfloat16),
@@ -379,33 +424,91 @@
         pltpu.VMEM((flat_n, chans), jnp.bfloat16),
         pltpu.VMEM((2, chans, 3 * chans), jnp.bfloat16),
         pltpu.VMEM((flat_n, chans), f32),
+        pltpu.VMEM((flat_n if final else 16, chans), jnp.bfloat16),
         pltpu.SemaphoreType.DMA((4 * n + 16,)),
     ]
-    first_prev = 3 + 2 * n + 3
+    first_prev = 3 + 5 + len(received)
     return pl.pallas_call(
         functools.partial(
-            row_kernel, n, segs, style_n, per, start,
-            [at for _, at in recv_f], [at for _, at in recv_c], len(prev),
+            rows_kernel, n, segs, style_n, per, first, from_f, from_c, to, len(prev), final,
         ),
         grid_spec=pltpu.PrefetchScalarGridSpec(
             num_scalar_prefetch=3,
-            grid=(1,),
+            grid=(rows,),
             in_specs=in_specs,
             out_specs=out_specs,
             scratch_shapes=scratch,
         ),
         out_shape=out_shape,
-        input_output_aliases={first_prev + i: i for i in range(len(prev))},
+        input_output_aliases={first_prev + i: 1 + i for i in range(1, len(prev))},
         compiler_params=pltpu.CompilerParams(vmem_limit_bytes=48 << 20),
         cost_estimate=pl.CostEstimate(
-            flops=6 * 2 * 3 * frames_n * chans * chans,
-            bytes_accessed=8 * frames_n * chans + 10 * flat_n * chans,
-            transcendentals=4 * frames_n * chans,
+            flops=int(COST * rows * 6 * 2 * 3 * frames_n * chans * chans), bytes_accessed=1000000,
+            transcendentals=0,
         ),
     )(
-        z, lengths, seg_blocks, frames, cotangent,
-        *[v for v, _ in recv_f], *[v for v, _ in recv_c], style, inv, weights, *prev,
-    )
+        z, lengths, seg_blocks, frames, cotangent, style, inv, weights,
+        *received, *prev,
+    )
+
+
+def pack_kernel(n, per, part, z_ref, i_ref, frames, conv1, conv2, fc1, fc2, biases, *refs):
+    outs, mine = refs[: n - 1], refs[n - 1]
+    stage, rows, sems = refs[n:]
+    count = itertools.count()
+
+    def copy(src, dst):
+        c = pltpu.make_async_copy(src, dst, sems.at[next(count)])
+        c.start()
+        return c
+
+    frames_n = frames.shape[1]
+    at, staged = 0, []
+    for ref in (conv1, conv2, fc1, fc2, biases):
+        staged.append(copy(ref, stage.at[pl.ds(at, ref.shape[0]), :]))
+        at += ref.shape[0]
+    read = []
+    for k in range(1, n):
+        read.append(copy(frames.at[lax.rem(z_ref[0] + k, n) * per], rows.at[k - 1]))
+    sent = []
+    if at < stage.shape[0]:
+        stage[at:, :] = jnp.zeros((stage.shape[0] - at, stage.shape[1]), stage.dtype)
+    for c in staged:
+        c.wait()
+    src = stage.at[pl.ds(pl.multiple_of(i_ref[0] * part, 16), part), :]
+    sent.append(copy(src, mine))
+    for k in range(1, n):
+        sent.append(copy(src, outs[k - 1].at[pl.ds(frames_n, part), :]))
+        read[k - 1].wait()
+        sent.append(copy(rows.at[k - 1], outs[k - 1].at[pl.ds(0, frames_n), :]))
+    for c in sent:
+        c.wait()
+
+
+def pack(n, n_rows, per, z, i, frames, weights):
+    frames_n, width = frames.shape[1:]
+    rows = sum(v.shape[0] for v in weights)
+    padded = -(-rows // (16 * n_rows)) * 16 * n_rows
+    part = padded // n_rows
+    any_space = pl.BlockSpec(memory_space=pl.ANY)
+    return pl.pallas_call(
+        functools.partial(pack_kernel, n, per, part),
+        grid_spec=pltpu.PrefetchScalarGridSpec(
+            num_scalar_prefetch=2,
+            grid=(1,),
+            in_specs=[any_space] * (1 + len(weights)),
+            out_specs=[any_space] * n,
+            scratch_shapes=[
+                pltpu.VMEM((padded, width), jnp.bfloat16),
+                pltpu.VMEM((n - 1, frames_n, width), jnp.bfloat16),
+                pltpu.SemaphoreType.DMA((3 * n + len(weights),)),
+            ],
+        ),
+        out_shape=[jax.ShapeDtypeStruct((frames_n + part, width), jnp.bfloat16)] * (n - 1)
+        + [jax.ShapeDtypeStruct((part, width), jnp.bfloat16)],
+        compiler_params=pltpu.CompilerParams(vmem_limit_bytes=56 << 20),
+        cost_estimate=pl.CostEstimate(flops=0, bytes_accessed=6 * padded * width, transcendentals=0),
+    )(z, i, frames, *weights)
 
 
 def per_device(
@@ -434,8 +537,9 @@
     def shift(k):
         return [(i, (i + k) % n) for i in range(n)]
 
-    def send(v, k):
-        return lax.ppermute(v, "ch", shift(k))
+    def send(v, k, what):
+        with jax.named_scope(what):
+            return lax.ppermute(v, "ch", shift(k))
 
     def over_ch(v, pieces, axis):
         whole = jnp.concatenate([v] * n, axis=axis)
@@ -450,43 +554,42 @@
 
     sizes = [3 * chans, 3 * chans, 2 * style_n, 2 * style_n, 2, 2, 1]
     used = sum(sizes)
-    padded = -(-used // (16 * n_rows)) * 16 * n_rows
-    shard = jnp.concatenate(
-        [
-            conv1_weight.reshape(-1, width),
-            conv2_weight.reshape(-1, width),
-            fc1_weight.reshape(-1, width),
-            fc2_weight.reshape(-1, width),
-            fc1_bias,
-            fc2_bias,
-            conv2_bias[None],
-            jnp.zeros((padded - used, width), conv1_weight.dtype),
-        ]
-    )
-    part = padded // n_rows
-    mine = lax.dynamic_slice_in_dim(shard, lax.axis_index("rows") * part, part, 0)
+    biases = jnp.concatenate(
+        [fc1_bias, fc2_bias, conv2_bias[None], jnp.zeros((11, width), fc1_bias.dtype)]
+    )
+    shard = [v.reshape(-1, width) for v in (conv1_weight, conv2_weight, fc1_weight, fc2_weight)]
+    *bundles, mine = pack(
+        n, n_rows, per, z[None], lax.axis_index("rows")[None], frames, shard + [biases]
+    )
 
     def piece(v, k, r):
         at = lax.rem(z + k, n) * per + r
         return lax.dynamic_slice_in_dim(v, at, 1, 0)[0]
 
-    recv_f, recv_c, weight_pieces = [], [], []
-    for r in range(per):
-        got_f, got_c = [], []
-        for k in range(1, n):
-            f, c = piece(frames, k, r), piece(cotangent, k, r)
-            if r == 0:
-                both = send(jnp.concatenate([f, mine]), k)
-                got_f.append((both, 0))
-                weight_pieces.append(both[frames_n:])
-                got_c.append((send(c, k), 0))
-            else:
-                both = send(jnp.concatenate([f, c]), k)
-                got_f.append((both, 0))
-                got_c.append((both, frames_n))
-        recv_f.append(got_f)
-        recv_c.append(got_c)
-    mine = after(over_ch(mine, weight_pieces, 1), [recv_c[0][0][0]])
+    def swap(v, what):
+        with jax.named_scope(what):
+            return lax.all_to_all(v, "ch", 0, 0)
+
+    def of_row(v, r):
+        return v.reshape(n, per, frames_n, width)[:, r]
+
+    def bundle(*names):
+        return [
+            jnp.concatenate([piece({"f": frames, "c": cotangent}[v], k, r) for v, r in names])
+            for k in range(1, n)
+        ]
+
+    def fetch(what, pieces):
+        return [send(v, k, what) for k, v in enumerate(pieces, 1)]
+
+    half = per // 2
+    early = [(v, r) for r in range(half) for v in "fc"]
+    late = [(v, r) for r in range(half, per) for v in "fc"]
+    got_a = fetch("frames_0", bundles)
+    got_b = fetch("inputs_1", bundle(*early[1:]))
+    got_c = fetch("inputs_2", after(bundle(*late), got_b))
+    mine = over_ch(mine, [v[frames_n:] for v in got_a], 1)
+    mine = after(mine, [got_b[0], got_b[2]])
     weights = lax.all_gather(mine, "rows", axis=0, tiled=True)
 
     first = z * per
@@ -504,43 +607,58 @@
         (1.0 / jnp.maximum(counts, 1.0))[:, :, None], (per, segs, chans)
     )
 
-    prev, back, dstyles = [], [], []
-    for r in range(per):
-        results = block_rows(
-            n, per, r, z[None], lengths[r : r + 1], seg_blocks[r : r + 1], frames, cotangent,
-            recv_f[r], recv_c[r], my_style, inv_count, weights, prev,
+    def run(first, count, recv, from_f, from_c, to, prev):
+        ids, sizes = seg_blocks[first : first + count], lengths[first : first + count]
+        return block_rows(
+            n, per, first, z[None], sizes, ids, frames, cotangent, my_style, inv_count, weights,
+            recv, from_f, from_c, to, prev, bool(prev),
         )
-        prev = list(results[:3])
-        dstyles.append(results[n + 2])
-        back.append([send(v, n - k) for k, v in enumerate(results[3 : n + 2], 1)])
-
-    output, grad_frames, sums = prev
-    for r in range(per):
-        for k in range(1, n):
-            at = lax.rem(z + k, n) * per + r
-            output = lax.dynamic_update_slice_in_dim(output, back[r][k - 1][0], at, 0)
-            grad_frames = lax.dynamic_update_slice_in_dim(grad_frames, back[r][k - 1][1], at, 0)
-
-    style_grad = jnp.concatenate(dstyles, axis=0)
-    grad_style = over_ch(style_grad, [send(style_grad, k) for k in range(1, n)], 0)
-
-    sums = after(sums, back[0])
+
+    def spots(group, skip, which, rows):
+        return [(group, (2 * r + which - skip) * frames_n) for r in rows]
+
+    sums, dstyle_a, *rest = run(
+        0, half, [got_a, got_b], [(0, 0)] + spots(1, 1, 0, range(1, half)),
+        spots(1, 1, 1, range(half)), [(0, r) for r in range(half)], [],
+    )
+    own, pieces = rest[:2], after(rest[2:], got_c)
+    back = [[send(v, n - k, "results_0") for k, v in enumerate(pieces, 1)]]
+    others = range(per - half)
+    sums, dstyle_b, *rest = run(
+        half, per - half, [got_c], spots(0, 0, 0, others), spots(0, 0, 1, others),
+        [(r, 0) for r in others], [sums, *own],
+    )
+    own, pieces = rest[:2], rest[2:]
+    for r in others:
+        group = pieces[r * (n - 1) : (r + 1) * (n - 1)]
+        if r == 0:
+            group = after(group, back[0][2])
+        back.append([send(v, n - k, f"results_{half + r}") for k, v in enumerate(group, 1)])
+    dstyles = [dstyle_a, dstyle_b]
+
+    sums = after(sums, back[0][:2])
     sums = lax.psum_scatter(sums, "rows", scatter_dimension=0, tiled=True)
-    sums = after(sums, back[1])
-    total = lax.dynamic_slice_in_dim(sums, z * width, width, 1)
-    for k in range(1, n):
+    sums = after(sums, [back[1][0], back[1][2]])
+    style_grad = jnp.concatenate(dstyles, axis=0).reshape(per * segs, style_n).astype(sums.dtype)
+
+    def share(k):
         at = lax.rem(z + k, n) * width
-        total = total + send(lax.dynamic_slice_in_dim(sums, at, width, 1), k)
-    total = after(total, back[2])
+        return lax.dynamic_slice_in_dim(sums, at, width, 1)
+
+    got = [send(jnp.concatenate([share(k), style_grad]), k, "sums") for k in range(1, n)]
+    part = sums.shape[0]
+    total = share(0).astype(f32)
+    for v in got:
+        total = total + v[:part].astype(f32)
+    grad_style = over_ch(style_grad, [v[part:] for v in got], 0)
+    grad_style = grad_style.astype(f32).reshape(style_vector.shape)
+    total = after(total, [back[1][1], back[2][0]])
     grads = lax.all_gather(total, "rows", axis=0, tiled=True)
     splits = [sum(sizes[: i + 1]) for i in range(len(sizes))]
     g1, g2, gf1, gf2, gb1, gb2, gb = [
         grads[end - size : end] for size, end in zip(sizes, splits)
     ]
-    return (
-        output,
-        grad_frames,
-        grad_style,
+    grads = [
         gf1.reshape(fc1_weight.shape),
         gb1,
         g1.reshape(conv1_weight.shape),
@@ -548,7 +666,20 @@
         gb2,
         g2.reshape(conv2_weight.shape),
         gb[0],
-    )
+    ]
+
+    results = [v.reshape(n, per, frames_n, width) for v in own]
+    for r in range(per):
+        if r == per - 1:
+            grads, results = lax.optimization_barrier((grads, results))
+        group, at = (0, r) if r < half else (r - half + 1, 0)
+        for which in range(2):
+            for k, v in enumerate(back[group], 1):
+                results[which] = lax.dynamic_update_slice(
+                    results[which], v[None, None, 2 * at + which], (lax.rem(z + k, n), r, 0, 0)
+                )
+    output, grad_frames = [v.reshape(frames.shape) for v in results]
+    return (output, grad_frames, grad_style, *grads)
 
 
 def solution(mesh):

time: 459 us -> 429 us (0.935); the launches traced: 450 us -> 428 us
  starting transfers between devices: 115 us -> 57.7 us
  waiting for transfers between devices: 133 us -> 176 us
  local copies, waits for them, and re-layouts: 45.6 us -> 39.7 us
    ppermute x33 -> x21, starting transfers between devices: 115 us -> 57.6 us  [send(): return lax.ppermute(v, 'ch', shift(k))]
    ppermute x33 -> x21, waiting for transfers between devices: 133 us -> 165 us  [send(): return lax.ppermute(v, 'ch', shift(k))]
    all_gather x1, waiting for transfers between devices: 0.01 us -> 11.5 us  [per_device(): grads = lax.all_gather(total, 'rows', axis=0, tiled=True)]
    concatenate x3 -> x1, local copies, waits for them, and re-layouts: 6.45 us -> 0.08 us  [per_device(): jnp.concatenate([fc1_bias, fc2_bias, conv2_bias[None], jnp.zeros((11, wid...]
    concatenate x10 -> x8, other arithmetic: 16.6 us -> 11.5 us  [the longest x5 9.36 us: bundle(): jnp.concatenate([piece({'f': frames, 'c': cotangent}[v], k, r) for v, r i...]
    pallas_call x4 -> x3, Pallas kernels: 123 us -> 124 us  [the longest x2 121 us: block_rows(): pl.pallas_call(functools.partial(rows_kernel, n, segs, style_n, per, firs...]
  transfers between devices with their start and end apart: 36 -> 24, of which waited for: 9 -> 12; matrix products, arithmetic and copies ran while one was open for 9% -> 10% of each run, Pallas kernels for 27% -> 28%
where the time goes in v2:
time: 429 us; the launch traced here: 428 us
  waiting for transfers between devices  176 us (41%)
  Pallas kernels  124 us (29%)
  starting transfers between devices  57.7 us (13%)
  local copies, waits for them, and re-layouts  39.7 us (9%)
  other arithmetic  16.7 us (4%)
  between operations  14 us (3%)
    ppermute x21, waiting for transfers between devices, send(): return lax.ppermute(v, 'ch', shift(k))  165 us
    pallas_call x2, Pallas kernels, block_rows(): pl.pallas_call(functools.partial(rows_kernel, n, segs, style_n, per, firs...  121 us
    ppermute x21, starting transfers between devices, send(): return lax.ppermute(v, 'ch', shift(k))  57.6 us
    dynamic_update_slice x12, local copies, waits for them, and re-layouts, per_device(): lax.dynamic_update_slice(results[which], v[None, None, 2 * at + which], (...  18.2 us
    all_gather x1, waiting for transfers between devices, per_device(): grads = lax.all_gather(total, 'rows', axis=0, tiled=True)  11.5 us
    concatenate x5, other arithmetic, bundle(): jnp.concatenate([piece({'f': frames, 'c': cotangent}[v], k, r) for v, r i...  9.36 us
    unnamed x38, local copies, waits for them, and re-layouts  8.95 us
  transfers between devices with their start and end apart: 24, of which 12 were waited for; matrix products, arithmetic and copies ran while one was open for 10% of the time, Pallas kernels for 28%

profile of v2, /device:TPU:0, one launch (start us, length us, event | category | flops | bytes accessed | tf_op | source)
XLA Modules:
  0.0 428.2 jit_solution(6614873769150839429)
XLA Ops:
  7.3 1.4 maximum_maximum_fusion.biases
  8.7 2.3 shard_map.195
  11.0 3.1 collective-permute-start
  14.1 2.6 collective-permute-start.1
  16.7 1.3 collective-permute-start.2
  18.1 2.9 dynamic-slice_bitcast_fusion.1
  21.4 1.3 dynamic-slice_bitcast_fusion.2
  22.8 0.9 pad_maximum_fusion.3
  24.4 0.9 pad_maximum_fusion.4
  25.3 3.1 collective-permute-start.4
  28.5 1.3 pad_maximum_fusion.6
  29.8 12.7 %collective-permute-done.1.refs_6_ = bf16[1488,128]{1,0:T(8,128)(2,1)S(1)} collective-permute-done((bf16[1488,128]{1,0:T(8,128)(2,1)}, bf16[1488,128]{1,0:T(8,128)(2,1)S(1)}, u32[]{:S(2)}, u32[]{:S(2)}) %collective-permute-start.1) | collective-permute-done | bytes 380960 | tf_op jit(solution)/shard_map/frames_0/ppermute | solution.py:542
  42.6 16.7 %collective-permute-done.3.refs_8_ = bf16[3072,128]{1,0:T(8,128)(2,1)S(1)} collective-permute-done((bf16[3072,128]{1,0:T(8,128)(2,1)}, bf16[3072,128]{1,0:T(8,128)(2,1)S(1)}, u32[]{:S(2)}, u32[]{:S(2)}) %collective-permute-start.3) | collective-permute-done | bytes 786464 | tf_op jit(solution)/shard_map/inputs_1/ppermute | solution.py:542
  59.3 15.9 %collective-permute-done.4.refs_10_ = bf16[3072,128]{1,0:T(8,128)(2,1)S(1)} collective-permute-done((bf16[3072,128]{1,0:T(8,128)(2,1)}, bf16[3072,128]{1,0:T(8,128)(2,1)S(1)}, u32[]{:S(2)}, u32[]{:S(2)}) %collective-permute-start.4) | collective-permute-done | bytes 786464 | tf_op jit(solution)/shard_map/inputs_1/ppermute | solution.py:542
  75.3 2.2 pad_maximum_fusion.5
  77.5 9.1 %collective-permute-start.5 = (bf16[3072,128]{1,0:T(8,128)(2,1)}, bf16[3072,128]{1,0:T(8,128)(2,1)S(1)}, u32[]{:S(2)}, u32[]{:S(2)}) collective-permute-start(bf16[3072,128]{1,0:T(8,128)(2,1)} %pad_maximum_fusion.5), channel_id=1, source_target_pairs={{0,2},{1,3},{2,0},{3,1},{4,6},{5,7},{6,4},{7,5},{8,10},{9,11},{10,... | collective-permute-start | bytes 2359304 | tf_op jit(solution)/shard_map/inputs_1/ppermute | solution.py:542
  86.6 1.4 fusion.24
  88.3 2.4 pad_maximum_fusion.2
  90.8 2.9 pad_maximum_fusion
  93.8 26.6 %collective-permute-done.5.refs_9_ = bf16[3072,128]{1,0:T(8,128)(2,1)S(1)} collective-permute-done((bf16[3072,128]{1,0:T(8,128)(2,1)}, bf16[3072,128]{1,0:T(8,128)(2,1)S(1)}, u32[]{:S(2)}, u32[]{:S(2)}) %collective-permute-start.5) | collective-permute-done | bytes 786464 | tf_op jit(solution)/shard_map/inputs_1/ppermute | solution.py:542
  120.3 0.9 copy-done.6
  121.6 3.3 collective-permute-start.7
  125.2 1.1 copy-done.3
  126.4 1.1 copy-done.5
  127.5 1.1 copy-done.7
  128.6 60.4 %shard_map.196 = (f32[3712,512]{1,0:T(8,128)}, f32[2,4,128]{2,1,0:T(4,128)S(1)}, bf16[16,1024,128]{2,1,0:T(8,128)(2,1)}, bf16[16,1024,128]{2,1,0:T(8,128)(2,1)},...) custom-call(s32[1]{0:T(128)} %bitcast.z_ref, ...), custom_call_target="tpu_custom_call" | custom-call | flops 9663676416 | bytes 1000000 | tf_op jit(solution)/shard_map/pallas_call | solution.py:431
  189.1 3.5 collective-permute-done.7.refs_6_
  192.6 22.0 %collective-permute-start.9 = (bf16[4,1024,128]{2,1,0:T(8,128)(2,1)S(1)}, bf16[4,1024,128]{2,1,0:T(8,128)(2,1)S(1)}, u32[]{:S(2)}, u32[]{:S(2)}) collective-permute-start(bf16[4,1024,128]{2,1,0:T(8,128)(2,1)S(1)} %get-tuple-element.68), channel_id=1, source_target_pairs={{0,3},{1,0},{2,1},{3,2},{4,7},{5,4},{6,5},{7,6},{8,11},{9,8},{10,9... | collective-permute-start | bytes 3145736 | tf_op jit(solution)/shard_map/results_0/ppermute | solution.py:542
  214.6 2.5 collective-permute-start.10
  217.1 61.0 %shard_map.197 = (bf16[3712,512]{1,0:T(8,128)(2,1)}, f32[2,4,128]{2,1,0:T(4,128)S(1)}, bf16[16,1024,128]{2,1,0:T(8,128)(2,1)}, bf16[16,1024,128]{2,1,0:T(8,128)(...) custom-call(s32[1]{0:T(128)} %bitcast.z_ref, ...), custom_call_target="tpu_custom_call", output_to_operand_aliasing={{2}: (12, {}), {3}: (13, {})} | custom-call | flops 9663676416 | bytes 1000000 | tf_op jit(solution)/shard_map/pallas_call | solution.py:431
  278.9 0.8 copy-done.9
  279.7 0.8 copy-done.10
  280.5 0.8 copy-done.11
  281.3 3.8 collective-permute-done.10
  285.1 1.0 copy-done.14
  286.2 26.5 %collective-permute-done.11 = bf16[4,1024,128]{2,1,0:T(8,128)(2,1)} collective-permute-done((bf16[4,1024,128]{2,1,0:T(8,128)(2,1)}, bf16[4,1024,128]{2,1,0:T(8,128)(2,1)}, u32[]{:S(2)}, u32[]{:S(2)}) %collective-permute-start.11) | collective-permute-done | bytes 1048608 | tf_op jit(solution)/shard_map/results_0/ppermute | solution.py:542
  312.7 2.0 collective-permute-start.13
  314.8 1.8 collective-permute-start.18
  316.6 22.6 %collective-permute-done.12 = bf16[2,1024,128]{2,1,0:T(8,128)(2,1)} collective-permute-done((bf16[2,1024,128]{2,1,0:T(8,128)(2,1)}, bf16[2,1024,128]{2,1,0:T(8,128)(2,1)}, u32[]{:S(2)}, u32[]{:S(2)}) %collective-permute-start.12) | collective-permute-done | bytes 524320 | tf_op jit(solution)/shard_map/results_2/ppermute | solution.py:542
  339.2 1.0 constant_dynamic-slice_fusion.2
  341.0 1.5 collective-permute-start.15
  342.4 1.5 collective-permute-start.14
  343.9 17.9 %collective-permute-done.16 = bf16[480,128]{1,0:T(8,128)(2,1)S(1)} collective-permute-done((bf16[480,128]{1,0:T(8,128)(2,1)}, bf16[480,128]{1,0:T(8,128)(2,1)S(1)}, u32[]{:S(2)}, u32[]{:S(2)}) %collective-permute-start.16) | collective-permute-done | bytes 122912 | tf_op jit(solution)/shard_map/sums/ppermute | solution.py:542
  361.8 17.3 %collective-permute-done.15 = bf16[480,128]{1,0:T(8,128)(2,1)S(1)} collective-permute-done((bf16[480,128]{1,0:T(8,128)(2,1)}, bf16[480,128]{1,0:T(8,128)(2,1)S(1)}, u32[]{:S(2)}, u32[]{:S(2)}) %collective-permute-start.15) | collective-permute-done | bytes 122912 | tf_op jit(solution)/shard_map/sums/ppermute | solution.py:542
  379.1 1.6 convert_add_fusion
  380.9 2.4 collective-permute-start.19
  383.3 0.8 fusion.14
  384.1 0.8 fusion.13
  384.9 1.9 fusion.12
  386.8 0.8 fusion.11
  387.6 0.8 fusion.10
  388.4 1.9 fusion.9
  390.3 1.9 fusion.8
  392.2 1.9 fusion.7
  394.1 1.9 fusion.6
  396.6 11.5 %all-gather.5.cloned.1.call-done = f32[3712,128]{1,0:T(8,128)} async-done(((f32[464,128]{1,0:T(8,128)}), f32[3712,128]{1,0:T(8,128)}) %all-gather.5.cloned.1.call-update) | async-done | bytes 1900560 | tf_op jit(solution)/shard_map/all_gather | solution.py:656
  408.1 1.7 fusion.27
  409.7 2.6 fusion.25
  412.3 1.3 fusion.26
  413.7 1.2 slice_bitcast_fusion.24
  414.9 1.9 fusion.2
  416.7 1.3 collective-permute-done.19
  418.0 1.9 fusion.1
  419.8 1.9 fusion
  (79 shorter events, 5.0 us)
Async XLA Ops:
  7.2 118.0 %copy-start = (bf16[16,4,128]{2,1,0:T(4,128)(2,1)S(1)}, bf16[16,4,128]{2,1,0:T(4,128)(2,1)}, u32[]{:S(2)}) copy-start(bf16[16,4,128]{2,1,0:T(4,128)(2,1)} %param.13) | copy-start | bytes 49156
  7.2 118.0 %all-gather.3.cloned.1.call-start = ((), (), s32[]{:S(2)}) async-start(), calls=%async_computation.1 | async-start | bytes 4276224 | tf_op jit(solution)/shard_map/all_gather | solution.py:593
  11.0 18.7 %collective-permute-start = (bf16[1488,128]{1,0:T(8,128)(2,1)}, bf16[1488,128]{1,0:T(8,128)(2,1)S(1)}, u32[]{:S(2)}, u32[]{:S(2)}) collective-permute-start(bf16[1488,128]{1,0:T(8,128)(2,1)} %get-tuple-element.54), channel_id=1, source_target_pairs={{0,1},{1,2},{2,3},{3,0},{4,5},{5,6},{6,7},{7,4},{8,9},{9,10},{10,1... | collective-permute-start | bytes 1142792 | tf_op jit(solution)/shard_map/frames_0/ppermute | solution.py:542
  14.1 28.4 %collective-permute-start.1 = (bf16[1488,128]{1,0:T(8,128)(2,1)}, bf16[1488,128]{1,0:T(8,128)(2,1)S(1)}, u32[]{:S(2)}, u32[]{:S(2)}) collective-permute-start(bf16[1488,128]{1,0:T(8,128)(2,1)} %get-tuple-element.55), channel_id=1, source_target_pairs={{0,2},{1,3},{2,0},{3,1},{4,6},{5,7},{6,4},{7,5},{8,10},{9,11},{10,... | collective-permute-start | bytes 1142792 | tf_op jit(solution)/shard_map/frames_0/ppermute | solution.py:542
  16.7 25.9 %collective-permute-start.2 = (bf16[1488,128]{1,0:T(8,128)(2,1)}, bf16[1488,128]{1,0:T(8,128)(2,1)S(1)}, u32[]{:S(2)}, u32[]{:S(2)}) collective-permute-start(bf16[1488,128]{1,0:T(8,128)(2,1)} %get-tuple-element.56), channel_id=1, source_target_pairs={{0,3},{1,0},{2,1},{3,2},{4,7},{5,4},{6,5},{7,6},{8,11},{9,8},{10,9... | collective-permute-start | bytes 1142792 | tf_op jit(solution)/shard_map/frames_0/ppermute | solution.py:542
  18.1 3.4 copy-start.12
  23.7 35.6 %collective-permute-start.3 = (bf16[3072,128]{1,0:T(8,128)(2,1)}, bf16[3072,128]{1,0:T(8,128)(2,1)S(1)}, u32[]{:S(2)}, u32[]{:S(2)}) collective-permute-start(bf16[3072,128]{1,0:T(8,128)(2,1)} %pad_maximum_fusion.3), channel_id=1, source_target_pairs={{0,1},{1,2},{2,3},{3,0},{4,5},{5,6},{6,7},{7,4},{8,9},{9,10},{10,1... | collective-permute-start | bytes 2359304 | tf_op jit(solution)/shard_map/inputs_1/ppermute | solution.py:542
  25.3 49.9 %collective-permute-start.4 = (bf16[3072,128]{1,0:T(8,128)(2,1)}, bf16[3072,128]{1,0:T(8,128)(2,1)S(1)}, u32[]{:S(2)}, u32[]{:S(2)}) collective-permute-start(bf16[3072,128]{1,0:T(8,128)(2,1)} %pad_maximum_fusion.4), channel_id=1, source_target_pairs={{0,3},{1,0},{2,1},{3,2},{4,7},{5,4},{6,5},{7,6},{8,11},{9,8},{10,9... | collective-permute-start | bytes 2359304 | tf_op jit(solution)/shard_map/inputs_1/ppermute | solution.py:542
  42.6 32.6 %copy-start.13 = (bf16[464,512]{1,0:T(8,128)(2,1)}, bf16[464,512]{1,0:T(8,128)(2,1)S(1)}, u32[]{:S(2)}) copy-start(bf16[464,512]{1,0:T(8,128)(2,1)S(1)} %slice_dynamic-update-slice_fusion) | copy-start | bytes 1425412
  59.3 28.9 %copy-start.2 = (bf16[3072,128]{1,0:T(8,128)(2,1)}, bf16[3072,128]{1,0:T(8,128)(2,1)S(1)}, u32[]{:S(2)}) copy-start(bf16[3072,128]{1,0:T(8,128)(2,1)S(1)} %collective-permute-done.3.refs_8_) | copy-start | bytes 2359300
  75.2 18.5 %copy-start.4 = (bf16[3072,128]{1,0:T(8,128)(2,1)}, bf16[3072,128]{1,0:T(8,128)(2,1)S(1)}, u32[]{:S(2)}) copy-start(bf16[3072,128]{1,0:T(8,128)(2,1)S(1)} %collective-permute-done.4.refs_10_) | copy-start | bytes 2359300
  75.3 263.9 %reduce-scatter.2.cloned.1.call-start = ((), (), s32[]{:S(2)}) async-start(), calls=%async_computation.2 | async-start | bytes 4276224 | tf_op jit(solution)/shard_map/reduce_scatter | solution.py:640
  77.5 42.9 %collective-permute-start.5 = (bf16[3072,128]{1,0:T(8,128)(2,1)}, bf16[3072,128]{1,0:T(8,128)(2,1)S(1)}, u32[]{:S(2)}, u32[]{:S(2)}) collective-permute-start(bf16[3072,128]{1,0:T(8,128)(2,1)} %pad_maximum_fusion.5), channel_id=1, source_target_pairs={{0,2},{1,3},{2,0},{3,1},{4,6},{5,7},{6,4},{7,5},{8,10},{9,11},{10,... | collective-permute-start | bytes 2359304 | tf_op jit(solution)/shard_map/inputs_1/ppermute | solution.py:542
  88.2 36.9 %copy-start.18 = (s32[4]{0:T(128)S(1)}, s32[4]{0:T(128)}, u32[]{:S(2)}) copy-start(s32[4]{0:T(128)} %get-tuple-element.96) | copy-start | bytes 52
  120.3 0.9 copy-start.6
  121.2 67.9 %collective-permute-start.6 = (bf16[4096,128]{1,0:T(8,128)(2,1)}, bf16[4096,128]{1,0:T(8,128)(2,1)S(1)}, u32[]{:S(2)}, u32[]{:S(2)}) collective-permute-start(bf16[4096,128]{1,0:T(8,128)(2,1)} %get-tuple-element.58), channel_id=1, source_target_pairs={{0,1},{1,2},{2,3},{3,0},{4,5},{5,6},{6,7},{7,4},{8,9},{9,10},{10,1... | collective-permute-start | bytes 3145736 | tf_op jit(solution)/shard_map/inputs_2/ppermute | solution.py:542
  121.6 70.9 %collective-permute-start.7 = (bf16[4096,128]{1,0:T(8,128)(2,1)}, bf16[4096,128]{1,0:T(8,128)(2,1)S(1)}, u32[]{:S(2)}, u32[]{:S(2)}) collective-permute-start(bf16[4096,128]{1,0:T(8,128)(2,1)} %get-tuple-element.59), channel_id=1, source_target_pairs={{0,2},{1,3},{2,0},{3,1},{4,6},{5,7},{6,4},{7,5},{8,10},{9,11},{10,... | collective-permute-start | bytes 3145736 | tf_op jit(solution)/shard_map/inputs_2/ppermute | solution.py:542
  124.9 67.7 %collective-permute-start.8 = (bf16[4096,128]{1,0:T(8,128)(2,1)}, bf16[4096,128]{1,0:T(8,128)(2,1)}, u32[]{:S(2)}, u32[]{:S(2)}) collective-permute-start(bf16[4096,128]{1,0:T(8,128)(2,1)} %pad_maximum_fusion.2), channel_id=1, source_target_pairs={{0,3},{1,0},{2,1},{3,2},{4,7},{5,4},{6,5},{7,6},{8,11},{9,8},{10,9... | collective-permute-start | bytes 3145736 | tf_op jit(solution)/shard_map/inputs_2/ppermute | solution.py:542
  125.2 1.1 copy-start.3
  126.4 1.1 copy-start.5
  127.5 1.1 copy-start.7
  192.6 88.7 %collective-permute-start.9 = (bf16[4,1024,128]{2,1,0:T(8,128)(2,1)S(1)}, bf16[4,1024,128]{2,1,0:T(8,128)(2,1)S(1)}, u32[]{:S(2)}, u32[]{:S(2)}) collective-permute-start(bf16[4,1024,128]{2,1,0:T(8,128)(2,1)S(1)} %get-tuple-element.68), channel_id=1, source_target_pairs={{0,3},{1,0},{2,1},{3,2},{4,7},{5,4},{6,5},{7,6},{8,11},{9,8},{10,9... | collective-permute-start | bytes 3145736 | tf_op jit(solution)/shard_map/results_0/ppermute | solution.py:542
  214.6 70.5 %collective-permute-start.10 = (bf16[4,1024,128]{2,1,0:T(8,128)(2,1)S(1)}, bf16[4,1024,128]{2,1,0:T(8,128)(2,1)S(1)}, u32[]{:S(2)}, u32[]{:S(2)}) collective-permute-start(bf16[4,1024,128]{2,1,0:T(8,128)(2,1)S(1)} %get-tuple-element.69), channel_id=1, source_target_pairs={{0,2},{1,3},{2,0},{3,1},{4,6},{5,7},{6,4},{7,5},{8,10},{9,11},{10,... | collective-permute-start | bytes 3145736 | tf_op jit(solution)/shard_map/results_0/ppermute | solution.py:542
  278.1 0.8 copy-start.8
  278.9 0.8 copy-start.9
  279.7 0.8 copy-start.10
  280.5 0.8 copy-start.11
  281.3 3.8 copy-start.16
  285.1 1.0 copy-start.14
  286.1 97.2 %copy-start.17 = (bf16[4,1024,128]{2,1,0:T(8,128)(2,1)S(1)}, bf16[4,1024,128]{2,1,0:T(8,128)(2,1)}, u32[]{:S(2)}) copy-start(bf16[4,1024,128]{2,1,0:T(8,128)(2,1)} %copy-done.16) | copy-start | bytes 3145732
  286.1 98.1 %copy-start.15 = (bf16[4,1024,128]{2,1,0:T(8,128)(2,1)S(1)}, bf16[4,1024,128]{2,1,0:T(8,128)(2,1)}, u32[]{:S(2)}) copy-start(bf16[4,1024,128]{2,1,0:T(8,128)(2,1)} %copy-done.14) | copy-start | bytes 3145732
  286.1 122.0 %all-gather.5.cloned.1.call-start = ((), (), s32[]{:S(2)}) async-start(), calls=%async_computation.3 | async-start | bytes 2138112 | tf_op jit(solution)/shard_map/all_gather | solution.py:656
  286.1 26.6 %collective-permute-start.11 = (bf16[4,1024,128]{2,1,0:T(8,128)(2,1)}, bf16[4,1024,128]{2,1,0:T(8,128)(2,1)}, u32[]{:S(2)}, u32[]{:S(2)}) collective-permute-start(bf16[4,1024,128]{2,1,0:T(8,128)(2,1)} %get-tuple-element.74), channel_id=1, source_target_pairs={{0,1},{1,2},{2,3},{3,0},{4,5},{5,6},{6,7},{7,4},{8,9},{9,10},{10,1... | collective-permute-start | bytes 3145736 | tf_op jit(solution)/shard_map/results_0/ppermute | solution.py:542
  312.7 26.4 %collective-permute-start.12 = (bf16[2,1024,128]{2,1,0:T(8,128)(2,1)}, bf16[2,1024,128]{2,1,0:T(8,128)(2,1)}, u32[]{:S(2)}, u32[]{:S(2)}) collective-permute-start(bf16[2,1024,128]{2,1,0:T(8,128)(2,1)} %copy-done.11), channel_id=1, source_target_pairs={{0,3},{1,0},{2,1},{3,2},{4,7},{5,4},{6,5},{7,6},{8,11},{9,8},{10,9... | collective-permute-start | bytes 1572872 | tf_op jit(solution)/shard_map/results_2/ppermute | solution.py:542
  312.7 26.4 %collective-permute-start.13 = (bf16[2,1024,128]{2,1,0:T(8,128)(2,1)}, bf16[2,1024,128]{2,1,0:T(8,128)(2,1)}, u32[]{:S(2)}, u32[]{:S(2)}) collective-permute-start(bf16[2,1024,128]{2,1,0:T(8,128)(2,1)} %copy-done.10), channel_id=1, source_target_pairs={{0,1},{1,2},{2,3},{3,0},{4,5},{5,6},{6,7},{7,4},{8,9},{9,10},{10,1... | collective-permute-start | bytes 1572872 | tf_op jit(solution)/shard_map/results_2/ppermute | solution.py:542
  314.8 66.0 %collective-permute-start.18 = (bf16[2,1024,128]{2,1,0:T(8,128)(2,1)}, bf16[2,1024,128]{2,1,0:T(8,128)(2,1)}, u32[]{:S(2)}, u32[]{:S(2)}) collective-permute-start(bf16[2,1024,128]{2,1,0:T(8,128)(2,1)} %copy-done.9), channel_id=1, source_target_pairs={{0,3},{1,0},{2,1},{3,2},{4,7},{5,4},{6,5},{7,6},{8,11},{9,8},{10,9... | collective-permute-start | bytes 1572872 | tf_op jit(solution)/shard_map/results_3/ppermute | solution.py:542
  316.6 64.2 %collective-permute-start.17 = (bf16[2,1024,128]{2,1,0:T(8,128)(2,1)}, bf16[2,1024,128]{2,1,0:T(8,128)(2,1)}, u32[]{:S(2)}, u32[]{:S(2)}) collective-permute-start(bf16[2,1024,128]{2,1,0:T(8,128)(2,1)} %copy-done.8), channel_id=1, source_target_pairs={{0,2},{1,3},{2,0},{3,1},{4,6},{5,7},{6,4},{7,5},{8,10},{9,11},{10,... | collective-permute-start | bytes 1572872 | tf_op jit(solution)/shard_map/results_2/ppermute | solution.py:542
  341.0 20.9 %collective-permute-start.16 = (bf16[480,128]{1,0:T(8,128)(2,1)}, bf16[480,128]{1,0:T(8,128)(2,1)S(1)}, u32[]{:S(2)}, u32[]{:S(2)}) collective-permute-start(bf16[480,128]{1,0:T(8,128)(2,1)} %get-tuple-element.153), channel_id=1, source_target_pairs={{0,3},{1,0},{2,1},{3,2},{4,7},{5,4},{6,5},{7,6},{8,11},{9,8},{10,9... | collective-permute-start | bytes 368648 | tf_op jit(solution)/shard_map/sums/ppermute | solution.py:542
  341.0 38.2 %collective-permute-start.15 = (bf16[480,128]{1,0:T(8,128)(2,1)}, bf16[480,128]{1,0:T(8,128)(2,1)S(1)}, u32[]{:S(2)}, u32[]{:S(2)}) collective-permute-start(bf16[480,128]{1,0:T(8,128)(2,1)} %get-tuple-element.154), channel_id=1, source_target_pairs={{0,2},{1,3},{2,0},{3,1},{4,6},{5,7},{6,4},{7,5},{8,10},{9,11},{10,... | collective-permute-start | bytes 368648 | tf_op jit(solution)/shard_map/sums/ppermute | solution.py:542
  342.4 36.7 %collective-permute-start.14 = (bf16[480,128]{1,0:T(8,128)(2,1)}, bf16[480,128]{1,0:T(8,128)(2,1)S(1)}, u32[]{:S(2)}, u32[]{:S(2)}) collective-permute-start(bf16[480,128]{1,0:T(8,128)(2,1)} %get-tuple-element.152), channel_id=1, source_target_pairs={{0,1},{1,2},{2,3},{3,0},{4,5},{5,6},{6,7},{7,4},{8,9},{9,10},{10,1... | collective-permute-start | bytes 368648 | tf_op jit(solution)/shard_map/sums/ppermute | solution.py:542
  380.9 37.1 %collective-permute-start.19 = (bf16[2,1024,128]{2,1,0:T(8,128)(2,1)S(1)}, bf16[2,1024,128]{2,1,0:T(8,128)(2,1)}, u32[]{:S(2)}, u32[]{:S(2)}) collective-permute-start(bf16[2,1024,128]{2,1,0:T(8,128)(2,1)S(1)} %get-tuple-element.86), channel_id=1, source_target_pairs={{0,2},{1,3},{2,0},{3,1},{4,6},{5,7},{6,4},{7,5},{8,10},{9,11},{10,... | collective-permute-start | bytes 1572872 | tf_op jit(solution)/shard_map/results_3/ppermute | solution.py:542
  383.3 36.5 %collective-permute-start.20 = (bf16[2,1024,128]{2,1,0:T(8,128)(2,1)S(1)}, bf16[2,1024,128]{2,1,0:T(8,128)(2,1)}, u32[]{:S(2)}, u32[]{:S(2)}) collective-permute-start(bf16[2,1024,128]{2,1,0:T(8,128)(2,1)S(1)} %get-tuple-element.87), channel_id=1, source_target_pairs={{0,1},{1,2},{2,3},{3,0},{4,5},{5,6},{6,7},{7,4},{8,9},{9,10},{10,1... | collective-permute-start | bytes 1572872 | tf_op jit(solution)/shard_map/results_3/ppermute | solution.py:542
  392.2 29.5 %copy-start.1 = (bf16[16,4,128]{2,1,0:T(4,128)(2,1)S(1)}, bf16[16,4,128]{2,1,0:T(4,128)(2,1)}, u32[]{:S(2)}) copy-start(bf16[16,4,128]{2,1,0:T(4,128)(2,1)} %param.13) | copy-start | bytes 49156
Sparse Core Ops, SparseCore 0:
  75.4 41.6 all-gather.2
  286.2 47.5 reduce-scatter.1
  380.9 27.0 all-gather.4

commit v3 on v2

--- a/solution.py
+++ b/solution.py
@@ -587,9 +587,9 @@
     late = [(v, r) for r in range(half, per) for v in "fc"]
     got_a = fetch("frames_0", bundles)
     got_b = fetch("inputs_1", bundle(*early[1:]))
-    got_c = fetch("inputs_2", after(bundle(*late), got_b))
+    got_c = fetch("inputs_2", after(bundle(*late), got_b[1]))
     mine = over_ch(mine, [v[frames_n:] for v in got_a], 1)
-    mine = after(mine, [got_b[0], got_b[2]])
+    mine = after(mine, got_b[1])
     weights = lax.all_gather(mine, "rows", axis=0, tiled=True)
 
     first = z * per
@@ -632,11 +632,11 @@
     for r in others:
         group = pieces[r * (n - 1) : (r + 1) * (n - 1)]
         if r == 0:
-            group = after(group, back[0][2])
+            group = [group[0], *after(group[1:], back[0][2])]
         back.append([send(v, n - k, f"results_{half + r}") for k, v in enumerate(group, 1)])
     dstyles = [dstyle_a, dstyle_b]
 
-    sums = after(sums, back[0][:2])
+    sums = after(sums, back[0][1:])
     sums = lax.psum_scatter(sums, "rows", scatter_dimension=0, tiled=True)
     sums = after(sums, [back[1][0], back[1][2]])
     style_grad = jnp.concatenate(dstyles, axis=0).reshape(per * segs, style_n).astype(sums.dtype)
@@ -652,7 +652,7 @@
         total = total + v[:part].astype(f32)
     grad_style = over_ch(style_grad, [v[part:] for v in got], 0)
     grad_style = grad_style.astype(f32).reshape(style_vector.shape)
-    total = after(total, [back[1][1], back[2][0]])
+    total = after(total, [back[1][1]])
     grads = lax.all_gather(total, "rows", axis=0, tiled=True)
     splits = [sum(sizes[: i + 1]) for i in range(len(sizes))]
     g1, g2, gf1, gf2, gb1, gb2, gb = [

time: 429 us -> 422 us (0.984)
  starting transfers between devices: 57.7 us -> 31.7 us
  waiting for transfers between devices: 176 us -> 196 us
    ppermute x21, starting transfers between devices: 57.6 us -> 31.6 us  [send(): return lax.ppermute(v, 'ch', shift(k))]
    reduce_scatter x1, waiting for transfers between devices: 0.01 us -> 21.3 us  [per_device(): sums = lax.psum_scatter(sums, 'rows', scatter_dimension=0, tiled=True)]
    all_gather x1, waiting for transfers between devices: 11.5 us -> 6.76 us  [per_device(): grads = lax.all_gather(total, 'rows', axis=0, tiled=True)]
    unnamed x38 -> x34, local copies, waits for them, and re-layouts: 8.95 us -> 5.8 us
  transfers between devices with their start and end apart: 24 -> 24, of which waited for: 12 -> 13; matrix products, arithmetic and copies ran while one was open for 10% -> 11% of each run, Pallas kernels for 28% -> 29%
where the time goes in v3:
time: 422 us; the launch traced here: 421 us
  waiting for transfers between devices  196 us (46%)
  Pallas kernels  124 us (29%)
  local copies, waits for them, and re-layouts  39.4 us (9%)
  starting transfers between devices  31.7 us (8%)
  other arithmetic  15.9 us (4%)
  between operations  14.1 us (3%)
    ppermute x21, waiting for transfers between devices, send(): return lax.ppermute(v, 'ch', shift(k))  168 us
    pallas_call x2, Pallas kernels, block_rows(): pl.pallas_call(functools.partial(rows_kernel, n, segs, style_n, per, firs...  122 us
    ppermute x21, starting transfers between devices, send(): return lax.ppermute(v, 'ch', shift(k))  31.6 us
    reduce_scatter x1, waiting for transfers between devices, per_device(): sums = lax.psum_scatter(sums, 'rows', scatter_dimension=0, tiled=True)  21.3 us
    dynamic_update_slice x12, local copies, waits for them, and re-layouts, per_device(): lax.dynamic_update_slice(results[which], v[None, None, 2 * at + which], (...  20.2 us
    concatenate x5, other arithmetic, bundle(): jnp.concatenate([piece({'f': frames, 'c': cotangent}[v], k, r) for v, r i...  9.02 us
  transfers between devices with their start and end apart: 24, of which 13 were waited for; matrix products, arithmetic and copies ran while one was open for 11% of the time, Pallas kernels for 29%

profile of v3, /device:TPU:0, one launch (start us, length us, event | category | flops | bytes accessed | tf_op | source)
XLA Modules:
  0.0 421.4 jit_solution(1032669541981375129)
XLA Ops:
  7.3 1.4 maximum_maximum_fusion.biases
  8.7 2.3 shard_map.195
  11.0 3.1 collective-permute-start
  14.1 2.6 collective-permute-start.1
  16.7 1.3 collective-permute-start.2
  18.1 2.8 dynamic-slice_bitcast_fusion.1
  21.3 1.5 dynamic-slice_bitcast_fusion.2
  22.8 0.9 pad_maximum_fusion.3
  24.0 1.3 pad_maximum_fusion.6
  25.2 0.9 collective-permute-done.refs_5_
  26.2 16.3 %collective-permute-done.1.refs_6_ = bf16[1488,128]{1,0:T(8,128)(2,1)S(1)} collective-permute-done((bf16[1488,128]{1,0:T(8,128)(2,1)}, bf16[1488,128]{1,0:T(8,128)(2,1)S(1)}, u32[]{:S(2)}, u32[]{:S(2)}) %collective-permute-start.1) | collective-permute-done | bytes 380960 | tf_op jit(solution)/shard_map/frames_0/ppermute | solution.py:542
  42.6 40.8 %collective-permute-done.3.refs_9_ = bf16[3072,128]{1,0:T(8,128)(2,1)S(1)} collective-permute-done((bf16[3072,128]{1,0:T(8,128)(2,1)}, bf16[3072,128]{1,0:T(8,128)(2,1)S(1)}, u32[]{:S(2)}, u32[]{:S(2)}) %collective-permute-start.3) | collective-permute-done | bytes 786464 | tf_op jit(solution)/shard_map/inputs_1/ppermute | solution.py:542
  83.5 2.3 pad_maximum_fusion.4
  85.9 2.0 pad_maximum_fusion.5
  87.9 3.8 collective-permute-start.8
  91.7 0.9 fusion.24
  93.1 2.7 pad_maximum_fusion
  95.8 1.0 pad_maximum_fusion.2
  97.5 3.2 collective-permute-start.6
  100.7 7.7 %collective-permute-done.7.refs_8_ = bf16[3072,128]{1,0:T(8,128)(2,1)} collective-permute-done((bf16[3072,128]{1,0:T(8,128)(2,1)}, bf16[3072,128]{1,0:T(8,128)(2,1)}, u32[]{:S(2)}, u32[]{:S(2)}) %collective-permute-start.7) | collective-permute-done | bytes 786464 | tf_op jit(solution)/shard_map/inputs_1/ppermute | solution.py:542
  108.5 38.7 %collective-permute-done.8.refs_10_ = bf16[3072,128]{1,0:T(8,128)(2,1)} collective-permute-done((bf16[3072,128]{1,0:T(8,128)(2,1)}, bf16[3072,128]{1,0:T(8,128)(2,1)}, u32[]{:S(2)}, u32[]{:S(2)}) %collective-permute-start.8) | collective-permute-done | bytes 786464 | tf_op jit(solution)/shard_map/inputs_1/ppermute | solution.py:542
  147.2 1.1 copy-done.3
  148.4 60.6 %shard_map.196 = (f32[3712,512]{1,0:T(8,128)}, f32[2,4,128]{2,1,0:T(4,128)S(1)}, bf16[16,1024,128]{2,1,0:T(8,128)(2,1)}, bf16[16,1024,128]{2,1,0:T(8,128)(2,1)},...) custom-call(s32[1]{0:T(128)} %bitcast.z_ref, ...), custom_call_target="tpu_custom_call" | custom-call | flops 9663676416 | bytes 1000000 | tf_op jit(solution)/shard_map/pallas_call | solution.py:431
  209.0 4.3 %collective-permute-start.9 = (bf16[4,1024,128]{2,1,0:T(8,128)(2,1)S(1)}, bf16[4,1024,128]{2,1,0:T(8,128)(2,1)S(1)}, u32[]{:S(2)}, u32[]{:S(2)}) collective-permute-start(bf16[4,1024,128]{2,1,0:T(8,128)(2,1)S(1)} %get-tuple-element.67), channel_id=1, source_target_pairs={{0,2},{1,3},{2,0},{3,1},{4,6},{5,7},{6,4},{7,5},{8,10},{9,11},{10,... | collective-permute-start | bytes 3145736 | tf_op jit(solution)/shard_map/results_0/ppermute | solution.py:542
  213.4 1.0 collective-permute-start.10
  214.4 61.2 %shard_map.197 = (bf16[3712,512]{1,0:T(8,128)(2,1)}, f32[2,4,128]{2,1,0:T(4,128)S(1)}, bf16[16,1024,128]{2,1,0:T(8,128)(2,1)}, bf16[16,1024,128]{2,1,0:T(8,128)(...) custom-call(s32[1]{0:T(128)} %bitcast.z_ref, ...), custom_call_target="tpu_custom_call", output_to_operand_aliasing={{2}: (12, {}), {3}: (13, {})} | custom-call | flops 9663676416 | bytes 1000000 | tf_op jit(solution)/shard_map/pallas_call | solution.py:431
  275.6 0.8 copy-done.4
  276.4 0.8 copy-done.6
  277.2 0.8 copy-done.7
  278.0 0.8 copy-done.8
  278.8 2.4 collective-permute-done.9
  281.2 1.0 copy-done.11
  282.7 1.6 collective-permute-start.12
  284.3 2.2 collective-permute-start.17
  286.5 12.1 %collective-permute-done.11 = bf16[2,1024,128]{2,1,0:T(8,128)(2,1)} collective-permute-done((bf16[2,1024,128]{2,1,0:T(8,128)(2,1)}, bf16[2,1024,128]{2,1,0:T(8,128)(2,1)}, u32[]{:S(2)}, u32[]{:S(2)}) %collective-permute-start.11) | collective-permute-done | bytes 524320 | tf_op jit(solution)/shard_map/results_2/ppermute | solution.py:542
  298.6 11.1 %collective-permute-done.12 = bf16[2,1024,128]{2,1,0:T(8,128)(2,1)S(1)} collective-permute-done((bf16[2,1024,128]{2,1,0:T(8,128)(2,1)}, bf16[2,1024,128]{2,1,0:T(8,128)(2,1)S(1)}, u32[]{:S(2)}, u32[]{:S(2)}) %collective-permute-start.12) | collective-permute-done | bytes 524320 | tf_op jit(solution)/shard_map/results_2/ppermute | solution.py:542
  309.7 21.3 %reduce-scatter.2.cloned.1.call-done = bf16[464,512]{1,0:T(8,128)(2,1)} async-done(((bf16[3712,512]{1,0:T(8,128)(2,1)}), bf16[464,512]{1,0:T(8,128)(2,1)}) %reduce-scatter.2.cloned.1.call-update) | async-done | bytes 475152 | tf_op jit(solution)/shard_map/reduce_scatter | solution.py:640
  331.0 1.0 constant_dynamic-slice_fusion.2
  332.1 0.7 pad_maximum_fusion.9
  332.8 3.3 collective-permute-start.15
  336.2 1.1 collective-permute-start.13
  337.3 5.7 %collective-permute-done.15 = bf16[480,128]{1,0:T(8,128)(2,1)S(1)} collective-permute-done((bf16[480,128]{1,0:T(8,128)(2,1)}, bf16[480,128]{1,0:T(8,128)(2,1)S(1)}, u32[]{:S(2)}, u32[]{:S(2)}) %collective-permute-start.15) | collective-permute-done | bytes 122912 | tf_op jit(solution)/shard_map/sums/ppermute | solution.py:542
  342.9 19.9 %collective-permute-done.14 = bf16[480,128]{1,0:T(8,128)(2,1)S(1)} collective-permute-done((bf16[480,128]{1,0:T(8,128)(2,1)}, bf16[480,128]{1,0:T(8,128)(2,1)S(1)}, u32[]{:S(2)}, u32[]{:S(2)}) %collective-permute-start.14) | collective-permute-done | bytes 122912 | tf_op jit(solution)/shard_map/sums/ppermute | solution.py:542
  362.8 1.7 convert_add_fusion
  365.4 1.9 collective-permute-start.20
  367.3 1.9 fusion.14
  369.2 1.9 fusion.13
  371.0 1.9 fusion.12
  372.9 1.9 fusion.11
  374.8 0.8 fusion.10
  375.6 1.9 fusion.9
  377.4 1.9 fusion.8
  379.3 1.9 fusion.7
  381.1 0.8 fusion.6
  382.0 0.7 constant_dynamic-update-slice_fusion.2
  383.3 6.8 %all-gather.5.cloned.1.call-done = f32[3712,128]{1,0:T(8,128)} async-done(((f32[464,128]{1,0:T(8,128)}), f32[3712,128]{1,0:T(8,128)}) %all-gather.5.cloned.1.call-update) | async-done | bytes 1900560 | tf_op jit(solution)/shard_map/all_gather | solution.py:656
  390.1 2.6 fusion.25
  392.7 1.7 fusion.27
  394.4 1.3 fusion.26
  395.7 1.2 slice_bitcast_fusion.24
  396.9 1.9 fusion.2
  398.7 12.5 %collective-permute-done.19 = bf16[2,1024,128]{2,1,0:T(8,128)(2,1)} collective-permute-done((bf16[2,1024,128]{2,1,0:T(8,128)(2,1)S(1)}, bf16[2,1024,128]{2,1,0:T(8,128)(2,1)}, u32[]{:S(2)}, u32[]{:S(2)}) %collective-permute-start.19) | collective-permute-done | bytes 524320 | tf_op jit(solution)/shard_map/results_3/ppermute | solution.py:542
  411.2 1.9 fusion.1
  413.1 1.9 fusion
  (75 shorter events, 4.1 us)
Async XLA Ops:
  7.2 93.5 %copy-start = (bf16[16,4,128]{2,1,0:T(4,128)(2,1)S(1)}, bf16[16,4,128]{2,1,0:T(4,128)(2,1)}, u32[]{:S(2)}) copy-start(bf16[16,4,128]{2,1,0:T(4,128)(2,1)} %param.13) | copy-start | bytes 49156
  7.2 140.0 %all-gather.3.cloned.1.call-start = ((), (), s32[]{:S(2)}) async-start(), calls=%async_computation.1 | async-start | bytes 4276224 | tf_op jit(solution)/shard_map/all_gather | solution.py:593
  11.0 15.1 %collective-permute-start = (bf16[1488,128]{1,0:T(8,128)(2,1)}, bf16[1488,128]{1,0:T(8,128)(2,1)S(1)}, u32[]{:S(2)}, u32[]{:S(2)}) collective-permute-start(bf16[1488,128]{1,0:T(8,128)(2,1)} %get-tuple-element.53), channel_id=1, source_target_pairs={{0,1},{1,2},{2,3},{3,0},{4,5},{5,6},{6,7},{7,4},{8,9},{9,10},{10,1... | collective-permute-start | bytes 1142792 | tf_op jit(solution)/shard_map/frames_0/ppermute | solution.py:542
  14.1 28.4 %collective-permute-start.1 = (bf16[1488,128]{1,0:T(8,128)(2,1)}, bf16[1488,128]{1,0:T(8,128)(2,1)S(1)}, u32[]{:S(2)}, u32[]{:S(2)}) collective-permute-start(bf16[1488,128]{1,0:T(8,128)(2,1)} %get-tuple-element.54), channel_id=1, source_target_pairs={{0,2},{1,3},{2,0},{3,1},{4,6},{5,7},{6,4},{7,5},{8,10},{9,11},{10,... | collective-permute-start | bytes 1142792 | tf_op jit(solution)/shard_map/frames_0/ppermute | solution.py:542
  16.7 25.8 %collective-permute-start.2 = (bf16[1488,128]{1,0:T(8,128)(2,1)}, bf16[1488,128]{1,0:T(8,128)(2,1)S(1)}, u32[]{:S(2)}, u32[]{:S(2)}) collective-permute-start(bf16[1488,128]{1,0:T(8,128)(2,1)} %get-tuple-element.55), channel_id=1, source_target_pairs={{0,3},{1,0},{2,1},{3,2},{4,7},{5,4},{6,5},{7,6},{8,11},{9,8},{10,9... | collective-permute-start | bytes 1142792 | tf_op jit(solution)/shard_map/frames_0/ppermute | solution.py:542
  18.0 3.3 copy-start.9
  23.8 59.7 %collective-permute-start.3 = (bf16[3072,128]{1,0:T(8,128)(2,1)}, bf16[3072,128]{1,0:T(8,128)(2,1)S(1)}, u32[]{:S(2)}, u32[]{:S(2)}) collective-permute-start(bf16[3072,128]{1,0:T(8,128)(2,1)} %pad_maximum_fusion.3), channel_id=1, source_target_pairs={{0,2},{1,3},{2,0},{3,1},{4,6},{5,7},{6,4},{7,5},{8,10},{9,11},{10,... | collective-permute-start | bytes 2359304 | tf_op jit(solution)/shard_map/inputs_1/ppermute | solution.py:542
  42.6 40.9 %copy-start.10 = (bf16[464,512]{1,0:T(8,128)(2,1)}, bf16[464,512]{1,0:T(8,128)(2,1)S(1)}, u32[]{:S(2)}) copy-start(bf16[464,512]{1,0:T(8,128)(2,1)S(1)} %slice_dynamic-update-slice_fusion) | copy-start | bytes 1425412
  83.4 9.4 %copy-start.2 = (bf16[3072,128]{1,0:T(8,128)(2,1)}, bf16[3072,128]{1,0:T(8,128)(2,1)S(1)}, u32[]{:S(2)}) copy-start(bf16[3072,128]{1,0:T(8,128)(2,1)S(1)} %collective-permute-done.3.refs_9_) | copy-start | bytes 2359300
  83.5 12.3 %copy-start.13 = (bf16[1024,128]{1,0:T(8,128)(2,1)S(1)}, bf16[1024,128]{1,0:T(8,128)(2,1)}, u32[]{:S(2)}) copy-start(bf16[1024,128]{1,0:T(8,128)(2,1)} %get-tuple-element.110) | copy-start | bytes 786436
  83.5 247.6 %reduce-scatter.2.cloned.1.call-start = ((), (), s32[]{:S(2)}) async-start(), calls=%async_computation.2 | async-start | bytes 4276224 | tf_op jit(solution)/shard_map/reduce_scatter | solution.py:640
  85.9 22.6 %collective-permute-start.7 = (bf16[3072,128]{1,0:T(8,128)(2,1)}, bf16[3072,128]{1,0:T(8,128)(2,1)}, u32[]{:S(2)}, u32[]{:S(2)}) collective-permute-start(bf16[3072,128]{1,0:T(8,128)(2,1)} %pad_maximum_fusion.4), channel_id=1, source_target_pairs={{0,1},{1,2},{2,3},{3,0},{4,5},{5,6},{6,7},{7,4},{8,9},{9,10},{10,1... | collective-permute-start | bytes 2359304 | tf_op jit(solution)/shard_map/inputs_1/ppermute | solution.py:542
  87.9 59.3 %collective-permute-start.8 = (bf16[3072,128]{1,0:T(8,128)(2,1)}, bf16[3072,128]{1,0:T(8,128)(2,1)}, u32[]{:S(2)}, u32[]{:S(2)}) collective-permute-start(bf16[3072,128]{1,0:T(8,128)(2,1)} %pad_maximum_fusion.5), channel_id=1, source_target_pairs={{0,3},{1,0},{2,1},{3,2},{4,7},{5,4},{6,5},{7,6},{8,11},{9,8},{10,9... | collective-permute-start | bytes 2359304 | tf_op jit(solution)/shard_map/inputs_1/ppermute | solution.py:542
  92.8 3.0 copy-start.14
  92.8 3.0 copy-start.15
  92.8 3.0 copy-start.16
  96.8 112.2 %collective-permute-start.4 = (bf16[4096,128]{1,0:T(8,128)(2,1)}, bf16[4096,128]{1,0:T(8,128)(2,1)S(1)}, u32[]{:S(2)}, u32[]{:S(2)}) collective-permute-start(bf16[4096,128]{1,0:T(8,128)(2,1)} %get-tuple-element.57), channel_id=1, source_target_pairs={{0,1},{1,2},{2,3},{3,0},{4,5},{5,6},{6,7},{7,4},{8,9},{9,10},{10,1... | collective-permute-start | bytes 3145736 | tf_op jit(solution)/shard_map/inputs_2/ppermute | solution.py:542
  96.8 112.2 %collective-permute-start.5 = (bf16[4096,128]{1,0:T(8,128)(2,1)}, bf16[4096,128]{1,0:T(8,128)(2,1)}, u32[]{:S(2)}, u32[]{:S(2)}) collective-permute-start(bf16[4096,128]{1,0:T(8,128)(2,1)} %get-tuple-element.58), channel_id=1, source_target_pairs={{0,2},{1,3},{2,0},{3,1},{4,6},{5,7},{6,4},{7,5},{8,10},{9,11},{10,... | collective-permute-start | bytes 3145736 | tf_op jit(solution)/shard_map/inputs_2/ppermute | solution.py:542
  97.5 111.6 %collective-permute-start.6 = (bf16[4096,128]{1,0:T(8,128)(2,1)}, bf16[4096,128]{1,0:T(8,128)(2,1)}, u32[]{:S(2)}, u32[]{:S(2)}) collective-permute-start(bf16[4096,128]{1,0:T(8,128)(2,1)} %pad_maximum_fusion.2), channel_id=1, source_target_pairs={{0,3},{1,0},{2,1},{3,2},{4,7},{5,4},{6,5},{7,6},{8,11},{9,8},{10,9... | collective-permute-start | bytes 3145736 | tf_op jit(solution)/shard_map/inputs_2/ppermute | solution.py:542
  147.2 1.1 copy-start.3
  209.0 72.2 %collective-permute-start.9 = (bf16[4,1024,128]{2,1,0:T(8,128)(2,1)S(1)}, bf16[4,1024,128]{2,1,0:T(8,128)(2,1)S(1)}, u32[]{:S(2)}, u32[]{:S(2)}) collective-permute-start(bf16[4,1024,128]{2,1,0:T(8,128)(2,1)S(1)} %get-tuple-element.67), channel_id=1, source_target_pairs={{0,2},{1,3},{2,0},{3,1},{4,6},{5,7},{6,4},{7,5},{8,10},{9,11},{10,... | collective-permute-start | bytes 3145736 | tf_op jit(solution)/shard_map/results_0/ppermute | solution.py:542
  213.4 68.8 %collective-permute-start.10 = (bf16[4,1024,128]{2,1,0:T(8,128)(2,1)}, bf16[4,1024,128]{2,1,0:T(8,128)(2,1)}, u32[]{:S(2)}, u32[]{:S(2)}) collective-permute-start(bf16[4,1024,128]{2,1,0:T(8,128)(2,1)} %get-tuple-element.68), channel_id=1, source_target_pairs={{0,1},{1,2},{2,3},{3,0},{4,5},{5,6},{6,7},{7,4},{8,9},{9,10},{10,1... | collective-permute-start | bytes 3145736 | tf_op jit(solution)/shard_map/results_0/ppermute | solution.py:542
  275.6 0.8 copy-start.4
  276.4 0.8 copy-start.6
  277.2 0.8 copy-start.7
  278.0 0.8 copy-start.8
  281.2 1.0 copy-start.11
  282.2 82.4 %copy-start.5 = (bf16[2,1024,128]{2,1,0:T(8,128)(2,1)S(1)}, bf16[2,1024,128]{2,1,0:T(8,128)(2,1)}, u32[]{:S(2)}) copy-start(bf16[2,1024,128]{2,1,0:T(8,128)(2,1)} %copy-done.4) | copy-start | bytes 1572868
  282.2 107.9 %all-gather.5.cloned.1.call-start = ((), (), s32[]{:S(2)}) async-start(), calls=%async_computation.3 | async-start | bytes 2138112 | tf_op jit(solution)/shard_map/all_gather | solution.py:656
  282.2 16.4 %collective-permute-start.11 = (bf16[2,1024,128]{2,1,0:T(8,128)(2,1)}, bf16[2,1024,128]{2,1,0:T(8,128)(2,1)}, u32[]{:S(2)}, u32[]{:S(2)}) collective-permute-start(bf16[2,1024,128]{2,1,0:T(8,128)(2,1)} %copy-done.8), channel_id=1, source_target_pairs={{0,3},{1,0},{2,1},{3,2},{4,7},{5,4},{6,5},{7,6},{8,11},{9,8},{10,9... | collective-permute-start | bytes 1572872 | tf_op jit(solution)/shard_map/results_2/ppermute | solution.py:542
  282.7 27.0 %collective-permute-start.12 = (bf16[2,1024,128]{2,1,0:T(8,128)(2,1)}, bf16[2,1024,128]{2,1,0:T(8,128)(2,1)S(1)}, u32[]{:S(2)}, u32[]{:S(2)}) collective-permute-start(bf16[2,1024,128]{2,1,0:T(8,128)(2,1)} %copy-done.7), channel_id=1, source_target_pairs={{0,1},{1,2},{2,3},{3,0},{4,5},{5,6},{6,7},{7,4},{8,9},{9,10},{10,1... | collective-permute-start | bytes 1572872 | tf_op jit(solution)/shard_map/results_2/ppermute | solution.py:542
  284.3 83.0 %collective-permute-start.17 = (bf16[4,1024,128]{2,1,0:T(8,128)(2,1)S(1)}, bf16[4,1024,128]{2,1,0:T(8,128)(2,1)}, u32[]{:S(2)}, u32[]{:S(2)}) collective-permute-start(bf16[4,1024,128]{2,1,0:T(8,128)(2,1)S(1)} %get-tuple-element.80), channel_id=1, source_target_pairs={{0,3},{1,0},{2,1},{3,2},{4,7},{5,4},{6,5},{7,6},{8,11},{9,8},{10,9... | collective-permute-start | bytes 3145736 | tf_op jit(solution)/shard_map/results_0/ppermute | solution.py:542
  286.5 78.0 %collective-permute-start.16 = (bf16[2,1024,128]{2,1,0:T(8,128)(2,1)}, bf16[2,1024,128]{2,1,0:T(8,128)(2,1)}, u32[]{:S(2)}, u32[]{:S(2)}) collective-permute-start(bf16[2,1024,128]{2,1,0:T(8,128)(2,1)} %copy-done.6), channel_id=1, source_target_pairs={{0,2},{1,3},{2,0},{3,1},{4,6},{5,7},{6,4},{7,5},{8,10},{9,11},{10,... | collective-permute-start | bytes 1572872 | tf_op jit(solution)/shard_map/results_2/ppermute | solution.py:542
  332.8 10.1 %collective-permute-start.15 = (bf16[480,128]{1,0:T(8,128)(2,1)}, bf16[480,128]{1,0:T(8,128)(2,1)S(1)}, u32[]{:S(2)}, u32[]{:S(2)}) collective-permute-start(bf16[480,128]{1,0:T(8,128)(2,1)} %get-tuple-element.151), channel_id=1, source_target_pairs={{0,3},{1,0},{2,1},{3,2},{4,7},{5,4},{6,5},{7,6},{8,11},{9,8},{10,9... | collective-permute-start | bytes 368648 | tf_op jit(solution)/shard_map/sums/ppermute | solution.py:542
  336.2 26.6 %collective-permute-start.14 = (bf16[480,128]{1,0:T(8,128)(2,1)}, bf16[480,128]{1,0:T(8,128)(2,1)S(1)}, u32[]{:S(2)}, u32[]{:S(2)}) collective-permute-start(bf16[480,128]{1,0:T(8,128)(2,1)} %get-tuple-element.152), channel_id=1, source_target_pairs={{0,2},{1,3},{2,0},{3,1},{4,6},{5,7},{6,4},{7,5},{8,10},{9,11},{10,... | collective-permute-start | bytes 368648 | tf_op jit(solution)/shard_map/sums/ppermute | solution.py:542
  336.2 26.6 %collective-permute-start.13 = (bf16[480,128]{1,0:T(8,128)(2,1)}, bf16[480,128]{1,0:T(8,128)(2,1)}, u32[]{:S(2)}, u32[]{:S(2)}) collective-permute-start(bf16[480,128]{1,0:T(8,128)(2,1)} %get-tuple-element.150), channel_id=1, source_target_pairs={{0,1},{1,2},{2,3},{3,0},{4,5},{5,6},{6,7},{7,4},{8,9},{9,10},{10,1... | collective-permute-start | bytes 368648 | tf_op jit(solution)/shard_map/sums/ppermute | solution.py:542
  364.6 10.2 %copy-start.12 = (bf16[4,1024,128]{2,1,0:T(8,128)(2,1)S(1)}, bf16[4,1024,128]{2,1,0:T(8,128)(2,1)}, u32[]{:S(2)}) copy-start(bf16[4,1024,128]{2,1,0:T(8,128)(2,1)} %copy-done.11) | copy-start | bytes 3145732
  364.6 32.3 %collective-permute-start.18 = (bf16[2,1024,128]{2,1,0:T(8,128)(2,1)S(1)}, bf16[2,1024,128]{2,1,0:T(8,128)(2,1)}, u32[]{:S(2)}, u32[]{:S(2)}) collective-permute-start(bf16[2,1024,128]{2,1,0:T(8,128)(2,1)S(1)} %copy-done.5), channel_id=1, source_target_pairs={{0,3},{1,0},{2,1},{3,2},{4,7},{5,4},{6,5},{7,6},{8,11},{9,8},{10,9... | collective-permute-start | bytes 1572872 | tf_op jit(solution)/shard_map/results_3/ppermute | solution.py:542
  364.7 46.5 %collective-permute-start.19 = (bf16[2,1024,128]{2,1,0:T(8,128)(2,1)S(1)}, bf16[2,1024,128]{2,1,0:T(8,128)(2,1)}, u32[]{:S(2)}, u32[]{:S(2)}) collective-permute-start(bf16[2,1024,128]{2,1,0:T(8,128)(2,1)S(1)} %get-tuple-element.84), channel_id=1, source_target_pairs={{0,2},{1,3},{2,0},{3,1},{4,6},{5,7},{6,4},{7,5},{8,10},{9,11},{10,... | collective-permute-start | bytes 1572872 | tf_op jit(solution)/shard_map/results_3/ppermute | solution.py:542
  365.4 47.7 %collective-permute-start.20 = (bf16[2,1024,128]{2,1,0:T(8,128)(2,1)S(1)}, bf16[2,1024,128]{2,1,0:T(8,128)(2,1)}, u32[]{:S(2)}, u32[]{:S(2)}) collective-permute-start(bf16[2,1024,128]{2,1,0:T(8,128)(2,1)S(1)} %get-tuple-element.85), channel_id=1, source_target_pairs={{0,1},{1,2},{2,3},{3,0},{4,5},{5,6},{6,7},{7,4},{8,9},{9,10},{10,1... | collective-permute-start | bytes 1572872 | tf_op jit(solution)/shard_map/results_3/ppermute | solution.py:542
  379.3 35.6 %copy-start.1 = (bf16[16,4,128]{2,1,0:T(4,128)(2,1)S(1)}, bf16[16,4,128]{2,1,0:T(4,128)(2,1)}, u32[]{:S(2)}) copy-start(bf16[16,4,128]{2,1,0:T(4,128)(2,1)} %param.13) | copy-start | bytes 49156
Sparse Core Ops, SparseCore 0:
  83.6 34.2 all-gather.2
  282.3 48.6 reduce-scatter.1
  364.7 25.3 all-gather.4

commit v4 on v3

--- a/solution.py
+++ b/solution.py
@@ -511,6 +511,54 @@
     )(z, i, frames, *weights)
 
 
+def bundle_kernel(n, per, names, z_ref, frames, cotangent, *refs):
+    outs, stage, sems = refs[: n - 1], refs[n - 1], refs[n]
+    frames_n = frames.shape[1]
+    count = itertools.count()
+
+    def copy(src, dst):
+        c = pltpu.make_async_copy(src, dst, sems.at[next(count)])
+        c.start()
+        return c
+
+    read = []
+    for k in range(1, n):
+        for i, (v, r) in enumerate(names):
+            src = (frames if v == "f" else cotangent).at[lax.rem(z_ref[0] + k, n) * per + r]
+            at = pl.ds(i * frames_n, frames_n)
+            read.append((k, at, copy(src, stage.at[k - 1, at, :])))
+    sent = []
+    for k, at, c in read:
+        c.wait()
+        sent.append(copy(stage.at[k - 1, at, :], outs[k - 1].at[at, :]))
+    for c in sent:
+        c.wait()
+
+
+def bundle_rows(n, per, names, z, frames, cotangent):
+    frames_n, width = frames.shape[1:]
+    size = len(names) * frames_n
+    any_space = pl.BlockSpec(memory_space=pl.ANY)
+    return pl.pallas_call(
+        functools.partial(bundle_kernel, n, per, names),
+        grid_spec=pltpu.PrefetchScalarGridSpec(
+            num_scalar_prefetch=1,
+            grid=(1,),
+            in_specs=[any_space] * 2,
+            out_specs=[any_space] * (n - 1),
+            scratch_shapes=[
+                pltpu.VMEM((n - 1, size, width), jnp.bfloat16),
+                pltpu.SemaphoreType.DMA((2 * (n - 1) * len(names),)),
+            ],
+        ),
+        out_shape=[jax.ShapeDtypeStruct((size, width), jnp.bfloat16)] * (n - 1),
+        compiler_params=pltpu.CompilerParams(vmem_limit_bytes=56 << 20),
+        cost_estimate=pl.CostEstimate(
+            flops=0, bytes_accessed=4 * (n - 1) * size * width, transcendentals=0
+        ),
+    )(z, frames, cotangent)
+
+
 def per_device(
     n,
     n_rows,
@@ -574,10 +622,7 @@
         return v.reshape(n, per, frames_n, width)[:, r]
 
     def bundle(*names):
-        return [
-            jnp.concatenate([piece({"f": frames, "c": cotangent}[v], k, r) for v, r in names])
-            for k in range(1, n)
-        ]
+        return bundle_rows(n, per, names, z[None], frames, cotangent)
 
     def fetch(what, pieces):
         return [send(v, k, what) for k, v in enumerate(pieces, 1)]

time: 422 us -> 417 us (0.988)
  other arithmetic: 15.9 us -> 5.61 us
  Pallas kernels: 124 us -> 130 us
    concatenate x5 -> x0, other arithmetic: 9.02 us -> none  [bundle(): jnp.concatenate([piece({'f': frames, 'c': cotangent}[v], k, r) for v, r i...]
    pallas_call x0 -> x2, Pallas kernels: none -> 5.75 us  [bundle_rows(): pl.pallas_call(functools.partial(bundle_kernel, n, per, names), grid_spec...]
    squeeze x2 -> x0, local copies, waits for them, and re-layouts: 4.32 us -> none  [piece(): return lax.dynamic_slice_in_dim(v, at, 1, 0)[0]]
    ppermute x21, waiting for transfers between devices: 168 us -> 172 us  [send(): return lax.ppermute(v, 'ch', shift(k))]
  transfers between devices with their start and end apart: 24 -> 24, of which waited for: 13 -> 13; matrix products, arithmetic and copies ran while one was open for 11% -> 8% of each run, Pallas kernels for 29% -> 31%
where the time goes in v4:
time: 417 us; the launch traced here: 416 us
  waiting for transfers between devices  200 us (48%)
  Pallas kernels  130 us (31%)
  local copies, waits for them, and re-layouts  37.5 us (9%)
  starting transfers between devices  29 us (7%)
  between operations  14 us (3%)
  other arithmetic  5.61 us (1%)
    ppermute x21, waiting for transfers between devices, send(): return lax.ppermute(v, 'ch', shift(k))  172 us
    pallas_call x2, Pallas kernels, block_rows(): pl.pallas_call(functools.partial(rows_kernel, n, segs, style_n, per, firs...  122 us
    ppermute x21, starting transfers between devices, send(): return lax.ppermute(v, 'ch', shift(k))  28.8 us
    reduce_scatter x1, waiting for transfers between devices, per_device(): sums = lax.psum_scatter(sums, 'rows', scatter_dimension=0, tiled=True)  21.3 us
    dynamic_update_slice x12, local copies, waits for them, and re-layouts, per_device(): lax.dynamic_update_slice(results[which], v[None, None, 2 * at + which], (...  21.3 us
  transfers between devices with their start and end apart: 24, of which 13 were waited for; matrix products, arithmetic and copies ran while one was open for 8% of the time, Pallas kernels for 31%

profile of v4, /device:TPU:0, one launch (start us, length us, event | category | flops | bytes accessed | tf_op | source)
XLA Modules:
  0.0 416.0 jit_solution(6337711231367316152)
XLA Ops:
  7.3 1.4 maximum_maximum_fusion.biases
  8.7 2.3 shard_map.195
  11.0 3.1 collective-permute-start
  14.1 2.6 collective-permute-start.1
  16.7 1.3 collective-permute-start.2
  18.1 2.5 shard_map.196
  20.6 0.3 collective-permute-start.3
  20.9 5.3 %collective-permute-done.refs_5_ = bf16[1488,128]{1,0:T(8,128)(2,1)S(1)} collective-permute-done((bf16[1488,128]{1,0:T(8,128)(2,1)}, bf16[1488,128]{1,0:T(8,128)(2,1)S(1)}, u32[]{:S(2)}, u32[]{:S(2)}) %collective-permute-start) | collective-permute-done | bytes 380960 | tf_op jit(solution)/shard_map/frames_0/ppermute | solution.py:590
  26.2 16.3 %collective-permute-done.1.refs_6_ = bf16[1488,128]{1,0:T(8,128)(2,1)S(1)} collective-permute-done((bf16[1488,128]{1,0:T(8,128)(2,1)}, bf16[1488,128]{1,0:T(8,128)(2,1)S(1)}, u32[]{:S(2)}, u32[]{:S(2)}) %collective-permute-start.1) | collective-permute-done | bytes 380960 | tf_op jit(solution)/shard_map/frames_0/ppermute | solution.py:590
  42.6 40.8 %collective-permute-done.3.refs_9_ = bf16[3072,128]{1,0:T(8,128)(2,1)S(1)} collective-permute-done((bf16[3072,128]{1,0:T(8,128)(2,1)}, bf16[3072,128]{1,0:T(8,128)(2,1)S(1)}, u32[]{:S(2)}, u32[]{:S(2)}) %collective-permute-start.3) | collective-permute-done | bytes 786464 | tf_op jit(solution)/shard_map/inputs_1/ppermute | solution.py:590
  83.4 0.9 copy-done.1
  84.5 3.8 collective-permute-start.8
  88.3 0.9 fusion.24
  89.3 0.2 select_reduce_fusion
  89.6 3.3 shard_map.197
  93.1 3.7 collective-permute-start.6
  96.8 10.1 %collective-permute-done.7.refs_8_ = bf16[3072,128]{1,0:T(8,128)(2,1)S(1)} collective-permute-done((bf16[3072,128]{1,0:T(8,128)(2,1)}, bf16[3072,128]{1,0:T(8,128)(2,1)S(1)}, u32[]{:S(2)}, u32[]{:S(2)}) %collective-permute-start.7) | collective-permute-done | bytes 786464 | tf_op jit(solution)/shard_map/inputs_1/ppermute | solution.py:590
  106.9 0.9 copy-done.3
  107.8 39.3 %collective-permute-done.8.refs_10_ = bf16[3072,128]{1,0:T(8,128)(2,1)} collective-permute-done((bf16[3072,128]{1,0:T(8,128)(2,1)}, bf16[3072,128]{1,0:T(8,128)(2,1)}, u32[]{:S(2)}, u32[]{:S(2)}) %collective-permute-start.8) | collective-permute-done | bytes 786464 | tf_op jit(solution)/shard_map/inputs_1/ppermute | solution.py:590
  147.2 1.1 copy-done.2
  148.3 1.1 copy-done.4
  149.5 60.6 %shard_map.198 = (f32[3712,512]{1,0:T(8,128)}, f32[2,4,128]{2,1,0:T(4,128)S(1)}, bf16[16,1024,128]{2,1,0:T(8,128)(2,1)}, bf16[16,1024,128]{2,1,0:T(8,128)(2,1)},...) custom-call(s32[1]{0:T(128)} %bitcast.z_ref, ...), custom_call_target="tpu_custom_call" | custom-call | flops 9663676416 | bytes 1000000 | tf_op jit(solution)/shard_map/pallas_call | solution.py:431
  210.1 0.9 collective-permute-start.9
  211.0 1.1 collective-permute-start.10
  212.1 61.2 %shard_map.199 = (bf16[3712,512]{1,0:T(8,128)(2,1)}, f32[2,4,128]{2,1,0:T(4,128)S(1)}, bf16[16,1024,128]{2,1,0:T(8,128)(2,1)}, bf16[16,1024,128]{2,1,0:T(8,128)(...) custom-call(s32[1]{0:T(128)} %bitcast.z_ref, ...), custom_call_target="tpu_custom_call", output_to_operand_aliasing={{2}: (12, {}), {3}: (13, {})} | custom-call | flops 9663676416 | bytes 1000000 | tf_op jit(solution)/shard_map/pallas_call | solution.py:431
  273.3 0.8 copy-done.5
  274.1 0.8 copy-done.7
  274.9 0.8 copy-done.8
  275.7 0.8 copy-done.9
  276.5 1.3 collective-permute-done.9
  277.9 1.5 collective-permute-start.11
  279.4 0.6 collective-permute-start.12
  280.0 3.2 collective-permute-start.17
  283.2 10.9 %collective-permute-done.11 = bf16[2,1024,128]{2,1,0:T(8,128)(2,1)} collective-permute-done((bf16[2,1024,128]{2,1,0:T(8,128)(2,1)}, bf16[2,1024,128]{2,1,0:T(8,128)(2,1)}, u32[]{:S(2)}, u32[]{:S(2)}) %collective-permute-start.11) | collective-permute-done | bytes 524320 | tf_op jit(solution)/shard_map/results_2/ppermute | solution.py:590
  294.1 11.1 %collective-permute-done.12 = bf16[2,1024,128]{2,1,0:T(8,128)(2,1)S(1)} collective-permute-done((bf16[2,1024,128]{2,1,0:T(8,128)(2,1)}, bf16[2,1024,128]{2,1,0:T(8,128)(2,1)S(1)}, u32[]{:S(2)}, u32[]{:S(2)}) %collective-permute-start.12) | collective-permute-done | bytes 524320 | tf_op jit(solution)/shard_map/results_2/ppermute | solution.py:590
  305.2 21.3 %reduce-scatter.2.cloned.1.call-done = bf16[464,512]{1,0:T(8,128)(2,1)} async-done(((bf16[3712,512]{1,0:T(8,128)(2,1)}), bf16[464,512]{1,0:T(8,128)(2,1)}) %reduce-scatter.2.cloned.1.call-update) | async-done | bytes 475152 | tf_op jit(solution)/shard_map/reduce_scatter | solution.py:685
  326.5 1.0 constant_dynamic-slice_fusion.2
  327.6 0.7 pad_maximum_fusion.3
  328.3 3.3 collective-permute-start.15
  331.7 1.1 collective-permute-start.13
  332.8 3.7 collective-permute-done.15
  336.5 22.0 %collective-permute-done.14 = bf16[480,128]{1,0:T(8,128)(2,1)S(1)} collective-permute-done((bf16[480,128]{1,0:T(8,128)(2,1)}, bf16[480,128]{1,0:T(8,128)(2,1)S(1)}, u32[]{:S(2)}, u32[]{:S(2)}) %collective-permute-start.14) | collective-permute-done | bytes 122912 | tf_op jit(solution)/shard_map/sums/ppermute | solution.py:590
  358.5 1.7 convert_add_fusion
  360.5 1.9 collective-permute-start.20
  362.4 1.9 fusion.14
  364.2 1.9 fusion.13
  366.1 1.9 fusion.12
  368.0 1.9 fusion.11
  369.8 1.9 fusion.10
  371.7 1.9 fusion.9
  373.5 1.9 fusion.8
  375.4 1.9 fusion.7
  377.2 0.8 fusion.6
  378.1 0.7 constant_dynamic-update-slice_fusion.2
  378.8 0.6 convert.9
  379.4 6.3 %all-gather.5.cloned.1.call-done = f32[3712,128]{1,0:T(8,128)} async-done(((f32[464,128]{1,0:T(8,128)}), f32[3712,128]{1,0:T(8,128)}) %all-gather.5.cloned.1.call-update) | async-done | bytes 1900560 | tf_op jit(solution)/shard_map/all_gather | solution.py:701
  385.7 2.6 fusion.25
  388.3 1.7 fusion.27
  389.9 1.3 fusion.26
  391.3 1.2 slice_bitcast_fusion.24
  392.5 1.9 fusion.2
  394.3 11.4 %collective-permute-done.19 = bf16[2,1024,128]{2,1,0:T(8,128)(2,1)} collective-permute-done((bf16[2,1024,128]{2,1,0:T(8,128)(2,1)S(1)}, bf16[2,1024,128]{2,1,0:T(8,128)(2,1)}, u32[]{:S(2)}, u32[]{:S(2)}) %collective-permute-start.19) | collective-permute-done | bytes 524320 | tf_op jit(solution)/shard_map/results_3/ppermute | solution.py:590
  405.7 1.9 fusion.1
  407.6 1.9 fusion
  (60 shorter events, 1.3 us)
Async XLA Ops:
  7.2 89.6 %copy-start = (bf16[16,4,128]{2,1,0:T(4,128)(2,1)S(1)}, bf16[16,4,128]{2,1,0:T(4,128)(2,1)}, u32[]{:S(2)}) copy-start(bf16[16,4,128]{2,1,0:T(4,128)(2,1)} %param.13) | copy-start | bytes 49156
  7.2 139.9 %all-gather.3.cloned.1.call-start = ((), (), s32[]{:S(2)}) async-start(), calls=%async_computation.1 | async-start | bytes 4276224 | tf_op jit(solution)/shard_map/all_gather | solution.py:638
  11.0 15.1 %collective-permute-start = (bf16[1488,128]{1,0:T(8,128)(2,1)}, bf16[1488,128]{1,0:T(8,128)(2,1)S(1)}, u32[]{:S(2)}, u32[]{:S(2)}) collective-permute-start(bf16[1488,128]{1,0:T(8,128)(2,1)} %get-tuple-element.59), channel_id=1, source_target_pairs={{0,1},{1,2},{2,3},{3,0},{4,5},{5,6},{6,7},{7,4},{8,9},{9,10},{10,1... | collective-permute-start | bytes 1142792 | tf_op jit(solution)/shard_map/frames_0/ppermute | solution.py:590
  14.1 28.4 %collective-permute-start.1 = (bf16[1488,128]{1,0:T(8,128)(2,1)}, bf16[1488,128]{1,0:T(8,128)(2,1)S(1)}, u32[]{:S(2)}, u32[]{:S(2)}) collective-permute-start(bf16[1488,128]{1,0:T(8,128)(2,1)} %get-tuple-element.60), channel_id=1, source_target_pairs={{0,2},{1,3},{2,0},{3,1},{4,6},{5,7},{6,4},{7,5},{8,10},{9,11},{10,... | collective-permute-start | bytes 1142792 | tf_op jit(solution)/shard_map/frames_0/ppermute | solution.py:590
  16.7 4.1 copy-start.11
  16.7 25.8 %collective-permute-start.2 = (bf16[1488,128]{1,0:T(8,128)(2,1)}, bf16[1488,128]{1,0:T(8,128)(2,1)S(1)}, u32[]{:S(2)}, u32[]{:S(2)}) collective-permute-start(bf16[1488,128]{1,0:T(8,128)(2,1)} %get-tuple-element.61), channel_id=1, source_target_pairs={{0,3},{1,0},{2,1},{3,2},{4,7},{5,4},{6,5},{7,6},{8,11},{9,8},{10,9... | collective-permute-start | bytes 1142792 | tf_op jit(solution)/shard_map/frames_0/ppermute | solution.py:590
  20.6 62.9 %collective-permute-start.3 = (bf16[3072,128]{1,0:T(8,128)(2,1)}, bf16[3072,128]{1,0:T(8,128)(2,1)S(1)}, u32[]{:S(2)}, u32[]{:S(2)}) collective-permute-start(bf16[3072,128]{1,0:T(8,128)(2,1)} %get-tuple-element.62), channel_id=1, source_target_pairs={{0,2},{1,3},{2,0},{3,1},{4,6},{5,7},{6,4},{7,5},{8,10},{9,11},{10,... | collective-permute-start | bytes 2359304 | tf_op jit(solution)/shard_map/inputs_1/ppermute | solution.py:590
  42.6 41.7 %copy-start.10 = (bf16[464,512]{1,0:T(8,128)(2,1)}, bf16[464,512]{1,0:T(8,128)(2,1)S(1)}, u32[]{:S(2)}) copy-start(bf16[464,512]{1,0:T(8,128)(2,1)S(1)} %slice_dynamic-update-slice_fusion) | copy-start | bytes 1425412
  83.4 0.9 copy-start.1
  84.3 242.2 %reduce-scatter.2.cloned.1.call-start = ((), (), s32[]{:S(2)}) async-start(), calls=%async_computation.2 | async-start | bytes 4276224 | tf_op jit(solution)/shard_map/reduce_scatter | solution.py:685
  84.4 22.5 %collective-permute-start.7 = (bf16[3072,128]{1,0:T(8,128)(2,1)}, bf16[3072,128]{1,0:T(8,128)(2,1)S(1)}, u32[]{:S(2)}, u32[]{:S(2)}) collective-permute-start(bf16[3072,128]{1,0:T(8,128)(2,1)} %get-tuple-element.70), channel_id=1, source_target_pairs={{0,1},{1,2},{2,3},{3,0},{4,5},{5,6},{6,7},{7,4},{8,9},{9,10},{10,1... | collective-permute-start | bytes 2359304 | tf_op jit(solution)/shard_map/inputs_1/ppermute | solution.py:590
  84.5 62.7 %collective-permute-start.8 = (bf16[3072,128]{1,0:T(8,128)(2,1)}, bf16[3072,128]{1,0:T(8,128)(2,1)}, u32[]{:S(2)}, u32[]{:S(2)}) collective-permute-start(bf16[3072,128]{1,0:T(8,128)(2,1)} %get-tuple-element.71), channel_id=1, source_target_pairs={{0,3},{1,0},{2,1},{3,2},{4,7},{5,4},{6,5},{7,6},{8,11},{9,8},{10,9... | collective-permute-start | bytes 2359304 | tf_op jit(solution)/shard_map/inputs_1/ppermute | solution.py:590
  92.9 117.2 %collective-permute-start.4 = (bf16[4096,128]{1,0:T(8,128)(2,1)}, bf16[4096,128]{1,0:T(8,128)(2,1)S(1)}, u32[]{:S(2)}, u32[]{:S(2)}) collective-permute-start(bf16[4096,128]{1,0:T(8,128)(2,1)} %get-tuple-element.67), channel_id=1, source_target_pairs={{0,1},{1,2},{2,3},{3,0},{4,5},{5,6},{6,7},{7,4},{8,9},{9,10},{10,1... | collective-permute-start | bytes 3145736 | tf_op jit(solution)/shard_map/inputs_2/ppermute | solution.py:590
  92.9 117.1 %collective-permute-start.5 = (bf16[4096,128]{1,0:T(8,128)(2,1)}, bf16[4096,128]{1,0:T(8,128)(2,1)}, u32[]{:S(2)}, u32[]{:S(2)}) collective-permute-start(bf16[4096,128]{1,0:T(8,128)(2,1)} %get-tuple-element.68), channel_id=1, source_target_pairs={{0,2},{1,3},{2,0},{3,1},{4,6},{5,7},{6,4},{7,5},{8,10},{9,11},{10,... | collective-permute-start | bytes 3145736 | tf_op jit(solution)/shard_map/inputs_2/ppermute | solution.py:590
  93.1 117.0 %collective-permute-start.6 = (bf16[4096,128]{1,0:T(8,128)(2,1)}, bf16[4096,128]{1,0:T(8,128)(2,1)}, u32[]{:S(2)}, u32[]{:S(2)}) collective-permute-start(bf16[4096,128]{1,0:T(8,128)(2,1)} %get-tuple-element.69), channel_id=1, source_target_pairs={{0,3},{1,0},{2,1},{3,2},{4,7},{5,4},{6,5},{7,6},{8,11},{9,8},{10,9... | collective-permute-start | bytes 3145736 | tf_op jit(solution)/shard_map/inputs_2/ppermute | solution.py:590
  106.9 0.9 copy-start.3
  147.2 1.1 copy-start.2
  148.3 1.1 copy-start.4
  210.1 67.7 %collective-permute-start.9 = (bf16[4,1024,128]{2,1,0:T(8,128)(2,1)S(1)}, bf16[4,1024,128]{2,1,0:T(8,128)(2,1)}, u32[]{:S(2)}, u32[]{:S(2)}) collective-permute-start(bf16[4,1024,128]{2,1,0:T(8,128)(2,1)S(1)} %get-tuple-element.79), channel_id=1, source_target_pairs={{0,2},{1,3},{2,0},{3,1},{4,6},{5,7},{6,4},{7,5},{8,10},{9,11},{10,... | collective-permute-start | bytes 3145736 | tf_op jit(solution)/shard_map/results_0/ppermute | solution.py:590
  211.0 66.8 %collective-permute-start.10 = (bf16[4,1024,128]{2,1,0:T(8,128)(2,1)}, bf16[4,1024,128]{2,1,0:T(8,128)(2,1)}, u32[]{:S(2)}, u32[]{:S(2)}) collective-permute-start(bf16[4,1024,128]{2,1,0:T(8,128)(2,1)} %get-tuple-element.80), channel_id=1, source_target_pairs={{0,1},{1,2},{2,3},{3,0},{4,5},{5,6},{6,7},{7,4},{8,9},{9,10},{10,1... | collective-permute-start | bytes 3145736 | tf_op jit(solution)/shard_map/results_0/ppermute | solution.py:590
  273.3 0.8 copy-start.5
  274.1 0.8 copy-start.7
  274.9 0.8 copy-start.8
  275.7 0.8 copy-start.9
  277.8 82.5 %copy-start.6 = (bf16[2,1024,128]{2,1,0:T(8,128)(2,1)S(1)}, bf16[2,1024,128]{2,1,0:T(8,128)(2,1)}, u32[]{:S(2)}) copy-start(bf16[2,1024,128]{2,1,0:T(8,128)(2,1)} %copy-done.5) | copy-start | bytes 1572868
  277.8 107.8 %all-gather.5.cloned.1.call-start = ((), (), s32[]{:S(2)}) async-start(), calls=%async_computation.3 | async-start | bytes 2138112 | tf_op jit(solution)/shard_map/all_gather | solution.py:701
  277.9 16.2 %collective-permute-start.11 = (bf16[2,1024,128]{2,1,0:T(8,128)(2,1)}, bf16[2,1024,128]{2,1,0:T(8,128)(2,1)}, u32[]{:S(2)}, u32[]{:S(2)}) collective-permute-start(bf16[2,1024,128]{2,1,0:T(8,128)(2,1)} %copy-done.9), channel_id=1, source_target_pairs={{0,3},{1,0},{2,1},{3,2},{4,7},{5,4},{6,5},{7,6},{8,11},{9,8},{10,9... | collective-permute-start | bytes 1572872 | tf_op jit(solution)/shard_map/results_2/ppermute | solution.py:590
  279.4 25.8 %collective-permute-start.12 = (bf16[2,1024,128]{2,1,0:T(8,128)(2,1)}, bf16[2,1024,128]{2,1,0:T(8,128)(2,1)S(1)}, u32[]{:S(2)}, u32[]{:S(2)}) collective-permute-start(bf16[2,1024,128]{2,1,0:T(8,128)(2,1)} %copy-done.8), channel_id=1, source_target_pairs={{0,1},{1,2},{2,3},{3,0},{4,5},{5,6},{6,7},{7,4},{8,9},{9,10},{10,1... | collective-permute-start | bytes 1572872 | tf_op jit(solution)/shard_map/results_2/ppermute | solution.py:590
  280.0 82.4 %collective-permute-start.17 = (bf16[4,1024,128]{2,1,0:T(8,128)(2,1)S(1)}, bf16[4,1024,128]{2,1,0:T(8,128)(2,1)}, u32[]{:S(2)}, u32[]{:S(2)}) collective-permute-start(bf16[4,1024,128]{2,1,0:T(8,128)(2,1)S(1)} %get-tuple-element.92), channel_id=1, source_target_pairs={{0,3},{1,0},{2,1},{3,2},{4,7},{5,4},{6,5},{7,6},{8,11},{9,8},{10,9... | collective-permute-start | bytes 3145736 | tf_op jit(solution)/shard_map/results_0/ppermute | solution.py:590
  283.2 77.0 %collective-permute-start.16 = (bf16[2,1024,128]{2,1,0:T(8,128)(2,1)}, bf16[2,1024,128]{2,1,0:T(8,128)(2,1)}, u32[]{:S(2)}, u32[]{:S(2)}) collective-permute-start(bf16[2,1024,128]{2,1,0:T(8,128)(2,1)} %copy-done.7), channel_id=1, source_target_pairs={{0,2},{1,3},{2,0},{3,1},{4,6},{5,7},{6,4},{7,5},{8,10},{9,11},{10,... | collective-permute-start | bytes 1572872 | tf_op jit(solution)/shard_map/results_2/ppermute | solution.py:590
  328.3 8.2 %collective-permute-start.15 = (bf16[480,128]{1,0:T(8,128)(2,1)}, bf16[480,128]{1,0:T(8,128)(2,1)S(1)}, u32[]{:S(2)}, u32[]{:S(2)}) collective-permute-start(bf16[480,128]{1,0:T(8,128)(2,1)} %get-tuple-element.142), channel_id=1, source_target_pairs={{0,3},{1,0},{2,1},{3,2},{4,7},{5,4},{6,5},{7,6},{8,11},{9,8},{10,9... | collective-permute-start | bytes 368648 | tf_op jit(solution)/shard_map/sums/ppermute | solution.py:590
  331.6 26.8 %collective-permute-start.14 = (bf16[480,128]{1,0:T(8,128)(2,1)}, bf16[480,128]{1,0:T(8,128)(2,1)S(1)}, u32[]{:S(2)}, u32[]{:S(2)}) collective-permute-start(bf16[480,128]{1,0:T(8,128)(2,1)} %get-tuple-element.143), channel_id=1, source_target_pairs={{0,2},{1,3},{2,0},{3,1},{4,6},{5,7},{6,4},{7,5},{8,10},{9,11},{10,... | collective-permute-start | bytes 368648 | tf_op jit(solution)/shard_map/sums/ppermute | solution.py:590
  331.7 26.8 %collective-permute-start.13 = (bf16[480,128]{1,0:T(8,128)(2,1)}, bf16[480,128]{1,0:T(8,128)(2,1)}, u32[]{:S(2)}, u32[]{:S(2)}) collective-permute-start(bf16[480,128]{1,0:T(8,128)(2,1)} %get-tuple-element.141), channel_id=1, source_target_pairs={{0,1},{1,2},{2,3},{3,0},{4,5},{5,6},{6,7},{7,4},{8,9},{9,10},{10,1... | collective-permute-start | bytes 368648 | tf_op jit(solution)/shard_map/sums/ppermute | solution.py:590
  360.3 32.2 %collective-permute-start.18 = (bf16[2,1024,128]{2,1,0:T(8,128)(2,1)S(1)}, bf16[2,1024,128]{2,1,0:T(8,128)(2,1)}, u32[]{:S(2)}, u32[]{:S(2)}) collective-permute-start(bf16[2,1024,128]{2,1,0:T(8,128)(2,1)S(1)} %copy-done.6), channel_id=1, source_target_pairs={{0,3},{1,0},{2,1},{3,2},{4,7},{5,4},{6,5},{7,6},{8,11},{9,8},{10,9... | collective-permute-start | bytes 1572872 | tf_op jit(solution)/shard_map/results_3/ppermute | solution.py:590
  360.3 45.4 %collective-permute-start.19 = (bf16[2,1024,128]{2,1,0:T(8,128)(2,1)S(1)}, bf16[2,1024,128]{2,1,0:T(8,128)(2,1)}, u32[]{:S(2)}, u32[]{:S(2)}) collective-permute-start(bf16[2,1024,128]{2,1,0:T(8,128)(2,1)S(1)} %get-tuple-element.96), channel_id=1, source_target_pairs={{0,2},{1,3},{2,0},{3,1},{4,6},{5,7},{6,4},{7,5},{8,10},{9,11},{10,... | collective-permute-start | bytes 1572872 | tf_op jit(solution)/shard_map/results_3/ppermute | solution.py:590
  360.5 47.1 %collective-permute-start.20 = (bf16[2,1024,128]{2,1,0:T(8,128)(2,1)S(1)}, bf16[2,1024,128]{2,1,0:T(8,128)(2,1)}, u32[]{:S(2)}, u32[]{:S(2)}) collective-permute-start(bf16[2,1024,128]{2,1,0:T(8,128)(2,1)S(1)} %get-tuple-element.97), channel_id=1, source_target_pairs={{0,1},{1,2},{2,3},{3,0},{4,5},{5,6},{6,7},{7,4},{8,9},{9,10},{10,1... | collective-permute-start | bytes 1572872 | tf_op jit(solution)/shard_map/results_3/ppermute | solution.py:590
Sparse Core Ops, SparseCore 0:
  84.5 34.2 all-gather.2
  277.9 48.5 reduce-scatter.1
  360.3 25.2 all-gather.4

commit v5 on v4

--- a/solution.py
+++ b/solution.py
@@ -559,6 +559,48 @@
     )(z, frames, cotangent)
 
 
+def place_kernel(n, row, z_ref, *refs):
+    pieces, refs = refs[: n - 1], refs[n - 1 :]
+    results, stage, sems = refs[2:4], refs[4], refs[5]
+    read = [
+        pltpu.make_async_copy(ref, stage.at[k], sems.at[0, k]) for k, ref in enumerate(pieces)
+    ]
+    for c in read:
+        c.start()
+    sent = []
+    for k, c in enumerate(read):
+        c.wait()
+        for which in range(2):
+            dst = results[which].at[lax.rem(z_ref[0] + k + 1, n), row]
+            sent.append(pltpu.make_async_copy(stage.at[k, which], dst, sems.at[1 + which, k]))
+            sent[-1].start()
+    for c in sent:
+        c.wait()
+
+
+def place(n, row, z, pieces, results):
+    any_space = pl.BlockSpec(memory_space=pl.ANY)
+    return pl.pallas_call(
+        functools.partial(place_kernel, n, row),
+        grid_spec=pltpu.PrefetchScalarGridSpec(
+            num_scalar_prefetch=1,
+            grid=(1,),
+            in_specs=[any_space] * (n + 1),
+            out_specs=[any_space] * 2,
+            scratch_shapes=[
+                pltpu.VMEM((n - 1,) + pieces[0].shape, jnp.bfloat16),
+                pltpu.SemaphoreType.DMA((3, n - 1)),
+            ],
+        ),
+        out_shape=[jax.ShapeDtypeStruct(v.shape, v.dtype) for v in results],
+        input_output_aliases={n: 0, n + 1: 1},
+        compiler_params=pltpu.CompilerParams(vmem_limit_bytes=56 << 20),
+        cost_estimate=pl.CostEstimate(
+            flops=0, bytes_accessed=4 * (n - 1) * pieces[0].size, transcendentals=0
+        ),
+    )(z, *pieces, *results)
+
+
 def per_device(
     n,
     n_rows,
@@ -717,6 +759,8 @@
     for r in range(per):
         if r == per - 1:
             grads, results = lax.optimization_barrier((grads, results))
+            results = place(n, r, z[None], back[-1], results)
+            break
         group, at = (0, r) if r < half else (r - half + 1, 0)
         for which in range(2):
             for k, v in enumerate(back[group], 1):

time: 417 us -> 416 us (level)
  local copies, waits for them, and re-layouts: 37.5 us -> 32.7 us
    dynamic_update_slice x12 -> x9, local copies, waits for them, and re-layouts: 21.3 us -> 15.7 us  [per_device(): lax.dynamic_update_slice(results[which], v[None, None, 2 * at + which], (...]
  transfers between devices with their start and end apart: 24 -> 24, of which waited for: 13 -> 13; matrix products, arithmetic and copies ran while one was open for 8% -> 7% of each run, Pallas kernels for 31% -> 31%
where the time goes in v5:
time: 416 us; the launch traced here: 415 us
  waiting for transfers between devices  202 us (49%)
  Pallas kernels  132 us (32%)
  local copies, waits for them, and re-layouts  32.7 us (8%)
  starting transfers between devices  28.9 us (7%)
  between operations  14 us (3%)
  other arithmetic  5.63 us (1%)
    ppermute x21, waiting for transfers between devices, send(): return lax.ppermute(v, 'ch', shift(k))  175 us
    pallas_call x2, Pallas kernels, block_rows(): pl.pallas_call(functools.partial(rows_kernel, n, segs, style_n, per, firs...  122 us
    ppermute x21, starting transfers between devices, send(): return lax.ppermute(v, 'ch', shift(k))  28.8 us
    reduce_scatter x1, waiting for transfers between devices, per_device(): sums = lax.psum_scatter(sums, 'rows', scatter_dimension=0, tiled=True)  21.2 us
    dynamic_update_slice x9, local copies, waits for them, and re-layouts, per_device(): lax.dynamic_update_slice(results[which], v[None, None, 2 * at + which], (...  15.7 us
  transfers between devices with their start and end apart: 24, of which 13 were waited for; matrix products, arithmetic and copies ran while one was open for 7% of the time, Pallas kernels for 31%

profile of v5, /device:TPU:0, one launch (start us, length us, event | category | flops | bytes accessed | tf_op | source)
XLA Modules:
  0.0 415.2 jit_solution(17989782927899625507)
XLA Ops:
  7.3 1.4 maximum_maximum_fusion.biases
  8.7 2.4 shard_map.195
  11.1 3.1 collective-permute-start
  14.1 2.6 collective-permute-start.1
  16.7 1.3 collective-permute-start.2
  18.1 2.5 shard_map.196
  20.6 0.3 collective-permute-start.3
  20.9 5.3 %collective-permute-done.refs_5_ = bf16[1488,128]{1,0:T(8,128)(2,1)S(1)} collective-permute-done((bf16[1488,128]{1,0:T(8,128)(2,1)}, bf16[1488,128]{1,0:T(8,128)(2,1)S(1)}, u32[]{:S(2)}, u32[]{:S(2)}) %collective-permute-start) | collective-permute-done | bytes 380960 | tf_op jit(solution)/shard_map/frames_0/ppermute | solution.py:632
  26.2 16.3 %collective-permute-done.1.refs_6_ = bf16[1488,128]{1,0:T(8,128)(2,1)S(1)} collective-permute-done((bf16[1488,128]{1,0:T(8,128)(2,1)}, bf16[1488,128]{1,0:T(8,128)(2,1)S(1)}, u32[]{:S(2)}, u32[]{:S(2)}) %collective-permute-start.1) | collective-permute-done | bytes 380960 | tf_op jit(solution)/shard_map/frames_0/ppermute | solution.py:632
  42.6 40.8 %collective-permute-done.3.refs_9_ = bf16[3072,128]{1,0:T(8,128)(2,1)S(1)} collective-permute-done((bf16[3072,128]{1,0:T(8,128)(2,1)}, bf16[3072,128]{1,0:T(8,128)(2,1)S(1)}, u32[]{:S(2)}, u32[]{:S(2)}) %collective-permute-start.3) | collective-permute-done | bytes 786464 | tf_op jit(solution)/shard_map/inputs_1/ppermute | solution.py:632
  83.5 0.9 copy-done.1
  84.5 3.8 collective-permute-start.8
  88.3 0.9 fusion.18
  89.3 0.2 select_reduce_fusion
  89.6 3.3 shard_map.197
  93.1 3.7 collective-permute-start.6
  96.8 10.1 %collective-permute-done.7.refs_8_ = bf16[3072,128]{1,0:T(8,128)(2,1)S(1)} collective-permute-done((bf16[3072,128]{1,0:T(8,128)(2,1)}, bf16[3072,128]{1,0:T(8,128)(2,1)S(1)}, u32[]{:S(2)}, u32[]{:S(2)}) %collective-permute-start.7) | collective-permute-done | bytes 786464 | tf_op jit(solution)/shard_map/inputs_1/ppermute | solution.py:632
  106.9 0.9 copy-done.3
  107.8 39.3 %collective-permute-done.8.refs_10_ = bf16[3072,128]{1,0:T(8,128)(2,1)} collective-permute-done((bf16[3072,128]{1,0:T(8,128)(2,1)}, bf16[3072,128]{1,0:T(8,128)(2,1)}, u32[]{:S(2)}, u32[]{:S(2)}) %collective-permute-start.8) | collective-permute-done | bytes 786464 | tf_op jit(solution)/shard_map/inputs_1/ppermute | solution.py:632
  147.2 1.1 copy-done.2
  148.4 1.1 copy-done.4
  149.5 60.6 %shard_map.198 = (f32[3712,512]{1,0:T(8,128)}, f32[2,4,128]{2,1,0:T(4,128)S(1)}, bf16[16,1024,128]{2,1,0:T(8,128)(2,1)}, bf16[16,1024,128]{2,1,0:T(8,128)(2,1)},...) custom-call(s32[1]{0:T(128)} %bitcast.z_ref, ...), custom_call_target="tpu_custom_call" | custom-call | flops 9663676416 | bytes 1000000 | tf_op jit(solution)/shard_map/pallas_call | solution.py:431
  210.1 1.0 collective-permute-start.12
  211.0 1.1 collective-permute-start.13
  212.1 61.2 %shard_map.199 = (bf16[3712,512]{1,0:T(8,128)(2,1)}, f32[2,4,128]{2,1,0:T(4,128)S(1)}, bf16[16,1024,128]{2,1,0:T(8,128)(2,1)}, bf16[16,1024,128]{2,1,0:T(8,128)(...) custom-call(s32[1]{0:T(128)} %bitcast.z_ref, ...), custom_call_target="tpu_custom_call", output_to_operand_aliasing={{2}: (12, {}), {3}: (13, {})} | custom-call | flops 9663676416 | bytes 1000000 | tf_op jit(solution)/shard_map/pallas_call | solution.py:431
  273.3 0.8 copy-done.5
  274.1 0.8 copy-done.7
  274.9 0.8 copy-done.8
  275.7 0.8 copy-done.9
  276.5 1.3 collective-permute-done.12
  277.9 1.5 collective-permute-start.14
  279.4 0.6 collective-permute-start.15
  280.0 3.2 collective-permute-start.20
  283.2 10.9 %collective-permute-done.14 = bf16[2,1024,128]{2,1,0:T(8,128)(2,1)} collective-permute-done((bf16[2,1024,128]{2,1,0:T(8,128)(2,1)}, bf16[2,1024,128]{2,1,0:T(8,128)(2,1)}, u32[]{:S(2)}, u32[]{:S(2)}) %collective-permute-start.14) | collective-permute-done | bytes 524320 | tf_op jit(solution)/shard_map/results_2/ppermute | solution.py:632
  294.1 11.2 %collective-permute-done.15 = bf16[2,1024,128]{2,1,0:T(8,128)(2,1)} collective-permute-done((bf16[2,1024,128]{2,1,0:T(8,128)(2,1)}, bf16[2,1024,128]{2,1,0:T(8,128)(2,1)}, u32[]{:S(2)}, u32[]{:S(2)}) %collective-permute-start.15) | collective-permute-done | bytes 524320 | tf_op jit(solution)/shard_map/results_2/ppermute | solution.py:632
  305.3 21.2 %reduce-scatter.2.cloned.1.call-done = bf16[464,512]{1,0:T(8,128)(2,1)} async-done(((bf16[3712,512]{1,0:T(8,128)(2,1)}), bf16[464,512]{1,0:T(8,128)(2,1)}) %reduce-scatter.2.cloned.1.call-update) | async-done | bytes 475152 | tf_op jit(solution)/shard_map/reduce_scatter | solution.py:727
  326.5 1.0 constant_dynamic-slice_fusion.2
  327.6 0.7 pad_maximum_fusion.3
  328.3 3.3 collective-permute-start.18
  331.7 1.1 collective-permute-start.16
  332.8 3.7 collective-permute-done.18
  336.5 22.0 %collective-permute-done.17 = bf16[480,128]{1,0:T(8,128)(2,1)S(1)} collective-permute-done((bf16[480,128]{1,0:T(8,128)(2,1)}, bf16[480,128]{1,0:T(8,128)(2,1)S(1)}, u32[]{:S(2)}, u32[]{:S(2)}) %collective-permute-start.17) | collective-permute-done | bytes 122912 | tf_op jit(solution)/shard_map/sums/ppermute | solution.py:632
  358.5 1.7 convert_add_fusion
  360.3 0.7 copy-done.12
  361.0 0.2 collective-permute-start.10
  361.2 1.8 collective-permute-start.11
  363.1 1.9 fusion.8
  364.9 1.9 fusion.7
  366.8 1.9 fusion.6
  368.6 1.9 fusion.5
  370.5 1.9 fusion.4
  372.3 1.9 fusion.3
  374.2 1.9 fusion.2
  376.0 0.8 fusion.1
  376.9 1.9 fusion
  378.7 0.7 constant_dynamic-update-slice_fusion.2
  379.4 0.6 convert.9
  380.1 5.6 %all-gather.5.cloned.1.call-done = f32[3712,128]{1,0:T(8,128)} async-done(((f32[464,128]{1,0:T(8,128)}), f32[3712,128]{1,0:T(8,128)}) %all-gather.5.cloned.1.call-update) | async-done | bytes 1900560 | tf_op jit(solution)/shard_map/all_gather | solution.py:743
  385.7 1.7 fusion.21
  387.4 1.3 fusion.20
  388.7 1.2 slice_bitcast_fusion.18
  389.9 2.6 fusion.19
  392.5 13.9 %collective-permute-done.10.refs_1_ = bf16[2,1024,128]{2,1,0:T(8,128)(2,1)} collective-permute-done((bf16[2,1024,128]{2,1,0:T(8,128)(2,1)S(1)}, bf16[2,1024,128]{2,1,0:T(8,128)(2,1)}, u32[]{:S(2)}, u32[]{:S(2)}) %collective-permute-start.10) | collective-permute-done | bytes 524320 | tf_op jit(solution)/shard_map/results_3/ppermute | solution.py:632
  406.4 2.3 shard_map.200
  (64 shorter events, 1.1 us)
Async XLA Ops:
  7.2 89.7 %copy-start = (bf16[16,4,128]{2,1,0:T(4,128)(2,1)S(1)}, bf16[16,4,128]{2,1,0:T(4,128)(2,1)}, u32[]{:S(2)}) copy-start(bf16[16,4,128]{2,1,0:T(4,128)(2,1)} %param.13) | copy-start | bytes 49156
  7.2 140.0 %all-gather.3.cloned.1.call-start = ((), (), s32[]{:S(2)}) async-start(), calls=%async_computation.1 | async-start | bytes 4276224 | tf_op jit(solution)/shard_map/all_gather | solution.py:680
  11.1 15.1 %collective-permute-start = (bf16[1488,128]{1,0:T(8,128)(2,1)}, bf16[1488,128]{1,0:T(8,128)(2,1)S(1)}, u32[]{:S(2)}, u32[]{:S(2)}) collective-permute-start(bf16[1488,128]{1,0:T(8,128)(2,1)} %get-tuple-element.61), channel_id=1, source_target_pairs={{0,1},{1,2},{2,3},{3,0},{4,5},{5,6},{6,7},{7,4},{8,9},{9,10},{10,1... | collective-permute-start | bytes 1142792 | tf_op jit(solution)/shard_map/frames_0/ppermute | solution.py:632
  14.1 28.4 %collective-permute-start.1 = (bf16[1488,128]{1,0:T(8,128)(2,1)}, bf16[1488,128]{1,0:T(8,128)(2,1)S(1)}, u32[]{:S(2)}, u32[]{:S(2)}) collective-permute-start(bf16[1488,128]{1,0:T(8,128)(2,1)} %get-tuple-element.62), channel_id=1, source_target_pairs={{0,2},{1,3},{2,0},{3,1},{4,6},{5,7},{6,4},{7,5},{8,10},{9,11},{10,... | collective-permute-start | bytes 1142792 | tf_op jit(solution)/shard_map/frames_0/ppermute | solution.py:632
  16.7 4.1 copy-start.14
  16.7 25.8 %collective-permute-start.2 = (bf16[1488,128]{1,0:T(8,128)(2,1)}, bf16[1488,128]{1,0:T(8,128)(2,1)S(1)}, u32[]{:S(2)}, u32[]{:S(2)}) collective-permute-start(bf16[1488,128]{1,0:T(8,128)(2,1)} %get-tuple-element.63), channel_id=1, source_target_pairs={{0,3},{1,0},{2,1},{3,2},{4,7},{5,4},{6,5},{7,6},{8,11},{9,8},{10,9... | collective-permute-start | bytes 1142792 | tf_op jit(solution)/shard_map/frames_0/ppermute | solution.py:632
  20.6 62.9 %collective-permute-start.3 = (bf16[3072,128]{1,0:T(8,128)(2,1)}, bf16[3072,128]{1,0:T(8,128)(2,1)S(1)}, u32[]{:S(2)}, u32[]{:S(2)}) collective-permute-start(bf16[3072,128]{1,0:T(8,128)(2,1)} %get-tuple-element.64), channel_id=1, source_target_pairs={{0,2},{1,3},{2,0},{3,1},{4,6},{5,7},{6,4},{7,5},{8,10},{9,11},{10,... | collective-permute-start | bytes 2359304 | tf_op jit(solution)/shard_map/inputs_1/ppermute | solution.py:632
  42.6 41.7 %copy-start.10 = (bf16[464,512]{1,0:T(8,128)(2,1)}, bf16[464,512]{1,0:T(8,128)(2,1)S(1)}, u32[]{:S(2)}) copy-start(bf16[464,512]{1,0:T(8,128)(2,1)S(1)} %slice_dynamic-update-slice_fusion) | copy-start | bytes 1425412
  83.5 0.9 copy-start.1
  84.4 242.2 %reduce-scatter.2.cloned.1.call-start = ((), (), s32[]{:S(2)}) async-start(), calls=%async_computation.2 | async-start | bytes 4276224 | tf_op jit(solution)/shard_map/reduce_scatter | solution.py:727
  84.4 22.5 %collective-permute-start.7 = (bf16[3072,128]{1,0:T(8,128)(2,1)}, bf16[3072,128]{1,0:T(8,128)(2,1)S(1)}, u32[]{:S(2)}, u32[]{:S(2)}) collective-permute-start(bf16[3072,128]{1,0:T(8,128)(2,1)} %get-tuple-element.72), channel_id=1, source_target_pairs={{0,1},{1,2},{2,3},{3,0},{4,5},{5,6},{6,7},{7,4},{8,9},{9,10},{10,1... | collective-permute-start | bytes 2359304 | tf_op jit(solution)/shard_map/inputs_1/ppermute | solution.py:632
  84.5 62.7 %collective-permute-start.8 = (bf16[3072,128]{1,0:T(8,128)(2,1)}, bf16[3072,128]{1,0:T(8,128)(2,1)}, u32[]{:S(2)}, u32[]{:S(2)}) collective-permute-start(bf16[3072,128]{1,0:T(8,128)(2,1)} %get-tuple-element.73), channel_id=1, source_target_pairs={{0,3},{1,0},{2,1},{3,2},{4,7},{5,4},{6,5},{7,6},{8,11},{9,8},{10,9... | collective-permute-start | bytes 2359304 | tf_op jit(solution)/shard_map/inputs_1/ppermute | solution.py:632
  92.9 117.2 %collective-permute-start.4 = (bf16[4096,128]{1,0:T(8,128)(2,1)}, bf16[4096,128]{1,0:T(8,128)(2,1)S(1)}, u32[]{:S(2)}, u32[]{:S(2)}) collective-permute-start(bf16[4096,128]{1,0:T(8,128)(2,1)} %get-tuple-element.69), channel_id=1, source_target_pairs={{0,1},{1,2},{2,3},{3,0},{4,5},{5,6},{6,7},{7,4},{8,9},{9,10},{10,1... | collective-permute-start | bytes 3145736 | tf_op jit(solution)/shard_map/inputs_2/ppermute | solution.py:632
  92.9 117.1 %collective-permute-start.5 = (bf16[4096,128]{1,0:T(8,128)(2,1)}, bf16[4096,128]{1,0:T(8,128)(2,1)}, u32[]{:S(2)}, u32[]{:S(2)}) collective-permute-start(bf16[4096,128]{1,0:T(8,128)(2,1)} %get-tuple-element.70), channel_id=1, source_target_pairs={{0,2},{1,3},{2,0},{3,1},{4,6},{5,7},{6,4},{7,5},{8,10},{9,11},{10,... | collective-permute-start | bytes 3145736 | tf_op jit(solution)/shard_map/inputs_2/ppermute | solution.py:632
  93.1 117.0 %collective-permute-start.6 = (bf16[4096,128]{1,0:T(8,128)(2,1)}, bf16[4096,128]{1,0:T(8,128)(2,1)}, u32[]{:S(2)}, u32[]{:S(2)}) collective-permute-start(bf16[4096,128]{1,0:T(8,128)(2,1)} %get-tuple-element.71), channel_id=1, source_target_pairs={{0,3},{1,0},{2,1},{3,2},{4,7},{5,4},{6,5},{7,6},{8,11},{9,8},{10,9... | collective-permute-start | bytes 3145736 | tf_op jit(solution)/shard_map/inputs_2/ppermute | solution.py:632
  106.9 0.9 copy-start.3
  147.2 1.1 copy-start.2
  148.4 1.1 copy-start.4
  210.1 67.7 %collective-permute-start.12 = (bf16[4,1024,128]{2,1,0:T(8,128)(2,1)S(1)}, bf16[4,1024,128]{2,1,0:T(8,128)(2,1)}, u32[]{:S(2)}, u32[]{:S(2)}) collective-permute-start(bf16[4,1024,128]{2,1,0:T(8,128)(2,1)S(1)} %get-tuple-element.84), channel_id=1, source_target_pairs={{0,2},{1,3},{2,0},{3,1},{4,6},{5,7},{6,4},{7,5},{8,10},{9,11},{10,... | collective-permute-start | bytes 3145736 | tf_op jit(solution)/shard_map/results_0/ppermute | solution.py:632
  211.0 66.8 %collective-permute-start.13 = (bf16[4,1024,128]{2,1,0:T(8,128)(2,1)}, bf16[4,1024,128]{2,1,0:T(8,128)(2,1)}, u32[]{:S(2)}, u32[]{:S(2)}) collective-permute-start(bf16[4,1024,128]{2,1,0:T(8,128)(2,1)} %get-tuple-element.85), channel_id=1, source_target_pairs={{0,1},{1,2},{2,3},{3,0},{4,5},{5,6},{6,7},{7,4},{8,9},{9,10},{10,1... | collective-permute-start | bytes 3145736 | tf_op jit(solution)/shard_map/results_0/ppermute | solution.py:632
  273.3 0.8 copy-start.5
  274.1 0.8 copy-start.7
  274.9 0.8 copy-start.8
  275.7 0.8 copy-start.9
  277.8 83.2 %copy-start.6 = (bf16[2,1024,128]{2,1,0:T(8,128)(2,1)S(1)}, bf16[2,1024,128]{2,1,0:T(8,128)(2,1)}, u32[]{:S(2)}) copy-start(bf16[2,1024,128]{2,1,0:T(8,128)(2,1)} %copy-done.5) | copy-start | bytes 1572868
  277.8 107.8 %all-gather.5.cloned.1.call-start = ((), (), s32[]{:S(2)}) async-start(), calls=%async_computation.3 | async-start | bytes 2138112 | tf_op jit(solution)/shard_map/all_gather | solution.py:743
  277.9 16.2 %collective-permute-start.14 = (bf16[2,1024,128]{2,1,0:T(8,128)(2,1)}, bf16[2,1024,128]{2,1,0:T(8,128)(2,1)}, u32[]{:S(2)}, u32[]{:S(2)}) collective-permute-start(bf16[2,1024,128]{2,1,0:T(8,128)(2,1)} %copy-done.9), channel_id=1, source_target_pairs={{0,3},{1,0},{2,1},{3,2},{4,7},{5,4},{6,5},{7,6},{8,11},{9,8},{10,9... | collective-permute-start | bytes 1572872 | tf_op jit(solution)/shard_map/results_2/ppermute | solution.py:632
  279.4 25.9 %collective-permute-start.15 = (bf16[2,1024,128]{2,1,0:T(8,128)(2,1)}, bf16[2,1024,128]{2,1,0:T(8,128)(2,1)}, u32[]{:S(2)}, u32[]{:S(2)}) collective-permute-start(bf16[2,1024,128]{2,1,0:T(8,128)(2,1)} %copy-done.8), channel_id=1, source_target_pairs={{0,1},{1,2},{2,3},{3,0},{4,5},{5,6},{6,7},{7,4},{8,9},{9,10},{10,1... | collective-permute-start | bytes 1572872 | tf_op jit(solution)/shard_map/results_2/ppermute | solution.py:632
  280.0 83.1 %collective-permute-start.20 = (bf16[4,1024,128]{2,1,0:T(8,128)(2,1)S(1)}, bf16[4,1024,128]{2,1,0:T(8,128)(2,1)}, u32[]{:S(2)}, u32[]{:S(2)}) collective-permute-start(bf16[4,1024,128]{2,1,0:T(8,128)(2,1)S(1)} %get-tuple-element.97), channel_id=1, source_target_pairs={{0,3},{1,0},{2,1},{3,2},{4,7},{5,4},{6,5},{7,6},{8,11},{9,8},{10,9... | collective-permute-start | bytes 3145736 | tf_op jit(solution)/shard_map/results_0/ppermute | solution.py:632
  283.2 77.0 %collective-permute-start.19 = (bf16[2,1024,128]{2,1,0:T(8,128)(2,1)}, bf16[2,1024,128]{2,1,0:T(8,128)(2,1)S(1)}, u32[]{:S(2)}, u32[]{:S(2)}) collective-permute-start(bf16[2,1024,128]{2,1,0:T(8,128)(2,1)} %copy-done.7), channel_id=1, source_target_pairs={{0,2},{1,3},{2,0},{3,1},{4,6},{5,7},{6,4},{7,5},{8,10},{9,11},{10,... | collective-permute-start | bytes 1572872 | tf_op jit(solution)/shard_map/results_2/ppermute | solution.py:632
  328.3 8.2 %collective-permute-start.18 = (bf16[480,128]{1,0:T(8,128)(2,1)}, bf16[480,128]{1,0:T(8,128)(2,1)S(1)}, u32[]{:S(2)}, u32[]{:S(2)}) collective-permute-start(bf16[480,128]{1,0:T(8,128)(2,1)} %get-tuple-element.140), channel_id=1, source_target_pairs={{0,3},{1,0},{2,1},{3,2},{4,7},{5,4},{6,5},{7,6},{8,11},{9,8},{10,9... | collective-permute-start | bytes 368648 | tf_op jit(solution)/shard_map/sums/ppermute | solution.py:632
  331.7 26.8 %collective-permute-start.17 = (bf16[480,128]{1,0:T(8,128)(2,1)}, bf16[480,128]{1,0:T(8,128)(2,1)S(1)}, u32[]{:S(2)}, u32[]{:S(2)}) collective-permute-start(bf16[480,128]{1,0:T(8,128)(2,1)} %get-tuple-element.141), channel_id=1, source_target_pairs={{0,2},{1,3},{2,0},{3,1},{4,6},{5,7},{6,4},{7,5},{8,10},{9,11},{10,... | collective-permute-start | bytes 368648 | tf_op jit(solution)/shard_map/sums/ppermute | solution.py:632
  331.7 26.8 %collective-permute-start.16 = (bf16[480,128]{1,0:T(8,128)(2,1)}, bf16[480,128]{1,0:T(8,128)(2,1)}, u32[]{:S(2)}, u32[]{:S(2)}) collective-permute-start(bf16[480,128]{1,0:T(8,128)(2,1)} %get-tuple-element.139), channel_id=1, source_target_pairs={{0,1},{1,2},{2,3},{3,0},{4,5},{5,6},{6,7},{7,4},{8,9},{9,10},{10,1... | collective-permute-start | bytes 368648 | tf_op jit(solution)/shard_map/sums/ppermute | solution.py:632
  360.2 0.8 copy-start.12
  361.0 15.0 %copy-start.13 = (bf16[2,1024,128]{2,1,0:T(8,128)(2,1)S(1)}, bf16[2,1024,128]{2,1,0:T(8,128)(2,1)}, u32[]{:S(2)}) copy-start(bf16[2,1024,128]{2,1,0:T(8,128)(2,1)} %copy-done.12) | copy-start | bytes 1572868
  361.0 31.5 %collective-permute-start.9 = (bf16[2,1024,128]{2,1,0:T(8,128)(2,1)S(1)}, bf16[2,1024,128]{2,1,0:T(8,128)(2,1)S(1)}, u32[]{:S(2)}, u32[]{:S(2)}) collective-permute-start(bf16[2,1024,128]{2,1,0:T(8,128)(2,1)S(1)} %copy-done.6), channel_id=1, source_target_pairs={{0,3},{1,0},{2,1},{3,2},{4,7},{5,4},{6,5},{7,6},{8,11},{9,8},{10,9... | collective-permute-start | bytes 1572872 | tf_op jit(solution)/shard_map/results_3/ppermute | solution.py:632
  361.0 45.4 %collective-permute-start.10 = (bf16[2,1024,128]{2,1,0:T(8,128)(2,1)S(1)}, bf16[2,1024,128]{2,1,0:T(8,128)(2,1)}, u32[]{:S(2)}, u32[]{:S(2)}) collective-permute-start(bf16[2,1024,128]{2,1,0:T(8,128)(2,1)S(1)} %get-tuple-element.78), channel_id=1, source_target_pairs={{0,2},{1,3},{2,0},{3,1},{4,6},{5,7},{6,4},{7,5},{8,10},{9,11},{10,... | collective-permute-start | bytes 1572872 | tf_op jit(solution)/shard_map/results_3/ppermute | solution.py:632
  361.2 45.2 %collective-permute-start.11 = (bf16[2,1024,128]{2,1,0:T(8,128)(2,1)S(1)}, bf16[2,1024,128]{2,1,0:T(8,128)(2,1)}, u32[]{:S(2)}, u32[]{:S(2)}) collective-permute-start(bf16[2,1024,128]{2,1,0:T(8,128)(2,1)S(1)} %get-tuple-element.79), channel_id=1, source_target_pairs={{0,1},{1,2},{2,3},{3,0},{4,5},{5,6},{6,7},{7,4},{8,9},{9,10},{10,1... | collective-permute-start | bytes 1572872 | tf_op jit(solution)/shard_map/results_3/ppermute | solution.py:632
  392.5 13.9 %copy-start.11 = (bf16[2,1024,128]{2,1,0:T(8,128)(2,1)}, bf16[2,1024,128]{2,1,0:T(8,128)(2,1)S(1)}, u32[]{:S(2)}) copy-start(bf16[2,1024,128]{2,1,0:T(8,128)(2,1)S(1)} %collective-permute-done.9.refs_0_) | copy-start | bytes 1572868
Sparse Core Ops, SparseCore 0:
  84.5 34.2 all-gather.2
  278.0 48.5 reduce-scatter.1
  360.4 25.2 all-gather.4
